TPU v7x, 32 devices: a whole 2x2x4 slice. The times are simulated.
32 devices in a mesh: seq: 8 (over z, x), kvh: 4 (over y, core).
Axes of the slice: x: 2, y: 2, z: 4, core: 2. Of those that a mesh axis runs over, the one named last changes fastest.
Arguments:
- queries: bfloat16 [2048, 2048], P('seq', 'kvh'), may hold values from -12 to 12
- kv_cache: bfloat16 [2, 65536, 512], P(None, 'seq', 'kvh'), may hold values from -6 to 6
- selected: int32 [16, 4, 2], P('seq', 'kvh'), may hold values from 0 to 62, as said below
- out_weight: bfloat16 [2048, 4096], P('kvh', 'seq'), may hold values from -0.1875 to 0.1875
Outputs:
- output: bfloat16 [2048, 4096], P('seq', 'kvh')
Inputs may be any that keep to these rules, and one draw needn't show every extreme that they name: `selected`: for each KV head, the 4 blocks named by the tiles of one device of seq lie in the ranges of distinct devices (block b lies in the range of device b // 8); for each KV head, some device's range is named by a tile of every device.
All inputs are finite; a program needn't handle non-finite values.
Results may differ from a plain program's by a relative error of at most 0.017.
Values may be sent and summed in bfloat16 or wider, within the bound.
No kernel may reach another device: no remote copies, remote signals or barrier semaphores. Data moves between devices by JAX's collectives and lax.ppermute only.
A program may use at most 128 MiB of HBM per device.

v0:
```python
import jax
import jax.numpy as jnp
from jax import lax
from jax.sharding import PartitionSpec as P

GROUP = 4
HD = 128
BLK = 1024
TILE = 128
SEL = 2


def shortened(value):

    def short(part):
        return part.astype(jnp.bfloat16) if part.dtype == jnp.float32 else part

    return jax.tree.map(short, value)


def attend(query_tile, key_rows, value_rows, visible):
    scores = jnp.einsum(
        "igd,kd->gik", query_tile, key_rows, preferred_element_type=jnp.float32
    ) * HD ** (-0.5)
    scores = jnp.where(visible[None], scores, -jnp.inf)
    row_max = jnp.max(scores, axis=2)
    weights = jnp.exp(scores - row_max[:, :, None])
    row_sum = jnp.sum(weights, axis=2)
    summed = jnp.einsum(
        "gik,kd->gid", weights.astype(jnp.bfloat16), value_rows, preferred_element_type=jnp.float32
    )
    return (row_max, row_sum, (summed / row_sum[:, :, None]).astype(jnp.bfloat16))


def combine(row_maxes, row_sums, normeds):
    highest = row_maxes[0]
    for extra in row_maxes[1:]:
        highest = jnp.maximum(highest, extra)
    norm_sum = jnp.zeros_like(highest)
    blended = jnp.zeros(normeds[0].shape, jnp.float32)
    for top_value, sum_value, normed in zip(row_maxes, row_sums, normeds):
        factor = jnp.exp(top_value - highest) * sum_value
        norm_sum = norm_sum + factor
        blended = blended + factor[..., None] * normed.astype(jnp.float32)
    return blended / norm_sum[..., None]


def per_device(queries, kv_cache, selected, out_weight):
    seq_count = lax.axis_size("seq")
    device = lax.axis_index("seq")
    query_count = queries.shape[0]
    tiles_dev = query_count // TILE
    blocks = kv_cache.shape[1] // BLK
    requests = tiles_dev * SEL
    own_block = device * blocks + blocks - 1
    kv_blocks = kv_cache.reshape(2, blocks, BLK, HD)
    query_tiles = queries.reshape(tiles_dev, TILE, GROUP, HD)
    chosen = selected.reshape(requests)
    target = jnp.where(chosen >= own_block, chosen + 1, chosen)
    holder = target // blocks
    within = target % blocks
    request_tile = jnp.arange(requests, dtype=jnp.int32) // SEL
    peers = jnp.arange(seq_count, dtype=jnp.int32)
    routing = holder[None, :] == peers[:, None]
    filled = jnp.any(routing, axis=1).astype(jnp.int32)
    slot_block = jnp.sum(jnp.where(routing, within[None, :], 0), axis=1)
    slot_info = jnp.stack([filled, slot_block], axis=1)
    full_view = jnp.ones((TILE, BLK), dtype=bool)
    key_offsets = jnp.arange(BLK)

    def own_piece(tile_index):
        query_offsets = BLK - query_count + tile_index * TILE + jnp.arange(TILE)
        causal = key_offsets[None, :] <= query_offsets[:, None]
        return attend(
            query_tiles[tile_index], kv_blocks[0, blocks - 1], kv_blocks[1, blocks - 1], causal
        )

    own_max, own_sum, own_out = lax.map(own_piece, jnp.arange(tiles_dev, dtype=jnp.int32))
    slot_tile = jnp.sum(jnp.where(routing, request_tile[None, :], 0), axis=1)
    picking = (slot_tile[:, None] == jnp.arange(tiles_dev)[None, :]) & (filled[:, None] > 0)
    outgoing = jnp.dot(
        picking.astype(jnp.bfloat16),
        queries.reshape(tiles_dev, TILE * GROUP * HD),
        preferred_element_type=jnp.float32,
    )
    outgoing = outgoing.astype(jnp.bfloat16).reshape(seq_count, TILE, GROUP * HD)
    arrived, arrived_info = (
        lax.all_to_all(outgoing, "seq", split_axis=0, concat_axis=0, tiled=True),
        lax.all_to_all(slot_info, "seq", split_axis=0, concat_axis=0, tiled=True),
    )

    def serve(item):
        query_block, info = item
        query_tile = query_block.reshape(TILE, GROUP, HD)

        def work(unused):
            return attend(query_tile, kv_blocks[0, info[1]], kv_blocks[1, info[1]], full_view)

        def skip(unused):
            blank = jnp.zeros((GROUP, TILE), jnp.float32)
            return (blank, blank + 1.0, jnp.zeros((GROUP, TILE, HD), jnp.bfloat16))

        return lax.cond(info[0] > 0, work, skip, 0)

    part_max, part_sum, part_out = lax.map(serve, (arrived, arrived_info))
    back_out = jax.tree.map(
        lambda part, own: part.astype(own.dtype),
        lax.all_to_all(shortened(part_out), "seq", split_axis=0, concat_axis=0, tiled=True),
        part_out,
    )
    back_max, back_sum = (
        lax.all_to_all(part_max, "seq", split_axis=0, concat_axis=0, tiled=True),
        lax.all_to_all(part_sum, "seq", split_axis=0, concat_axis=0, tiled=True),
    )
    picked_max = jnp.take(back_max, holder, axis=0)
    picked_sum = jnp.take(back_sum, holder, axis=0)
    picked_out = jnp.take(back_out, holder, axis=0)
    picked_max = picked_max.reshape(tiles_dev, SEL, GROUP, TILE)
    picked_sum = picked_sum.reshape(tiles_dev, SEL, GROUP, TILE)
    picked_out = picked_out.reshape(tiles_dev, SEL, GROUP, TILE, HD)
    maxima = [own_max] + [picked_max[:, pick] for pick in range(SEL)]
    sums = [own_sum] + [picked_sum[:, pick] for pick in range(SEL)]
    outs = [own_out] + [picked_out[:, pick] for pick in range(SEL)]
    blended = combine(maxima, sums, outs)
    attention = (
        jnp.transpose(blended, (0, 2, 1, 3)).reshape(query_count, GROUP * HD).astype(jnp.bfloat16)
    )
    column_terms = jnp.dot(
        attention,
        lax.all_gather(out_weight, "seq", axis=1, tiled=True),
        preferred_element_type=jnp.float32,
    )
    return lax.psum_scatter(
        column_terms.astype(jnp.bfloat16), "kvh", scatter_dimension=1, tiled=True
    )


def solution(mesh):
    in_specs = (P("seq", "kvh"), P(None, "seq", "kvh"), P("seq", "kvh", None), P("kvh", "seq"))
    out_specs = P("seq", "kvh")
    return jax.shard_map(
        per_device, mesh=mesh, in_specs=in_specs, out_specs=out_specs, check_vma=False
    )
```

profile of v0, /device:TPU:0, one launch (start us, length us, event | category | flops | bytes accessed | tf_op | source)
XLA Modules:
  0.0 227.9 jit_solution(8810962553320524371)
XLA Ops:
  7.0 1.3 reduce.5
  8.7 0.7 copy.34
  9.4 7.3 %all-to-all-start = ((s32[8,1,2]{2,1,0:T(1,128)}), s32[8,1,2]{2,1,0:T(1,128)S(1)}, u32[]{:S(2)}, u32[]{:S(2)}) async-start(s32[8,1,2]{2,1,0:T(1,128)} %copy.34), calls=%async_computation | async-start | bytes 8192 | tf_op jit(solution)/shard_map/all_to_all | solution.py:89
  16.6 1.2 reshape.260
  18.3 1.7 copy.36
  20.0 3.0 %all-to-all-done = s32[8,1,2]{2,1,0:T(1,128)S(1)} async-done(((s32[8,1,2]{2,1,0:T(1,128)}), s32[8,1,2]{2,1,0:T(1,128)S(1)}, u32[]{:S(2)}, u32[]{:S(2)}) %all-to-all-start) | async-done | bytes 96 | tf_op jit(solution)/shard_map/all_to_all | solution.py:89
  23.0 3.6 %all-to-all-start.1 = ((bf16[8,128,512]{1,2,0:T(8,128)(2,1)}), bf16[8,128,512]{1,2,0:T(8,128)(2,1)S(1)}, u32[]{:S(2)}, u32[]{:S(2)}) async-start(bf16[8,128,512]{1,2,0:T(8,128)(2,1)} %copy.36), calls=%async_computation.1 | async-start | bytes 2097152 | tf_op jit(solution)/shard_map/all_to_all | solution.py:88
  26.6 0.7 all-gather.2.cloned.1.call-update
  27.4 38.6 %all-to-all-done.1 = bf16[8,128,512]{1,2,0:T(8,128)(2,1)S(1)} async-done(((bf16[8,128,512]{1,2,0:T(8,128)(2,1)}), bf16[8,128,512]{1,2,0:T(8,128)(2,1)S(1)}, u32[]{:S(2)}, u32[]{:S(2)}) %all-to-all-start.1) | async-done | bytes 1048608 | tf_op jit(solution)/shard_map/all_to_all | solution.py:88
  66.0 63.2 %while.29 = (s32[]{:T(128)}, f32[8,4,128]{2,1,0:T(4,128)}, f32[8,4,128]{2,1,0:T(4,128)S(1)}, bf16[8,4,128,128]{3,2,1,0:T(8,128)(2,1)}, s32[8,2]{1,0:T(8,128)S(1)...) while((s32[]{:T(128)}, f32[8,4,128]{2,1,0:T(4,128)}, ...), condition=%wide.region_12.13_spmd, body=%wide.region_7.12_spmd.sunk | while | flops 272759808 | bytes 7621869 | solution.py:105
  66.0 1.2 conditional.2
  67.2 1.2 constant_dynamic-update-slice_fusion.5
  68.5 0.7 constant_dynamic-update-slice_fusion.6
  69.2 1.2 conditional.2
  70.4 1.2 constant_dynamic-update-slice_fusion.5
  71.6 0.7 constant_dynamic-update-slice_fusion.6
  72.3 7.5 %conditional.2 = (f32[1,4,128]{2,1,0:T(4,128)}, f32[1,4,128]{2,1,0:T(4,128)}, bf16[1,4,128,128]{3,2,1,0:T(8,128)(2,1)S(1)}) conditional(s32[]{:T(128)} %bitcast.149, () %tuple.76, (s32[1,2]{1,0:T(1,128)S(1)}, bf16[2,8,1024,128]{3,2,1,0:T(8,128)(2,1)}, bf16[8,128,512]{1,2,0:T(8,128)(2,1)S(1)}, s32[]{:T(128)}) %tuple.77), branch_computations={%region_8.8_spmd, %region_9.11_spmd} | conditional | flops 272759808 | bytes 7350350 | solution.py:103
  74.8 2.0 bitcast_reduce_fusion
  76.8 1.6 fusion.4
  78.4 1.5 fusion.6
  79.9 1.3 constant_dynamic-update-slice_fusion.5
  81.1 0.7 constant_dynamic-update-slice_fusion.6
  81.8 7.5 %conditional.2 = (f32[1,4,128]{2,1,0:T(4,128)}, f32[1,4,128]{2,1,0:T(4,128)}, bf16[1,4,128,128]{3,2,1,0:T(8,128)(2,1)S(1)}) conditional(s32[]{:T(128)} %bitcast.149, () %tuple.76, (s32[1,2]{1,0:T(1,128)S(1)}, bf16[2,8,1024,128]{3,2,1,0:T(8,128)(2,1)}, bf16[8,128,512]{1,2,0:T(8,128)(2,1)S(1)}, s32[]{:T(128)}) %tuple.77), branch_computations={%region_8.8_spmd, %region_9.11_spmd} | conditional | flops 272759808 | bytes 7350350 | solution.py:103
  84.3 2.0 bitcast_reduce_fusion
  86.3 1.6 fusion.4
  87.8 1.5 fusion.6
  89.3 1.3 constant_dynamic-update-slice_fusion.5
  90.6 0.7 constant_dynamic-update-slice_fusion.6
  91.3 7.5 %conditional.2 = (f32[1,4,128]{2,1,0:T(4,128)}, f32[1,4,128]{2,1,0:T(4,128)}, bf16[1,4,128,128]{3,2,1,0:T(8,128)(2,1)S(1)}) conditional(s32[]{:T(128)} %bitcast.149, () %tuple.76, (s32[1,2]{1,0:T(1,128)S(1)}, bf16[2,8,1024,128]{3,2,1,0:T(8,128)(2,1)}, bf16[8,128,512]{1,2,0:T(8,128)(2,1)S(1)}, s32[]{:T(128)}) %tuple.77), branch_computations={%region_8.8_spmd, %region_9.11_spmd} | conditional | flops 272759808 | bytes 7350350 | solution.py:103
  93.8 1.9 bitcast_reduce_fusion
  95.7 1.6 fusion.4
  97.3 1.5 fusion.6
  98.8 1.3 constant_dynamic-update-slice_fusion.5
  100.8 7.5 %conditional.2 = (f32[1,4,128]{2,1,0:T(4,128)}, f32[1,4,128]{2,1,0:T(4,128)}, bf16[1,4,128,128]{3,2,1,0:T(8,128)(2,1)S(1)}) conditional(s32[]{:T(128)} %bitcast.149, () %tuple.76, (s32[1,2]{1,0:T(1,128)S(1)}, bf16[2,8,1024,128]{3,2,1,0:T(8,128)(2,1)}, bf16[8,128,512]{1,2,0:T(8,128)(2,1)S(1)}, s32[]{:T(128)}) %tuple.77), branch_computations={%region_8.8_spmd, %region_9.11_spmd} | conditional | flops 272759808 | bytes 7350350 | solution.py:103
  103.2 2.0 bitcast_reduce_fusion
  105.2 1.6 fusion.4
  106.8 1.5 fusion.6
  108.3 1.3 constant_dynamic-update-slice_fusion.5
  109.5 0.7 constant_dynamic-update-slice_fusion.6
  110.2 7.5 %conditional.2 = (f32[1,4,128]{2,1,0:T(4,128)}, f32[1,4,128]{2,1,0:T(4,128)}, bf16[1,4,128,128]{3,2,1,0:T(8,128)(2,1)S(1)}) conditional(s32[]{:T(128)} %bitcast.149, () %tuple.76, (s32[1,2]{1,0:T(1,128)S(1)}, bf16[2,8,1024,128]{3,2,1,0:T(8,128)(2,1)}, bf16[8,128,512]{1,2,0:T(8,128)(2,1)S(1)}, s32[]{:T(128)}) %tuple.77), branch_computations={%region_8.8_spmd, %region_9.11_spmd} | conditional | flops 272759808 | bytes 7350350 | solution.py:103
  112.7 1.9 bitcast_reduce_fusion
  114.7 1.6 fusion.4
  116.3 1.5 fusion.6
  117.8 1.3 constant_dynamic-update-slice_fusion.5
  119.0 0.7 constant_dynamic-update-slice_fusion.6
  119.7 7.5 %conditional.2 = (f32[1,4,128]{2,1,0:T(4,128)}, f32[1,4,128]{2,1,0:T(4,128)}, bf16[1,4,128,128]{3,2,1,0:T(8,128)(2,1)S(1)}) conditional(s32[]{:T(128)} %bitcast.149, () %tuple.76, (s32[1,2]{1,0:T(1,128)S(1)}, bf16[2,8,1024,128]{3,2,1,0:T(8,128)(2,1)}, bf16[8,128,512]{1,2,0:T(8,128)(2,1)S(1)}, s32[]{:T(128)}) %tuple.77), branch_computations={%region_8.8_spmd, %region_9.11_spmd} | conditional | flops 272759808 | bytes 7350350 | solution.py:103
  122.2 1.9 bitcast_reduce_fusion
  124.1 1.6 fusion.4
  125.7 1.5 fusion.6
  127.2 1.3 constant_dynamic-update-slice_fusion.5
  128.5 0.7 constant_dynamic-update-slice_fusion.6
  129.2 15.2 %all_to_all.32 = f32[8,4,128]{2,1,0:T(4,128)S(1)} all-to-all(f32[8,4,128]{2,1,0:T(4,128)S(1)} %get-tuple-element.123), channel_id=1, replica_groups=mesh['seq'=8,'kvh'=4] {'seq'}, dimensions={0} | all-to-all | bytes 32768 | tf_op jit(solution)/shard_map/all_to_all | solution.py:113
  144.4 3.3 %all-to-all-start.2 = ((f32[8,4,128]{2,1,0:T(4,128)}), f32[8,4,128]{2,1,0:T(4,128)S(1)}, u32[]{:S(2)}, u32[]{:S(2)}) async-start(f32[8,4,128]{2,1,0:T(4,128)} %get-tuple-element.120), calls=%async_computation.2 | async-start | bytes 32768 | tf_op jit(solution)/shard_map/all_to_all | solution.py:112
  147.8 6.4 %all-to-all-done.2 = f32[8,4,128]{2,1,0:T(4,128)S(1)} async-done(((f32[8,4,128]{2,1,0:T(4,128)}), f32[8,4,128]{2,1,0:T(4,128)S(1)}, u32[]{:S(2)}, u32[]{:S(2)}) %all-to-all-start.2) | async-done | bytes 16416 | tf_op jit(solution)/shard_map/all_to_all | solution.py:112
  154.2 3.6 %all-to-all-start.4 = ((bf16[8,4,128,128]{3,2,1,0:T(8,128)(2,1)}), bf16[8,4,128,128]{3,2,1,0:T(8,128)(2,1)S(1)}, u32[]{:S(2)}, u32[]{:S(2)}) async-start(bf16[8,4,128,128]{3,2,1,0:T(8,128)(2,1)} %get-tuple-element.124), calls=%async_computation.4 | async-start | bytes 2097152 | tf_op jit(solution)/shard_map/all_to_all | solution.py:108
  157.9 14.4 %while.30 = (s32[]{:T(128)}, f32[2,4,128]{2,1,0:T(4,128)S(1)}, f32[2,4,128]{2,1,0:T(4,128)S(1)}, bf16[2,4,128,128]{3,2,1,0:T(8,128)(2,1)S(1)}, s32[2]{0:T(128)S(...) while((s32[]{:T(128)}, f32[2,4,128]{2,1,0:T(4,128)S(1)}, ...), condition=%wide.region_3.4_spmd.clone, body=%wide.region_0.3_spmd.clone.sunk | while | flops 274463872 | bytes 7884487 | solution.py:78
  161.3 1.5 bitcast_reduce_fusion.3
  163.4 1.7 fusion.63
  168.5 1.5 bitcast_reduce_fusion.3
  170.6 1.7 fusion.63
  173.7 11.3 %all-to-all-done.4 = bf16[8,4,128,128]{3,2,1,0:T(8,128)(2,1)S(1)} async-done(((bf16[8,4,128,128]{3,2,1,0:T(8,128)(2,1)}), bf16[8,4,128,128]{3,2,1,0:T(8,128)(2,1)S(1)}, u32[]{:S(2)}, u32[]{:S(2)}) %all-to-all-start.4) | async-done | bytes 1048608 | tf_op jit(solution)/shard_map/all_to_all | solution.py:108
  185.8 0.7 fusion.42
  186.8 4.8 %convolution_convert_fusion.1 = bf16[256,4096]{1,0:T(8,128)(2,1)} fusion(bf16[512,4096]{1,0:T(8,128)(2,1)} %all-gather.2.cloned.1.call-done, bf16[32,8,4,128]{3,2,1,0:T(4,128)(2,1)S(1)} %bitcast.163), kind=kOutput, calls=%fused_computation.55 | convolution fusion | flops 1074790400 | bytes 6553600 | tf_op jit(solution)/shard_map/dot_general | solution.py:128
  191.6 29.5 %reduce-scatter.2.cloned.1.call-done = bf16[256,1024]{1,0:T(8,128)(2,1)} async-done(((bf16[256,4096]{1,0:T(8,128)(2,1)}), bf16[256,1024]{1,0:T(8,128)(2,1)}) %reduce-scatter.2.cloned.1.call-update) | async-done | bytes 524304 | tf_op jit(solution)/shard_map/reduce_scatter | solution.py:133
  (77 shorter events, 13.4 us)
Async XLA Ops:
  9.4 13.6 %all-to-all-start = ((s32[8,1,2]{2,1,0:T(1,128)}), s32[8,1,2]{2,1,0:T(1,128)S(1)}, u32[]{:S(2)}, u32[]{:S(2)}) async-start(s32[8,1,2]{2,1,0:T(1,128)} %copy.34), calls=%async_computation | async-start | bytes 8192 | tf_op jit(solution)/shard_map/all_to_all | solution.py:89
  23.0 43.0 %all-to-all-start.1 = ((bf16[8,128,512]{1,2,0:T(8,128)(2,1)}), bf16[8,128,512]{1,2,0:T(8,128)(2,1)S(1)}, u32[]{:S(2)}, u32[]{:S(2)}) async-start(bf16[8,128,512]{1,2,0:T(8,128)(2,1)} %copy.36), calls=%async_computation.1 | async-start | bytes 2097152 | tf_op jit(solution)/shard_map/all_to_all | solution.py:88
  26.6 160.2 %all-gather.2.cloned.1.call-start = ((), (), s32[]{:S(2)}) async-start(), calls=%async_computation.6 | async-start | bytes 4718592 | tf_op jit(solution)/shard_map/all_gather | solution.py:130
  66.0 81.7 %copy-start = (bf16[256,512]{1,0:T(8,128)(2,1)S(1)}, bf16[256,512]{1,0:T(8,128)(2,1)}, u32[]{:S(2)}) copy-start(bf16[256,512]{1,0:T(8,128)(2,1)} %param.12) | copy-start | bytes 786436
  144.4 9.9 %all-to-all-start.2 = ((f32[8,4,128]{2,1,0:T(4,128)}), f32[8,4,128]{2,1,0:T(4,128)S(1)}, u32[]{:S(2)}, u32[]{:S(2)}) async-start(f32[8,4,128]{2,1,0:T(4,128)} %get-tuple-element.120), calls=%async_computation.2 | async-start | bytes 32768 | tf_op jit(solution)/shard_map/all_to_all | solution.py:112
  154.2 30.8 %all-to-all-start.4 = ((bf16[8,4,128,128]{3,2,1,0:T(8,128)(2,1)}), bf16[8,4,128,128]{3,2,1,0:T(8,128)(2,1)S(1)}, u32[]{:S(2)}, u32[]{:S(2)}) async-start(bf16[8,4,128,128]{3,2,1,0:T(8,128)(2,1)} %get-tuple-element.124), calls=%async_computation.4 | async-start | bytes 2097152 | tf_op jit(solution)/shard_map/all_to_all | solution.py:108
  157.8 63.3 %reduce-scatter.2.cloned.1.call-start = ((), (), s32[]{:S(2)}) async-start(), calls=%async_computation.7 | async-start | bytes 2621440 | tf_op jit(solution)/shard_map/reduce_scatter | solution.py:133
  157.9 14.5 %copy-start.1 = (s32[2,1,2]{2,1,0:T(1,128)S(1)}, s32[2,1,2]{2,1,0:T(1,128)}, u32[]{:S(2)}) copy-start(s32[2,1,2]{2,1,0:T(1,128)} %param.14) | copy-start | bytes 52
Sparse Core Ops, SparseCore 0:
  29.5 85.4 all-gather.1
  191.7 29.3 reduce-scatter.1
where the time goes:
time: 228 us
  waiting for transfers between devices  89.6 us (39%)
  matrix products  32.3 us (14%)
  local copies, waits for them, and re-layouts  29.1 us (13%)
  starting transfers between devices  17.8 us (8%)
  loops' own time  16.8 us (7%)
  blocking collectives  15.2 us (7%)
  between operations  13.6 us (6%)
  other arithmetic  13.5 us (6%)
    all_to_all x1, waiting for transfers between devices, per_device(): lax.all_to_all(outgoing, 'seq', split_axis=0, concat_axis=0, tiled=True)  38.6 us
    reduce_scatter x1, waiting for transfers between devices, per_device(): lax.psum_scatter(column_terms.astype(jnp.bfloat16), 'kvh', scatter_dimens...  29.5 us
    dynamic_update_slice x16, local copies, waits for them, and re-layouts, per_device(): part_max, part_sum, part_out = lax.map(serve, (arrived, arrived_info))  15.3 us
    all_to_all x1, blocking collectives, per_device(): lax.all_to_all(part_sum, 'seq', split_axis=0, concat_axis=0, tiled=True)  15.2 us
    dot_general x8, matrix products, attend(): jnp.einsum('igd,kd->gik', query_tile, key_rows, preferred_element_type=jn...  14.8 us
    dot_general x8, matrix products, attend(): jnp.einsum('gik,kd->gid', weights.astype(jnp.bfloat16), value_rows, prefe...  12.2 us
    all_to_all x1, waiting for transfers between devices, per_device(): lax.all_to_all(shortened(part_out), 'seq', split_axis=0, concat_axis=0, t...  11.3 us
    another operation x8, loops' own time, serve(): return lax.cond(info[0] > 0, work, skip, 0)  11.1 us
  transfers between devices with their start and end apart: 6, of which 5 were waited for; matrix products, arithmetic and copies ran while one was open for 30% of the time, Pallas kernels for 0%

commit v1 on v0

v1 whole, which is shorter than its diff:
```python
import functools
import math

import jax
import jax.numpy as jnp
from jax import lax
from jax.experimental import pallas as pl
from jax.experimental.pallas import tpu as pltpu
from jax.sharding import PartitionSpec as P

GROUP = 4
HD = 128
BLK = 1024
TILE = 128
SEL = 2
ROWS = GROUP * TILE
SLOT = ROWS + 16
SCALE = HD ** (-0.5)
LOG2E = math.log2(math.e)
VMEM_LIMIT = 48 * 1024 * 1024

vmem = pl.BlockSpec(memory_space=pltpu.VMEM)
smem = pl.BlockSpec(memory_space=pltpu.SMEM)
hbm = pl.BlockSpec(memory_space=pl.ANY)


def params():
    return pltpu.CompilerParams(vmem_limit_bytes=VMEM_LIMIT)


def route(selected_ref, own_seq, peer, tiles, blocks):
    own_block = own_seq * blocks + blocks - 1
    tile, block, filled = jnp.int32(0), jnp.int32(0), jnp.int32(0)
    for request in range(tiles * SEL):
        chosen = selected_ref[request]
        target = jnp.where(chosen >= own_block, chosen + 1, chosen)
        here = lax.div(target, jnp.int32(blocks)) == peer
        tile = jnp.where(here, request // SEL, tile)
        block = jnp.where(here, lax.rem(target, jnp.int32(blocks)), block)
        filled = jnp.where(here, 1, filled)
    return tile, block, filled


def pack_kernel(tiles, blocks, me_ref, selected_ref, query_ref, *slots):
    for offset, slot in enumerate(slots):
        peer = me_ref[0] ^ offset
        tile, block, _ = route(selected_ref, me_ref[0], peer, tiles, blocks)
        rows = pl.ds(pl.multiple_of(tile * TILE, TILE), TILE)
        for head in range(GROUP):
            slot[head * TILE : (head + 1) * TILE, :] = query_ref[rows, head * HD : (head + 1) * HD]
        slot[ROWS:SLOT, :] = jnp.full((16, HD), block.astype(jnp.float32)).astype(jnp.bfloat16)


def pack(me, selected, queries, seq_count, blocks):
    tiles = queries.shape[0] // TILE
    return pl.pallas_call(
        functools.partial(pack_kernel, tiles, blocks),
        out_shape=[jax.ShapeDtypeStruct((SLOT, HD), jnp.bfloat16)] * seq_count,
        in_specs=[smem, smem, vmem],
        out_specs=[vmem] * seq_count,
        compiler_params=params(),
        name="pack_queries",
    )(me, selected, queries)


def attend(query, keys, values, first_offset, out_ref):
    scores = lax.dot_general(
        query, keys, (((1,), (1,)), ((), ())), preferred_element_type=jnp.float32
    )
    if first_offset is not None:
        offsets = first_offset + lax.rem(
            lax.broadcasted_iota(jnp.int32, (ROWS, BLK), 0), jnp.int32(TILE)
        )
        seen = lax.broadcasted_iota(jnp.int32, (ROWS, BLK), 1) <= offsets
        scores = jnp.where(seen, scores, -jnp.inf)
    top = jnp.max(scores, axis=1, keepdims=True)
    weights = jnp.exp2((scores - top) * (SCALE * LOG2E))
    total = jnp.sum(weights, axis=1, keepdims=True)
    summed = jnp.dot(weights.astype(jnp.bfloat16), values, preferred_element_type=jnp.float32)
    out_ref[0:ROWS, :] = (summed / total).astype(jnp.bfloat16)
    level = top * SCALE + jnp.log(total)
    lane = lax.rem(lax.broadcasted_iota(jnp.int32, (TILE, TILE), 1), jnp.int32(GROUP))
    spread = jnp.zeros((TILE, TILE), jnp.float32)
    for head in range(GROUP):
        spread = jnp.where(lane == head, level[head * TILE : (head + 1) * TILE], spread)
    lines = spread.T[0:16]
    high = lines.astype(jnp.bfloat16).astype(jnp.float32)
    middle = (lines - high).astype(jnp.bfloat16).astype(jnp.float32)
    low = lines - high - middle
    row = lax.broadcasted_iota(jnp.int32, (16, TILE), 0)
    parts = jnp.where(row < GROUP, high, jnp.where(row < 2 * GROUP, middle, low))
    out_ref[ROWS:SLOT, :] = parts.astype(jnp.bfloat16)


def own_kernel(tiles, blocks, query_ref, kv_ref, out_ref, keys, values, sems):
    start = (blocks - 1) * BLK
    copies = [
        pltpu.make_async_copy(kv_ref.at[0, pl.ds(start, BLK)], keys, sems.at[0]),
        pltpu.make_async_copy(kv_ref.at[1, pl.ds(start, BLK)], values, sems.at[1]),
    ]
    for copy in copies:
        copy.start()
    for copy in copies:
        copy.wait()

    def one(tile, carry):
        rows = pl.ds(pl.multiple_of(tile * TILE, TILE), TILE)
        query = jnp.concatenate(
            [query_ref[rows, head * HD : (head + 1) * HD] for head in range(GROUP)], axis=0
        )
        first_offset = BLK - tiles * TILE + tile * TILE
        attend(query, keys[...], values[...], first_offset, out_ref.at[tile])
        return carry

    lax.fori_loop(0, tiles, one, 0)


def own_pieces(queries, kv_cache):
    tiles, blocks = queries.shape[0] // TILE, kv_cache.shape[1] // BLK
    return pl.pallas_call(
        functools.partial(own_kernel, tiles, blocks),
        out_shape=jax.ShapeDtypeStruct((tiles, SLOT, HD), jnp.bfloat16),
        in_specs=[vmem, hbm],
        out_specs=vmem,
        scratch_shapes=[
            pltpu.VMEM((BLK, HD), jnp.bfloat16),
            pltpu.VMEM((BLK, HD), jnp.bfloat16),
            pltpu.SemaphoreType.DMA((2,)),
        ],
        compiler_params=params(),
        cost_estimate=pl.CostEstimate(
            flops=4 * tiles * ROWS * BLK * HD, bytes_accessed=4 * BLK * HD, transcendentals=tiles * ROWS * BLK
        ),
        name="own_pieces",
    )(queries, kv_cache)


def serve_kernel(slot_ref, kv_ref, out_ref, keys, values, sems):
    number = jnp.max(slot_ref[ROWS:SLOT, :].astype(jnp.float32)).astype(jnp.int32)
    start = pl.multiple_of(number * BLK, BLK)
    key_copy = pltpu.make_async_copy(kv_ref.at[0, pl.ds(start, BLK)], keys, sems.at[0])
    value_copy = pltpu.make_async_copy(kv_ref.at[1, pl.ds(start, BLK)], values, sems.at[1])
    key_copy.start()
    value_copy.start()
    key_copy.wait()
    value_copy.wait()
    attend(slot_ref[0:ROWS, :], keys[...], values[...], None, out_ref)


def serve(slot, kv_cache):
    return pl.pallas_call(
        serve_kernel,
        out_shape=jax.ShapeDtypeStruct((SLOT, HD), jnp.bfloat16),
        in_specs=[vmem, hbm],
        out_specs=vmem,
        scratch_shapes=[
            pltpu.VMEM((BLK, HD), jnp.bfloat16),
            pltpu.VMEM((BLK, HD), jnp.bfloat16),
            pltpu.SemaphoreType.DMA((2,)),
        ],
        compiler_params=params(),
        cost_estimate=pl.CostEstimate(
            flops=4 * ROWS * BLK * HD, bytes_accessed=4 * BLK * HD, transcendentals=ROWS * BLK
        ),
        name="serve_slot",
    )(slot, kv_cache)


def levels_of(parts):
    parts = parts.astype(jnp.float32)
    return parts[0:GROUP] + parts[GROUP : 2 * GROUP] + parts[2 * GROUP : 3 * GROUP]


def combine_kernel(tiles, blocks, seq_count, me_ref, selected_ref, own_ref, *refs):
    slots, out_ref, blend = refs[:seq_count], refs[seq_count], refs[seq_count + 1]
    routes = [
        route(selected_ref, me_ref[0], me_ref[0] ^ offset, tiles, blocks)
        for offset in range(seq_count)
    ]
    slot_levels = [levels_of(slot[ROWS:SLOT, :]) for slot in slots]
    for tile in range(tiles):
        own_level = levels_of(own_ref[tile, ROWS:SLOT, :])
        mine = [(filled > 0) & (number == tile) for number, _, filled in routes]
        levels = [own_level] + [
            jnp.where(used, level, -jnp.inf) for used, level in zip(mine, slot_levels)
        ]
        highest = functools.reduce(jnp.maximum, levels)
        factors = [jnp.exp(level - highest) for level in levels]
        norm = functools.reduce(jnp.add, factors)
        lines = jnp.concatenate([factor / norm for factor in factors], axis=0)
        count = lines.shape[0]
        room = -count % TILE
        if room:
            lines = jnp.concatenate([lines, jnp.zeros((room, TILE), jnp.float32)], axis=0)
        columns = jnp.concatenate(
            [lines[part * TILE : (part + 1) * TILE].T for part in range(lines.shape[0] // TILE)],
            axis=1,
        )
        for head in range(GROUP):
            part = slice(head * TILE, (head + 1) * TILE)
            blend[part, :] = columns[:, head : head + 1] * own_ref[tile, part, :].astype(jnp.float32)
        for index, used in enumerate(mine):

            @pl.when(used)
            def _(index=index, columns=columns):
                for head in range(GROUP):
                    part = slice(head * TILE, (head + 1) * TILE)
                    column = (index + 1) * GROUP + head
                    blend[part, :] += columns[:, column : column + 1] * slots[index][part, :].astype(
                        jnp.float32
                    )

        for head in range(GROUP):
            out_ref[tile * TILE : (tile + 1) * TILE, head * HD : (head + 1) * HD] = blend[
                head * TILE : (head + 1) * TILE, :
            ].astype(jnp.bfloat16)


def combine(me, selected, own, slots, blocks):
    tiles = own.shape[0]
    seq_count = len(slots)
    return pl.pallas_call(
        functools.partial(combine_kernel, tiles, blocks, seq_count),
        out_shape=jax.ShapeDtypeStruct((tiles * TILE, GROUP * HD), jnp.bfloat16),
        in_specs=[smem, smem, vmem] + [vmem] * seq_count,
        out_specs=vmem,
        scratch_shapes=[pltpu.VMEM((ROWS, HD), jnp.float32)],
        compiler_params=params(),
        name="combine_pieces",
    )(me, selected, own, *slots)


def project_kernel(heads, me_ref, *refs):
    attentions, shards, out_ref = refs[:heads], refs[heads:-1], refs[-1]
    width = shards[0].shape[1]
    order = len(shards) // heads
    z, x, h = me_ref[0], me_ref[1], me_ref[2]
    for side in range(order):
        total = None
        for index in range(heads):
            place = (z ^ index) ^ h
            left = attentions[0][...]
            for other in range(1, heads):
                left = jnp.where(place == other, attentions[other][...], left)
            term = jnp.dot(left, shards[side * heads + index][...], preferred_element_type=jnp.float32)
            total = term if total is None else total + term
        start = pl.multiple_of((x ^ side) * width, width)
        out_ref[:, pl.ds(start, width)] = total.astype(jnp.bfloat16)


def project(numbers, attentions, shards):
    rows, width = attentions[0].shape[0], shards[0].shape[1]
    heads = len(attentions)
    columns = width * len(shards) // heads
    return pl.pallas_call(
        functools.partial(project_kernel, heads),
        out_shape=jax.ShapeDtypeStruct((rows, columns), jnp.bfloat16),
        in_specs=[smem] + [vmem] * (heads + len(shards)),
        out_specs=vmem,
        compiler_params=params(),
        name="project",
    )(numbers, *attentions, *shards)


def pairs(count, offset):
    return [(index, index ^ offset) for index in range(count)]


def spread_weight(weight, kvh_count):
    joint = ("seq", "kvh")

    def jump(flip):
        moves = []
        for z in range(kvh_count):
            for x in range(2):
                for h in range(kvh_count):
                    moves.append(((z * 2 + x) * kvh_count + h, ((h ^ flip) * 2 + x) * kvh_count + z))
        return lax.ppermute(weight, joint, moves)

    seq_count = 2 * kvh_count
    shards = [None] * kvh_count
    for index in range(0, kvh_count, 2):
        shards[index] = jump(index)
        shards[index + 1] = lax.ppermute(shards[index], "seq", pairs(seq_count, 2))
    return shards + [lax.ppermute(shard, "seq", pairs(seq_count, 1)) for shard in shards]


def per_device(queries, kv_cache, selected, out_weight):
    seq_count, kvh_count = lax.axis_size("seq"), lax.axis_size("kvh")
    seq, kvh = lax.axis_index("seq"), lax.axis_index("kvh")
    blocks = kv_cache.shape[1] // BLK
    me = seq.astype(jnp.int32).reshape(1)
    requests = selected.reshape(-1)
    outgoing = pack(me, requests, queries, seq_count, blocks)
    arrived = [outgoing[0]] + [
        lax.ppermute(outgoing[offset], "seq", pairs(seq_count, offset))
        for offset in range(1, seq_count)
    ]
    own = own_pieces(queries, kv_cache)
    returned = [
        serve(arrived[0], kv_cache)
    ] + [
        lax.ppermute(serve(arrived[offset], kv_cache), "seq", pairs(seq_count, offset))
        for offset in range(1, seq_count)
    ]
    attention = combine(me, requests, own, returned, blocks)
    if seq_count == 2 * kvh_count and kvh_count & (kvh_count - 1) == 0:
        shards = spread_weight(out_weight, kvh_count)
        gathered = [attention]
        bit = kvh_count // 2
        parts = {0: attention}
        while bit:
            for offset in list(parts):
                parts[offset | bit] = lax.ppermute(parts[offset], "kvh", pairs(kvh_count, bit))
            bit //= 2
        gathered = [parts[offset] for offset in range(kvh_count)]
        numbers = jnp.stack([seq // 2, seq % 2, kvh]).astype(jnp.int32)
        return project(numbers, gathered, shards)
    column_terms = jnp.dot(
        attention,
        lax.all_gather(out_weight, "seq", axis=1, tiled=True),
        preferred_element_type=jnp.float32,
    )
    return lax.psum_scatter(
        column_terms.astype(jnp.bfloat16), "kvh", scatter_dimension=1, tiled=True
    )


def solution(mesh):
    in_specs = (P("seq", "kvh"), P(None, "seq", "kvh"), P("seq", "kvh", None), P("kvh", "seq"))
    out_specs = P("seq", "kvh")
    return jax.shard_map(
        per_device, mesh=mesh, in_specs=in_specs, out_specs=out_specs, check_vma=False
    )
```

time: 228 us -> 157 us (0.69)
  matrix products: 32.3 us -> 0 us
  starting transfers between devices: 17.8 us -> 45.9 us
  local copies, waits for them, and re-layouts: 29.1 us -> 5.4 us
  Pallas kernels: 0 us -> 22.5 us
  loops' own time: 16.8 us -> 0 us
  blocking collectives: 15.2 us -> 0 us
  between operations: 13.6 us -> 0.17 us
  other arithmetic: 13.5 us -> 1.42 us
  waiting for transfers between devices: 89.6 us -> 81.2 us
    ppermute x0 -> x25, waiting for transfers between devices: none -> 81.2 us  [the longest x4 34.9 us: spread_weight(): lax.ppermute(shard, 'seq', pairs(seq_count, 1))]
    all_to_all x4 -> x0, waiting for transfers between devices: 59.4 us -> none  [the longest x1 38.6 us: per_device(): lax.all_to_all(outgoing, 'seq', split_axis=0, concat_axis=0, tiled=True)]
    ppermute x0 -> x25, starting transfers between devices: none -> 45.9 us  [the longest x7 18.6 us: per_device(): lax.ppermute(outgoing[offset], 'seq', pairs(seq_count, offset))]
    dot_general x18 -> x0, matrix products: 32.3 us -> none  [the longest x8 14.8 us: attend(): jnp.einsum('igd,kd->gik', query_tile, key_rows, preferred_element_type=jn...]
    reduce_scatter x1 -> x0, waiting for transfers between devices: 29.5 us -> none  [per_device(): lax.psum_scatter(column_terms.astype(jnp.bfloat16), 'kvh', scatter_dimens...]
    pallas_call x0 -> x12, Pallas kernels: none -> 22.5 us  [the longest x8 13.1 us: serve(): pl.pallas_call(serve_kernel, out_shape=jax.ShapeDtypeStruct((SLOT, HD), j...]
    all_to_all x4 -> x0, starting transfers between devices: 17.7 us -> none  [the longest x1 7.25 us: per_device(): lax.all_to_all(slot_info, 'seq', split_axis=0, concat_axis=0, tiled=True)]
    another operation x10 -> x0, loops' own time: 16.8 us -> none  [the longest x8 11.1 us: serve(): return lax.cond(info[0] > 0, work, skip, 0)]
  transfers between devices with their start and end apart: 6 -> 25, of which waited for: 5 -> 11; matrix products, arithmetic and copies ran while one was open for 30% -> 1% of each run, Pallas kernels for 0% -> 12%
where the time goes in v1:
time: 157 us
  waiting for transfers between devices  81.2 us (52%)
  starting transfers between devices  45.9 us (29%)
  Pallas kernels  22.5 us (14%)
  local copies, waits for them, and re-layouts  5.4 us (3%)
    ppermute x4, waiting for transfers between devices, spread_weight(): lax.ppermute(shard, 'seq', pairs(seq_count, 1))  34.9 us
    ppermute x7, waiting for transfers between devices, per_device(): lax.ppermute(serve(arrived[offset], kv_cache), 'seq', pairs(seq_count, of...  20.7 us
    ppermute x7, waiting for transfers between devices, per_device(): lax.ppermute(outgoing[offset], 'seq', pairs(seq_count, offset))  19.1 us
    ppermute x7, starting transfers between devices, per_device(): lax.ppermute(outgoing[offset], 'seq', pairs(seq_count, offset))  18.6 us
    pallas_call x8, Pallas kernels, serve(): pl.pallas_call(serve_kernel, out_shape=jax.ShapeDtypeStruct((SLOT, HD), j...  13.1 us
    ppermute x7, starting transfers between devices, per_device(): lax.ppermute(serve(arrived[offset], kv_cache), 'seq', pairs(seq_count, of...  11 us
    ppermute x2, starting transfers between devices, jump(): return lax.ppermute(weight, joint, moves)  7.28 us
    ppermute x3, waiting for transfers between devices, per_device(): lax.ppermute(parts[offset], 'kvh', pairs(kvh_count, bit))  6.55 us
  transfers between devices with their start and end apart: 25, of which 11 were waited for; matrix products, arithmetic and copies ran while one was open for 1% of the time, Pallas kernels for 12%

profile of v1, /device:TPU:0, one launch (start us, length us, event | category | flops | bytes accessed | tf_op | source)
XLA Modules:
  0.0 156.7 jit_solution(17272804028156696517)
XLA Ops:
  0.0 1.7 %collective-permute-start.17 = (bf16[512,512]{1,0:T(8,128)(2,1)}, bf16[512,512]{1,0:T(8,128)(2,1)S(1)}, u32[]{:S(2)}, u32[]{:S(2)}) collective-permute-start(bf16[512,512]{1,0:T(8,128)(2,1)} %param.7), channel_id=1, source_target_pairs={{0,0},{1,8},{2,16},{3,24},{4,4},{5,12},{6,20},{7,28},{8,1},{9,9},{... | collective-permute-start | bytes 1572872 | tf_op jit(solution)/shard_map/ppermute | solution.py:278
  1.7 5.6 %collective-permute-start.19 = (bf16[512,512]{1,0:T(8,128)(2,1)}, bf16[512,512]{1,0:T(8,128)(2,1)S(1)}, u32[]{:S(2)}, u32[]{:S(2)}) collective-permute-start(bf16[512,512]{1,0:T(8,128)(2,1)} %param.7), channel_id=1, source_target_pairs={{0,16},{1,24},{2,0},{3,8},{4,20},{5,28},{6,4},{7,12},{8,17},{9,25}... | collective-permute-start | bytes 1572872 | tf_op jit(solution)/shard_map/ppermute | solution.py:278
  7.3 0.5 broadcast.5
  7.8 1.3 reduce.3
  9.1 0.1 reshape.7.selected_ref
  9.2 0.9 copy-done.2
  10.2 0.8 pack_queries.1
  11.0 1.6 collective-permute-start
  12.5 2.4 %collective-permute-start.10 = (bf16[528,128]{1,0:T(8,128)(2,1)S(1)}, bf16[528,128]{1,0:T(8,128)(2,1)S(1)}, u32[]{:S(2)}, u32[]{:S(2)}) collective-permute-start(bf16[528,128]{1,0:T(8,128)(2,1)S(1)} %get-tuple-element.19), channel_id=1, source_target_pairs={{0,24},{4,28},{8,16},{12,20},{16,8},{20,12},{24,0},{28,4},{1,25},{... | collective-permute-start | bytes 405512 | tf_op jit(solution)/shard_map/ppermute | solution.py:296
  14.9 1.4 collective-permute-start.12
  16.3 0.7 collective-permute-done.slot_ref
  17.0 0.4 collective-permute-start.2
  17.4 14.2 %collective-permute-done.10.slot_ref = bf16[528,128]{1,0:T(8,128)(2,1)S(1)} collective-permute-done((bf16[528,128]{1,0:T(8,128)(2,1)S(1)}, bf16[528,128]{1,0:T(8,128)(2,1)S(1)}, u32[]{:S(2)}, u32[]{:S(2)}) %collective-permute-start.10) | collective-permute-done | bytes 135200 | tf_op jit(solution)/shard_map/ppermute | solution.py:296
  31.6 9.9 %collective-permute-start.4 = (bf16[528,128]{1,0:T(8,128)(2,1)S(1)}, bf16[528,128]{1,0:T(8,128)(2,1)S(1)}, u32[]{:S(2)}, u32[]{:S(2)}) collective-permute-start(bf16[528,128]{1,0:T(8,128)(2,1)S(1)} %get-tuple-element.16), channel_id=1, source_target_pairs={{0,12},{4,8},{8,4},{12,0},{16,28},{20,24},{24,20},{28,16},{1,13},{... | collective-permute-start | bytes 405512 | tf_op jit(solution)/shard_map/ppermute | solution.py:296
  41.5 2.2 %copy-done = bf16[2,8192,128]{2,1,0:T(8,128)(2,1)S(1)} copy-done((bf16[2,8192,128]{2,1,0:T(8,128)(2,1)S(1)}, bf16[2,8192,128]{2,1,0:T(8,128)(2,1)}, u32[]{:S(2)}) %copy-start) | copy-done | bytes 4194328
  43.7 1.6 %serve_slot.9 = bf16[528,128]{1,0:T(8,128)(2,1)S(1)} custom-call(bf16[528,128]{1,0:T(8,128)(2,1)S(1)} %collective-permute-done.slot_ref, bf16[2,8192,128]{2,1,0:T(8,128)(2,1)S(1)} %copy-done), custom_call_target="tpu_custom_call" | custom-call | flops 268435456 | bytes 524288 | tf_op jit(solution)/shard_map/serve_slot/pallas_call | solution.py:151
  45.3 0.0 collective-permute-done.12.slot_ref
  45.3 0.7 collective-permute-start.6
  46.1 0.0 collective-permute-done.2.slot_ref
  46.1 2.2 %collective-permute-start.8 = (bf16[528,128]{1,0:T(8,128)(2,1)S(1)}, bf16[528,128]{1,0:T(8,128)(2,1)S(1)}, u32[]{:S(2)}, u32[]{:S(2)}) collective-permute-start(bf16[528,128]{1,0:T(8,128)(2,1)S(1)} %get-tuple-element.18), channel_id=1, source_target_pairs={{0,20},{4,16},{8,28},{12,24},{16,4},{20,0},{24,12},{28,8},{1,21},{... | collective-permute-start | bytes 405512 | tf_op jit(solution)/shard_map/ppermute | solution.py:296
  48.3 1.5 collective-permute-start.1
  49.8 1.6 %serve_slot.14 = bf16[528,128]{1,0:T(8,128)(2,1)S(1)} custom-call(bf16[528,128]{1,0:T(8,128)(2,1)S(1)} %collective-permute-done.10.slot_ref, bf16[2,8192,128]{2,1,0:T(8,128)(2,1)S(1)} %copy-done), custom_call_target="tpu_custom_call" | custom-call | flops 268435456 | bytes 524288 | tf_op jit(solution)/shard_map/serve_slot/pallas_call | solution.py:151
  51.4 1.6 %serve_slot.15 = bf16[528,128]{1,0:T(8,128)(2,1)S(1)} custom-call(bf16[528,128]{1,0:T(8,128)(2,1)S(1)} %collective-permute-done.12.slot_ref, bf16[2,8192,128]{2,1,0:T(8,128)(2,1)S(1)} %copy-done), custom_call_target="tpu_custom_call" | custom-call | flops 268435456 | bytes 524288 | tf_op jit(solution)/shard_map/serve_slot/pallas_call | solution.py:151
  53.1 1.6 %serve_slot.10 = bf16[528,128]{1,0:T(8,128)(2,1)S(1)} custom-call(bf16[528,128]{1,0:T(8,128)(2,1)S(1)} %collective-permute-done.2.slot_ref, bf16[2,8192,128]{2,1,0:T(8,128)(2,1)S(1)} %copy-done), custom_call_target="tpu_custom_call" | custom-call | flops 268435456 | bytes 524288 | tf_op jit(solution)/shard_map/serve_slot/pallas_call | solution.py:151
  54.7 2.7 %collective-permute-done.6.slot_ref = bf16[528,128]{1,0:T(8,128)(2,1)S(1)} collective-permute-done((bf16[528,128]{1,0:T(8,128)(2,1)S(1)}, bf16[528,128]{1,0:T(8,128)(2,1)S(1)}, u32[]{:S(2)}, u32[]{:S(2)}) %collective-permute-start.6) | collective-permute-done | bytes 135200 | tf_op jit(solution)/shard_map/ppermute | solution.py:296
  57.4 1.4 collective-permute-start.11
  58.8 1.5 collective-permute-done.8.slot_ref
  60.3 2.3 %collective-permute-start.13 = (bf16[528,128]{1,0:T(8,128)(2,1)S(1)}, bf16[528,128]{1,0:T(8,128)(2,1)S(1)}, u32[]{:S(2)}, u32[]{:S(2)}) collective-permute-start(bf16[528,128]{1,0:T(8,128)(2,1)S(1)} %serve_slot.15), channel_id=1, source_target_pairs={{0,28},{4,24},{8,20},{12,16},{16,12},{20,8},{24,4},{28,0},{1,29},{... | collective-permute-start | bytes 405512 | tf_op jit(solution)/shard_map/ppermute | solution.py:303
  62.6 0.0 collective-permute-done.1.refs_1_
  62.6 0.0 collective-permute-start.3
  62.6 0.0 collective-permute-done.17.refs_4_
  62.6 2.0 %collective-permute-start.18 = (bf16[512,512]{1,0:T(8,128)(2,1)S(1)}, bf16[512,512]{1,0:T(8,128)(2,1)S(1)}, u32[]{:S(2)}, u32[]{:S(2)}) collective-permute-start(bf16[512,512]{1,0:T(8,128)(2,1)S(1)} %collective-permute-done.17.refs_4_), channel_id=1, source_target_pairs={{0,8},{4,12},{8,0},{12,4},{16,24},{20,28},{24,16},{28,20},{1,9},{5... | collective-permute-start | bytes 1572872 | tf_op jit(solution)/shard_map/ppermute | solution.py:284
  64.6 0.0 collective-permute-done.19.refs_6_
  64.6 0.1 collective-permute-start.20
  64.7 1.6 %serve_slot.11 = bf16[528,128]{1,0:T(8,128)(2,1)S(1)} custom-call(bf16[528,128]{1,0:T(8,128)(2,1)S(1)} %collective-permute-done.4.slot_ref, bf16[2,8192,128]{2,1,0:T(8,128)(2,1)S(1)} %copy-done), custom_call_target="tpu_custom_call" | custom-call | flops 268435456 | bytes 524288 | tf_op jit(solution)/shard_map/serve_slot/pallas_call | solution.py:151
  66.3 1.6 %serve_slot.12 = bf16[528,128]{1,0:T(8,128)(2,1)S(1)} custom-call(bf16[528,128]{1,0:T(8,128)(2,1)S(1)} %collective-permute-done.6.slot_ref, bf16[2,8192,128]{2,1,0:T(8,128)(2,1)S(1)} %copy-done), custom_call_target="tpu_custom_call" | custom-call | flops 268435456 | bytes 524288 | tf_op jit(solution)/shard_map/serve_slot/pallas_call | solution.py:151
  68.0 0.0 copy-start.1
  68.0 0.0 copy-start.3
  68.0 1.6 %serve_slot.13 = bf16[528,128]{1,0:T(8,128)(2,1)S(1)} custom-call(bf16[528,128]{1,0:T(8,128)(2,1)S(1)} %collective-permute-done.8.slot_ref, bf16[2,8192,128]{2,1,0:T(8,128)(2,1)S(1)} %copy-done), custom_call_target="tpu_custom_call" | custom-call | flops 268435456 | bytes 524288 | tf_op jit(solution)/shard_map/serve_slot/pallas_call | solution.py:151
  69.7 3.0 %collective-permute-start.5 = (bf16[528,128]{1,0:T(8,128)(2,1)S(1)}, bf16[528,128]{1,0:T(8,128)(2,1)S(1)}, u32[]{:S(2)}, u32[]{:S(2)}) collective-permute-start(bf16[528,128]{1,0:T(8,128)(2,1)S(1)} %serve_slot.11), channel_id=1, source_target_pairs={{0,12},{4,8},{8,4},{12,0},{16,28},{20,24},{24,20},{28,16},{1,13},{... | collective-permute-start | bytes 405512 | tf_op jit(solution)/shard_map/ppermute | solution.py:303
  72.6 0.0 collective-permute-done.13.refs_7_
  72.6 0.6 collective-permute-start.7
  73.2 0.0 collective-permute-done.3.refs_2_
  73.2 2.3 %collective-permute-start.9 = (bf16[528,128]{1,0:T(8,128)(2,1)S(1)}, bf16[528,128]{1,0:T(8,128)(2,1)S(1)}, u32[]{:S(2)}, u32[]{:S(2)}) collective-permute-start(bf16[528,128]{1,0:T(8,128)(2,1)S(1)} %serve_slot.13), channel_id=1, source_target_pairs={{0,20},{4,16},{8,28},{12,24},{16,4},{20,0},{24,12},{28,8},{1,21},{... | collective-permute-start | bytes 405512 | tf_op jit(solution)/shard_map/ppermute | solution.py:303
  75.5 1.6 %serve_slot.8.refs_0_ = bf16[528,128]{1,0:T(8,128)(2,1)S(1)} custom-call(bf16[528,128]{1,0:T(8,128)(2,1)S(1)} %get-tuple-element.13.slot_ref, bf16[2,8192,128]{2,1,0:T(8,128)(2,1)S(1)} %copy-done), custom_call_target="tpu_custom_call" | custom-call | flops 268435456 | bytes 524288 | tf_op jit(solution)/shard_map/serve_slot/pallas_call | solution.py:151
  77.2 3.5 %own_pieces.1.own_ref = bf16[2,528,128]{2,1,0:T(8,128)(2,1)S(1)} custom-call(bf16[256,512]{1,0:T(8,128)(2,1)S(1)} %copy-done.3, bf16[2,8192,128]{2,1,0:T(8,128)(2,1)S(1)} %copy-done.1), custom_call_target="tpu_custom_call" | custom-call | flops 536870912 | bytes 524288 | tf_op jit(solution)/shard_map/own_pieces/pallas_call | solution.py:120
  80.6 20.7 %collective-permute-done.5.refs_3_ = bf16[528,128]{1,0:T(8,128)(2,1)S(1)} collective-permute-done((bf16[528,128]{1,0:T(8,128)(2,1)S(1)}, bf16[528,128]{1,0:T(8,128)(2,1)S(1)}, u32[]{:S(2)}, u32[]{:S(2)}) %collective-permute-start.5) | collective-permute-done | bytes 135200 | tf_op jit(solution)/shard_map/ppermute | solution.py:303
  101.3 0.0 collective-permute-done.7.refs_4_
  101.3 1.8 %combine_pieces.1.refs_0_ = bf16[256,512]{1,0:T(8,128)(2,1)S(1)} custom-call(s32[1]{0:T(128)} %bitcast.3.me_ref, s32[4]{0:T(128)S(1)} %reshape.7.selected_ref, bf16[2,528,128]{2,1,0:T(8,128)(2,1)S(1)} %own_pieces.1.own_ref, bf16[528,128]{1,0:T(8,128)(2,1)S(1)} %serve_slot.8.refs_0_, bf16[528,128]{1,0:T(8,128)(2,1)S(1)} %collective-permute-done.1.refs_1_, ...), custom_call_target="tpu_custom_call" | custom-call | tf_op jit(solution)/shard_map/combine_pieces/pallas_call | solution.py:222
  103.1 1.1 collective-permute-start.15
  104.2 1.5 collective-permute-start.21
  105.7 4.7 %collective-permute-done.15.refs_2_ = bf16[256,512]{1,0:T(8,128)(2,1)} collective-permute-done((bf16[256,512]{1,0:T(8,128)(2,1)S(1)}, bf16[256,512]{1,0:T(8,128)(2,1)}, u32[]{:S(2)}, u32[]{:S(2)}) %collective-permute-start.15) | collective-permute-done | bytes 262176 | tf_op jit(solution)/shard_map/ppermute | solution.py:314
  110.4 2.3 %collective-permute-start.23 = (bf16[512,512]{1,0:T(8,128)(2,1)S(1)}, bf16[512,512]{1,0:T(8,128)(2,1)S(1)}, u32[]{:S(2)}, u32[]{:S(2)}) collective-permute-start(bf16[512,512]{1,0:T(8,128)(2,1)S(1)} %collective-permute-done.19.refs_6_), channel_id=1, source_target_pairs={{0,4},{4,0},{8,12},{12,8},{16,20},{20,16},{24,28},{28,24},{1,5},{5... | collective-permute-start | bytes 1572872 | tf_op jit(solution)/shard_map/ppermute | solution.py:285
  112.8 0.0 collective-permute-start.22
  112.8 2.0 %collective-permute-start.24 = (bf16[512,512]{1,0:T(8,128)(2,1)S(1)}, bf16[512,512]{1,0:T(8,128)(2,1)}, u32[]{:S(2)}, u32[]{:S(2)}) collective-permute-start(bf16[512,512]{1,0:T(8,128)(2,1)S(1)} %collective-permute-done.20.refs_7_), channel_id=1, source_target_pairs={{0,4},{4,0},{8,12},{12,8},{16,20},{20,16},{24,28},{28,24},{1,5},{5... | collective-permute-start | bytes 1572872 | tf_op jit(solution)/shard_map/ppermute | solution.py:285
  114.8 0.7 copy-done.4
  115.5 0.1 pad_add_fusion.me_ref
  115.6 1.8 %collective-permute-done.16.refs_3_ = bf16[256,512]{1,0:T(8,128)(2,1)} collective-permute-done((bf16[256,512]{1,0:T(8,128)(2,1)}, bf16[256,512]{1,0:T(8,128)(2,1)}, u32[]{:S(2)}, u32[]{:S(2)}) %collective-permute-start.16) | collective-permute-done | bytes 262176 | tf_op jit(solution)/shard_map/ppermute | solution.py:314
  117.4 1.5 collective-permute-done.21.refs_8_
  118.9 11.2 %collective-permute-done.23.refs_10_ = bf16[512,512]{1,0:T(8,128)(2,1)S(1)} collective-permute-done((bf16[512,512]{1,0:T(8,128)(2,1)S(1)}, bf16[512,512]{1,0:T(8,128)(2,1)S(1)}, u32[]{:S(2)}, u32[]{:S(2)}) %collective-permute-start.23) | collective-permute-done | bytes 524320 | tf_op jit(solution)/shard_map/ppermute | solution.py:285
  130.1 11.3 %collective-permute-done.22.refs_9_ = bf16[512,512]{1,0:T(8,128)(2,1)} collective-permute-done((bf16[512,512]{1,0:T(8,128)(2,1)S(1)}, bf16[512,512]{1,0:T(8,128)(2,1)}, u32[]{:S(2)}, u32[]{:S(2)}) %collective-permute-start.22) | collective-permute-done | bytes 524320 | tf_op jit(solution)/shard_map/ppermute | solution.py:285
  141.4 10.9 %collective-permute-done.24.refs_11_ = bf16[512,512]{1,0:T(8,128)(2,1)} collective-permute-done((bf16[512,512]{1,0:T(8,128)(2,1)S(1)}, bf16[512,512]{1,0:T(8,128)(2,1)}, u32[]{:S(2)}, u32[]{:S(2)}) %collective-permute-start.24) | collective-permute-done | bytes 524320 | tf_op jit(solution)/shard_map/ppermute | solution.py:285
  152.3 0.9 copy-done.5
  153.3 3.4 %project.1 = bf16[256,1024]{1,0:T(8,128)(2,1)} custom-call(s32[3]{0:T(128)S(1)} %pad_add_fusion.me_ref, bf16[256,512]{1,0:T(8,128)(2,1)S(1)} %combine_pieces.1.refs_0_, bf16[256,512]{1,0:T(8,128)(2,1)S(1)} %copy-done.5, bf16[256,512]{1,0:T(8,128)(2,1)} %collective-permute-done.15.refs_2_, bf16[256,512]{1,0:T(8,128)(2,1)} %collective-permute-done.16.refs_3_, ...), custom_call_target="tpu_custom_call" | custom-call | tf_op jit(solution)/shard_map/project/pallas_call | solution.py:255
  (14 shorter events, 0.0 us)
Async XLA Ops:
  0.0 62.6 %collective-permute-start.17 = (bf16[512,512]{1,0:T(8,128)(2,1)}, bf16[512,512]{1,0:T(8,128)(2,1)S(1)}, u32[]{:S(2)}, u32[]{:S(2)}) collective-permute-start(bf16[512,512]{1,0:T(8,128)(2,1)} %param.7), channel_id=1, source_target_pairs={{0,0},{1,8},{2,16},{3,24},{4,4},{5,12},{6,20},{7,28},{8,1},{9,9},{... | collective-permute-start | bytes 1572872 | tf_op jit(solution)/shard_map/ppermute | solution.py:278
  1.7 62.9 %collective-permute-start.19 = (bf16[512,512]{1,0:T(8,128)(2,1)}, bf16[512,512]{1,0:T(8,128)(2,1)S(1)}, u32[]{:S(2)}, u32[]{:S(2)}) collective-permute-start(bf16[512,512]{1,0:T(8,128)(2,1)} %param.7), channel_id=1, source_target_pairs={{0,16},{1,24},{2,0},{3,8},{4,20},{5,28},{6,4},{7,12},{8,17},{9,25}... | collective-permute-start | bytes 1572872 | tf_op jit(solution)/shard_map/ppermute | solution.py:278
  9.2 0.9 copy-start.2
  11.0 6.0 %collective-permute-start = (bf16[528,128]{1,0:T(8,128)(2,1)S(1)}, bf16[528,128]{1,0:T(8,128)(2,1)S(1)}, u32[]{:S(2)}, u32[]{:S(2)}) collective-permute-start(bf16[528,128]{1,0:T(8,128)(2,1)S(1)} %get-tuple-element.14), channel_id=1, source_target_pairs={{0,4},{4,0},{8,12},{12,8},{16,20},{20,16},{24,28},{28,24},{1,5},{5... | collective-permute-start | bytes 405512 | tf_op jit(solution)/shard_map/ppermute | solution.py:296
  12.5 19.1 %collective-permute-start.10 = (bf16[528,128]{1,0:T(8,128)(2,1)S(1)}, bf16[528,128]{1,0:T(8,128)(2,1)S(1)}, u32[]{:S(2)}, u32[]{:S(2)}) collective-permute-start(bf16[528,128]{1,0:T(8,128)(2,1)S(1)} %get-tuple-element.19), channel_id=1, source_target_pairs={{0,24},{4,28},{8,16},{12,20},{16,8},{20,12},{24,0},{28,4},{1,25},{... | collective-permute-start | bytes 405512 | tf_op jit(solution)/shard_map/ppermute | solution.py:296
  14.9 30.4 %collective-permute-start.12 = (bf16[528,128]{1,0:T(8,128)(2,1)S(1)}, bf16[528,128]{1,0:T(8,128)(2,1)S(1)}, u32[]{:S(2)}, u32[]{:S(2)}) collective-permute-start(bf16[528,128]{1,0:T(8,128)(2,1)S(1)} %get-tuple-element.20), channel_id=1, source_target_pairs={{0,28},{4,24},{8,20},{12,16},{16,12},{20,8},{24,4},{28,0},{1,29},{... | collective-permute-start | bytes 405512 | tf_op jit(solution)/shard_map/ppermute | solution.py:296
  17.0 29.1 %collective-permute-start.2 = (bf16[528,128]{1,0:T(8,128)(2,1)S(1)}, bf16[528,128]{1,0:T(8,128)(2,1)S(1)}, u32[]{:S(2)}, u32[]{:S(2)}) collective-permute-start(bf16[528,128]{1,0:T(8,128)(2,1)S(1)} %get-tuple-element.15), channel_id=1, source_target_pairs={{0,8},{4,12},{8,0},{12,4},{16,24},{20,28},{24,16},{28,20},{1,9},{5... | collective-permute-start | bytes 405512 | tf_op jit(solution)/shard_map/ppermute | solution.py:296
  31.6 16.7 %collective-permute-start.4 = (bf16[528,128]{1,0:T(8,128)(2,1)S(1)}, bf16[528,128]{1,0:T(8,128)(2,1)S(1)}, u32[]{:S(2)}, u32[]{:S(2)}) collective-permute-start(bf16[528,128]{1,0:T(8,128)(2,1)S(1)} %get-tuple-element.16), channel_id=1, source_target_pairs={{0,12},{4,8},{8,4},{12,0},{16,28},{20,24},{24,20},{28,16},{1,13},{... | collective-permute-start | bytes 405512 | tf_op jit(solution)/shard_map/ppermute | solution.py:296
  41.5 2.2 %copy-start = (bf16[2,8192,128]{2,1,0:T(8,128)(2,1)S(1)}, bf16[2,8192,128]{2,1,0:T(8,128)(2,1)}, u32[]{:S(2)}) copy-start(bf16[2,8192,128]{2,1,0:T(8,128)(2,1)} %kv_ref.17) | copy-start | bytes 12582916
  45.3 12.1 %collective-permute-start.6 = (bf16[528,128]{1,0:T(8,128)(2,1)S(1)}, bf16[528,128]{1,0:T(8,128)(2,1)S(1)}, u32[]{:S(2)}, u32[]{:S(2)}) collective-permute-start(bf16[528,128]{1,0:T(8,128)(2,1)S(1)} %get-tuple-element.17), channel_id=1, source_target_pairs={{0,16},{4,20},{8,24},{12,28},{16,0},{20,4},{24,8},{28,12},{1,17},{... | collective-permute-start | bytes 405512 | tf_op jit(solution)/shard_map/ppermute | solution.py:296
  46.1 14.2 %collective-permute-start.8 = (bf16[528,128]{1,0:T(8,128)(2,1)S(1)}, bf16[528,128]{1,0:T(8,128)(2,1)S(1)}, u32[]{:S(2)}, u32[]{:S(2)}) collective-permute-start(bf16[528,128]{1,0:T(8,128)(2,1)S(1)} %get-tuple-element.18), channel_id=1, source_target_pairs={{0,20},{4,16},{8,28},{12,24},{16,4},{20,0},{24,12},{28,8},{1,21},{... | collective-permute-start | bytes 405512 | tf_op jit(solution)/shard_map/ppermute | solution.py:296
  48.3 14.3 %collective-permute-start.1 = (bf16[528,128]{1,0:T(8,128)(2,1)S(1)}, bf16[528,128]{1,0:T(8,128)(2,1)S(1)}, u32[]{:S(2)}, u32[]{:S(2)}) collective-permute-start(bf16[528,128]{1,0:T(8,128)(2,1)S(1)} %serve_slot.9), channel_id=1, source_target_pairs={{0,4},{4,0},{8,12},{12,8},{16,20},{20,16},{24,28},{28,24},{1,5},{5... | collective-permute-start | bytes 405512 | tf_op jit(solution)/shard_map/ppermute | solution.py:303
  57.4 12.2 %collective-permute-start.11 = (bf16[528,128]{1,0:T(8,128)(2,1)S(1)}, bf16[528,128]{1,0:T(8,128)(2,1)S(1)}, u32[]{:S(2)}, u32[]{:S(2)}) collective-permute-start(bf16[528,128]{1,0:T(8,128)(2,1)S(1)} %serve_slot.14), channel_id=1, source_target_pairs={{0,24},{4,28},{8,16},{12,20},{16,8},{20,12},{24,0},{28,4},{1,25},{... | collective-permute-start | bytes 405512 | tf_op jit(solution)/shard_map/ppermute | solution.py:303
  60.3 12.3 %collective-permute-start.13 = (bf16[528,128]{1,0:T(8,128)(2,1)S(1)}, bf16[528,128]{1,0:T(8,128)(2,1)S(1)}, u32[]{:S(2)}, u32[]{:S(2)}) collective-permute-start(bf16[528,128]{1,0:T(8,128)(2,1)S(1)} %serve_slot.15), channel_id=1, source_target_pairs={{0,28},{4,24},{8,20},{12,16},{16,12},{20,8},{24,4},{28,0},{1,29},{... | collective-permute-start | bytes 405512 | tf_op jit(solution)/shard_map/ppermute | solution.py:303
  62.6 10.6 %collective-permute-start.3 = (bf16[528,128]{1,0:T(8,128)(2,1)S(1)}, bf16[528,128]{1,0:T(8,128)(2,1)S(1)}, u32[]{:S(2)}, u32[]{:S(2)}) collective-permute-start(bf16[528,128]{1,0:T(8,128)(2,1)S(1)} %serve_slot.10), channel_id=1, source_target_pairs={{0,8},{4,12},{8,0},{12,4},{16,24},{20,28},{24,16},{28,20},{1,9},{5... | collective-permute-start | bytes 405512 | tf_op jit(solution)/shard_map/ppermute | solution.py:303
  62.6 50.2 %collective-permute-start.18 = (bf16[512,512]{1,0:T(8,128)(2,1)S(1)}, bf16[512,512]{1,0:T(8,128)(2,1)S(1)}, u32[]{:S(2)}, u32[]{:S(2)}) collective-permute-start(bf16[512,512]{1,0:T(8,128)(2,1)S(1)} %collective-permute-done.17.refs_4_), channel_id=1, source_target_pairs={{0,8},{4,12},{8,0},{12,4},{16,24},{20,28},{24,16},{28,20},{1,9},{5... | collective-permute-start | bytes 1572872 | tf_op jit(solution)/shard_map/ppermute | solution.py:284
  64.6 48.2 %collective-permute-start.20 = (bf16[512,512]{1,0:T(8,128)(2,1)S(1)}, bf16[512,512]{1,0:T(8,128)(2,1)S(1)}, u32[]{:S(2)}, u32[]{:S(2)}) collective-permute-start(bf16[512,512]{1,0:T(8,128)(2,1)S(1)} %collective-permute-done.19.refs_6_), channel_id=1, source_target_pairs={{0,8},{4,12},{8,0},{12,4},{16,24},{20,28},{24,16},{28,20},{1,9},{5... | collective-permute-start | bytes 1572872 | tf_op jit(solution)/shard_map/ppermute | solution.py:284
  68.0 9.2 %copy-start.1 = (bf16[2,8192,128]{2,1,0:T(8,128)(2,1)S(1)}, bf16[2,8192,128]{2,1,0:T(8,128)(2,1)}, u32[]{:S(2)}) copy-start(bf16[2,8192,128]{2,1,0:T(8,128)(2,1)} %kv_ref.17) | copy-start | bytes 12582916
  68.0 9.2 %copy-start.3 = (bf16[256,512]{1,0:T(8,128)(2,1)S(1)}, bf16[256,512]{1,0:T(8,128)(2,1)}, u32[]{:S(2)}) copy-start(bf16[256,512]{1,0:T(8,128)(2,1)} %query_ref.3) | copy-start | bytes 786436
  69.7 31.6 %collective-permute-start.5 = (bf16[528,128]{1,0:T(8,128)(2,1)S(1)}, bf16[528,128]{1,0:T(8,128)(2,1)S(1)}, u32[]{:S(2)}, u32[]{:S(2)}) collective-permute-start(bf16[528,128]{1,0:T(8,128)(2,1)S(1)} %serve_slot.11), channel_id=1, source_target_pairs={{0,12},{4,8},{8,4},{12,0},{16,28},{20,24},{24,20},{28,16},{1,13},{... | collective-permute-start | bytes 405512 | tf_op jit(solution)/shard_map/ppermute | solution.py:303
  72.6 28.7 %collective-permute-start.7 = (bf16[528,128]{1,0:T(8,128)(2,1)S(1)}, bf16[528,128]{1,0:T(8,128)(2,1)S(1)}, u32[]{:S(2)}, u32[]{:S(2)}) collective-permute-start(bf16[528,128]{1,0:T(8,128)(2,1)S(1)} %serve_slot.12), channel_id=1, source_target_pairs={{0,16},{4,20},{8,24},{12,28},{16,0},{20,4},{24,8},{28,12},{1,17},{... | collective-permute-start | bytes 405512 | tf_op jit(solution)/shard_map/ppermute | solution.py:303
  73.2 28.1 %collective-permute-start.9 = (bf16[528,128]{1,0:T(8,128)(2,1)S(1)}, bf16[528,128]{1,0:T(8,128)(2,1)S(1)}, u32[]{:S(2)}, u32[]{:S(2)}) collective-permute-start(bf16[528,128]{1,0:T(8,128)(2,1)S(1)} %serve_slot.13), channel_id=1, source_target_pairs={{0,20},{4,16},{8,28},{12,24},{16,4},{20,0},{24,12},{28,8},{1,21},{... | collective-permute-start | bytes 405512 | tf_op jit(solution)/shard_map/ppermute | solution.py:303
  103.1 7.4 %collective-permute-start.15 = (bf16[256,512]{1,0:T(8,128)(2,1)S(1)}, bf16[256,512]{1,0:T(8,128)(2,1)}, u32[]{:S(2)}, u32[]{:S(2)}) collective-permute-start(bf16[256,512]{1,0:T(8,128)(2,1)S(1)} %combine_pieces.1.refs_0_), channel_id=1, source_target_pairs={{0,2},{1,3},{2,0},{3,1},{4,6},{5,7},{6,4},{7,5},{8,10},{9,11},{10,... | collective-permute-start | bytes 786440 | tf_op jit(solution)/shard_map/ppermute | solution.py:314
  104.2 10.6 %collective-permute-start.14 = (bf16[256,512]{1,0:T(8,128)(2,1)S(1)}, bf16[256,512]{1,0:T(8,128)(2,1)S(1)}, u32[]{:S(2)}, u32[]{:S(2)}) collective-permute-start(bf16[256,512]{1,0:T(8,128)(2,1)S(1)} %combine_pieces.1.refs_0_), channel_id=1, source_target_pairs={{0,1},{1,0},{2,3},{3,2},{4,5},{5,4},{6,7},{7,6},{8,9},{9,8},{10,11... | collective-permute-start | bytes 786440 | tf_op jit(solution)/shard_map/ppermute | solution.py:314
  104.2 14.7 %collective-permute-start.21 = (bf16[512,512]{1,0:T(8,128)(2,1)S(1)}, bf16[512,512]{1,0:T(8,128)(2,1)S(1)}, u32[]{:S(2)}, u32[]{:S(2)}) collective-permute-start(bf16[512,512]{1,0:T(8,128)(2,1)S(1)} %collective-permute-done.17.refs_4_), channel_id=1, source_target_pairs={{0,4},{4,0},{8,12},{12,8},{16,20},{20,16},{24,28},{28,24},{1,5},{5... | collective-permute-start | bytes 1572872 | tf_op jit(solution)/shard_map/ppermute | solution.py:285
  110.4 19.7 %collective-permute-start.23 = (bf16[512,512]{1,0:T(8,128)(2,1)S(1)}, bf16[512,512]{1,0:T(8,128)(2,1)S(1)}, u32[]{:S(2)}, u32[]{:S(2)}) collective-permute-start(bf16[512,512]{1,0:T(8,128)(2,1)S(1)} %collective-permute-done.19.refs_6_), channel_id=1, source_target_pairs={{0,4},{4,0},{8,12},{12,8},{16,20},{20,16},{24,28},{28,24},{1,5},{5... | collective-permute-start | bytes 1572872 | tf_op jit(solution)/shard_map/ppermute | solution.py:285
  112.8 28.7 %collective-permute-start.22 = (bf16[512,512]{1,0:T(8,128)(2,1)S(1)}, bf16[512,512]{1,0:T(8,128)(2,1)}, u32[]{:S(2)}, u32[]{:S(2)}) collective-permute-start(bf16[512,512]{1,0:T(8,128)(2,1)S(1)} %collective-permute-done.18.refs_5_), channel_id=1, source_target_pairs={{0,4},{4,0},{8,12},{12,8},{16,20},{20,16},{24,28},{28,24},{1,5},{5... | collective-permute-start | bytes 1572872 | tf_op jit(solution)/shard_map/ppermute | solution.py:285
  112.8 39.5 %collective-permute-start.24 = (bf16[512,512]{1,0:T(8,128)(2,1)S(1)}, bf16[512,512]{1,0:T(8,128)(2,1)}, u32[]{:S(2)}, u32[]{:S(2)}) collective-permute-start(bf16[512,512]{1,0:T(8,128)(2,1)S(1)} %collective-permute-done.20.refs_7_), channel_id=1, source_target_pairs={{0,4},{4,0},{8,12},{12,8},{16,20},{20,16},{24,28},{28,24},{1,5},{5... | collective-permute-start | bytes 1572872 | tf_op jit(solution)/shard_map/ppermute | solution.py:285
  114.8 0.7 copy-start.4
  115.5 1.9 %collective-permute-start.16 = (bf16[256,512]{1,0:T(8,128)(2,1)}, bf16[256,512]{1,0:T(8,128)(2,1)}, u32[]{:S(2)}, u32[]{:S(2)}) collective-permute-start(bf16[256,512]{1,0:T(8,128)(2,1)} %collective-permute-done.15.refs_2_), channel_id=1, source_target_pairs={{0,1},{1,0},{2,3},{3,2},{4,5},{5,4},{6,7},{7,6},{8,9},{9,8},{10,11... | collective-permute-start | bytes 786440 | tf_op jit(solution)/shard_map/ppermute | solution.py:314
  152.3 1.0 copy-start.5

commit v2 on v1

--- a/solution.py
+++ b/solution.py
@@ -21,7 +21,8 @@
 
 vmem = pl.BlockSpec(memory_space=pltpu.VMEM)
 smem = pl.BlockSpec(memory_space=pltpu.SMEM)
-hbm = pl.BlockSpec(memory_space=pl.ANY)
+hbm = pl.BlockSpec(memory_space=pltpu.HBM)
+anywhere = pl.BlockSpec(memory_space=pl.ANY)
 
 
 def params():
@@ -32,7 +33,7 @@
     own_block = own_seq * blocks + blocks - 1
     tile, block, filled = jnp.int32(0), jnp.int32(0), jnp.int32(0)
     for request in range(tiles * SEL):
-        chosen = selected_ref[request]
+        chosen = selected_ref[request // SEL, 0, request % SEL]
         target = jnp.where(chosen >= own_block, chosen + 1, chosen)
         here = lax.div(target, jnp.int32(blocks)) == peer
         tile = jnp.where(here, request // SEL, tile)
@@ -92,7 +93,8 @@
     out_ref[ROWS:SLOT, :] = parts.astype(jnp.bfloat16)
 
 
-def own_kernel(tiles, blocks, query_ref, kv_ref, out_ref, keys, values, sems):
+def own_kernel(tiles, blocks, query_ref, kv_ref, *refs):
+    out_ref, keys, values, sems = refs[-4:]
     start = (blocks - 1) * BLK
     copies = [
         pltpu.make_async_copy(kv_ref.at[0, pl.ds(start, BLK)], keys, sems.at[0]),
@@ -115,12 +117,12 @@
     lax.fori_loop(0, tiles, one, 0)
 
 
-def own_pieces(queries, kv_cache):
+def own_pieces(queries, kv_cache, after):
     tiles, blocks = queries.shape[0] // TILE, kv_cache.shape[1] // BLK
     return pl.pallas_call(
         functools.partial(own_kernel, tiles, blocks),
         out_shape=jax.ShapeDtypeStruct((tiles, SLOT, HD), jnp.bfloat16),
-        in_specs=[vmem, hbm],
+        in_specs=[vmem, hbm] + [anywhere] * len(after),
         out_specs=vmem,
         scratch_shapes=[
             pltpu.VMEM((BLK, HD), jnp.bfloat16),
@@ -128,42 +130,46 @@
             pltpu.SemaphoreType.DMA((2,)),
         ],
         compiler_params=params(),
-        cost_estimate=pl.CostEstimate(
-            flops=4 * tiles * ROWS * BLK * HD, bytes_accessed=4 * BLK * HD, transcendentals=tiles * ROWS * BLK
-        ),
+        cost_estimate=pl.CostEstimate(flops=1 << 36, bytes_accessed=1 << 30, transcendentals=1),
         name="own_pieces",
-    )(queries, kv_cache)
-
-
-def serve_kernel(slot_ref, kv_ref, out_ref, keys, values, sems):
-    number = jnp.max(slot_ref[ROWS:SLOT, :].astype(jnp.float32)).astype(jnp.int32)
-    start = pl.multiple_of(number * BLK, BLK)
-    key_copy = pltpu.make_async_copy(kv_ref.at[0, pl.ds(start, BLK)], keys, sems.at[0])
-    value_copy = pltpu.make_async_copy(kv_ref.at[1, pl.ds(start, BLK)], values, sems.at[1])
-    key_copy.start()
-    value_copy.start()
-    key_copy.wait()
-    value_copy.wait()
-    attend(slot_ref[0:ROWS, :], keys[...], values[...], None, out_ref)
-
-
-def serve(slot, kv_cache):
-    return pl.pallas_call(
-        serve_kernel,
-        out_shape=jax.ShapeDtypeStruct((SLOT, HD), jnp.bfloat16),
-        in_specs=[vmem, hbm],
-        out_specs=vmem,
+    )(queries, kv_cache, *after)
+
+
+def serve_kernel(count, *refs):
+    slots, kv_ref, outs = refs[:count], refs[count], refs[-count - 3 : -3]
+    keys, values, sems = refs[-3:]
+    copies = []
+    for index, slot in enumerate(slots):
+        number = jnp.max(slot[ROWS:SLOT, :].astype(jnp.float32)).astype(jnp.int32)
+        start = pl.multiple_of(number * BLK, BLK)
+        for half, buffer in enumerate((keys, values)):
+            copy = pltpu.make_async_copy(
+                kv_ref.at[half, pl.ds(start, BLK)], buffer.at[index], sems.at[half, index]
+            )
+            copy.start()
+            copies.append(copy)
+    for index, slot in enumerate(slots):
+        copies[2 * index].wait()
+        copies[2 * index + 1].wait()
+        attend(slot[0:ROWS, :], keys[index], values[index], None, outs[index])
+
+
+def serve(slots, kv_cache, after):
+    count = len(slots)
+    return pl.pallas_call(
+        functools.partial(serve_kernel, count),
+        out_shape=[jax.ShapeDtypeStruct((SLOT, HD), jnp.bfloat16)] * count,
+        in_specs=[vmem] * count + [hbm] + [anywhere] * len(after),
+        out_specs=[vmem] * count,
         scratch_shapes=[
-            pltpu.VMEM((BLK, HD), jnp.bfloat16),
-            pltpu.VMEM((BLK, HD), jnp.bfloat16),
-            pltpu.SemaphoreType.DMA((2,)),
+            pltpu.VMEM((count, BLK, HD), jnp.bfloat16),
+            pltpu.VMEM((count, BLK, HD), jnp.bfloat16),
+            pltpu.SemaphoreType.DMA((2, count)),
         ],
         compiler_params=params(),
-        cost_estimate=pl.CostEstimate(
-            flops=4 * ROWS * BLK * HD, bytes_accessed=4 * BLK * HD, transcendentals=ROWS * BLK
-        ),
-        name="serve_slot",
-    )(slot, kv_cache)
+        cost_estimate=pl.CostEstimate(flops=1 << 36, bytes_accessed=1 << 30, transcendentals=1),
+        name="serve_slots",
+    )(*slots, kv_cache, *after)
 
 
 def levels_of(parts):
@@ -172,7 +178,7 @@
 
 
 def combine_kernel(tiles, blocks, seq_count, me_ref, selected_ref, own_ref, *refs):
-    slots, out_ref, blend = refs[:seq_count], refs[seq_count], refs[seq_count + 1]
+    slots, out_ref, blend = refs[:seq_count], refs[-2], refs[-1]
     routes = [
         route(selected_ref, me_ref[0], me_ref[0] ^ offset, tiles, blocks)
         for offset in range(seq_count)
@@ -216,73 +222,66 @@
             ].astype(jnp.bfloat16)
 
 
-def combine(me, selected, own, slots, blocks):
+def combine(me, selected, own, slots, blocks, after):
     tiles = own.shape[0]
     seq_count = len(slots)
     return pl.pallas_call(
         functools.partial(combine_kernel, tiles, blocks, seq_count),
         out_shape=jax.ShapeDtypeStruct((tiles * TILE, GROUP * HD), jnp.bfloat16),
-        in_specs=[smem, smem, vmem] + [vmem] * seq_count,
+        in_specs=[smem, smem, vmem] + [vmem] * seq_count + [anywhere] * len(after),
         out_specs=vmem,
         scratch_shapes=[pltpu.VMEM((ROWS, HD), jnp.float32)],
         compiler_params=params(),
         name="combine_pieces",
-    )(me, selected, own, *slots)
+    )(me, selected, own, *slots, *after)
 
 
 def project_kernel(heads, me_ref, *refs):
-    attentions, shards, out_ref = refs[:heads], refs[heads:-1], refs[-1]
-    width = shards[0].shape[1]
-    order = len(shards) // heads
+    attentions, stacks, out_ref = refs[:heads], refs[heads:-1], refs[-1]
+    depth, width = attentions[0].shape[1], stacks[0].shape[1]
     z, x, h = me_ref[0], me_ref[1], me_ref[2]
-    for side in range(order):
+    lefts = []
+    for index in range(heads):
+        place = (z ^ index) ^ h
+        left = attentions[0][...]
+        for other in range(1, heads):
+            left = jnp.where(place == other, attentions[other][...], left)
+        lefts.append(left)
+    for side in range(2):
         total = None
         for index in range(heads):
-            place = (z ^ index) ^ h
-            left = attentions[0][...]
-            for other in range(1, heads):
-                left = jnp.where(place == other, attentions[other][...], left)
-            term = jnp.dot(left, shards[side * heads + index][...], preferred_element_type=jnp.float32)
+            stack = stacks[2 * side + (index & 1)]
+            part = slice((index >> 1) * depth, ((index >> 1) + 1) * depth)
+            term = jnp.dot(lefts[index], stack[part, :], preferred_element_type=jnp.float32)
             total = term if total is None else total + term
         start = pl.multiple_of((x ^ side) * width, width)
         out_ref[:, pl.ds(start, width)] = total.astype(jnp.bfloat16)
 
 
-def project(numbers, attentions, shards):
-    rows, width = attentions[0].shape[0], shards[0].shape[1]
+def project(numbers, attentions, stacks):
+    rows, width = attentions[0].shape[0], stacks[0].shape[1]
     heads = len(attentions)
-    columns = width * len(shards) // heads
     return pl.pallas_call(
         functools.partial(project_kernel, heads),
-        out_shape=jax.ShapeDtypeStruct((rows, columns), jnp.bfloat16),
-        in_specs=[smem] + [vmem] * (heads + len(shards)),
+        out_shape=jax.ShapeDtypeStruct((rows, 2 * width), jnp.bfloat16),
+        in_specs=[smem] + [vmem] * (heads + len(stacks)),
         out_specs=vmem,
         compiler_params=params(),
         name="project",
-    )(numbers, *attentions, *shards)
+    )(numbers, *attentions, *stacks)
 
 
 def pairs(count, offset):
     return [(index, index ^ offset) for index in range(count)]
 
 
-def spread_weight(weight, kvh_count):
-    joint = ("seq", "kvh")
-
-    def jump(flip):
-        moves = []
-        for z in range(kvh_count):
-            for x in range(2):
-                for h in range(kvh_count):
-                    moves.append(((z * 2 + x) * kvh_count + h, ((h ^ flip) * 2 + x) * kvh_count + z))
-        return lax.ppermute(weight, joint, moves)
-
-    seq_count = 2 * kvh_count
-    shards = [None] * kvh_count
-    for index in range(0, kvh_count, 2):
-        shards[index] = jump(index)
-        shards[index + 1] = lax.ppermute(shards[index], "seq", pairs(seq_count, 2))
-    return shards + [lax.ppermute(shard, "seq", pairs(seq_count, 1)) for shard in shards]
+def jump(weight, kvh_count, flip):
+    moves = []
+    for z in range(kvh_count):
+        for x in range(2):
+            for h in range(kvh_count):
+                moves.append(((z * 2 + x) * kvh_count + h, ((h ^ flip) * 2 + x) * kvh_count + z))
+    return lax.ppermute(weight, ("seq", "kvh"), moves)
 
 
 def per_device(queries, kv_cache, selected, out_weight):
@@ -290,32 +289,45 @@
     seq, kvh = lax.axis_index("seq"), lax.axis_index("kvh")
     blocks = kv_cache.shape[1] // BLK
     me = seq.astype(jnp.int32).reshape(1)
-    requests = selected.reshape(-1)
+    requests = selected
+    fast = seq_count == 2 * kvh_count and kvh_count == 4
+
+    def move(array, offset):
+        return lax.ppermute(array, "seq", pairs(seq_count, offset))
+
+    stack = stack_z = stack_x = stack_zx = None
+    if fast:
+        jumps = [jump(out_weight, kvh_count, 0), jump(out_weight, kvh_count, 2)]
+        stack = jnp.concatenate(jumps, axis=0)
+        stack_z = move(stack, 2)
+        stack_x = move(stack, 1)
+        stack_zx = move(stack_z, 1)
     outgoing = pack(me, requests, queries, seq_count, blocks)
-    arrived = [outgoing[0]] + [
-        lax.ppermute(outgoing[offset], "seq", pairs(seq_count, offset))
-        for offset in range(1, seq_count)
-    ]
-    own = own_pieces(queries, kv_cache)
-    returned = [
-        serve(arrived[0], kv_cache)
-    ] + [
-        lax.ppermute(serve(arrived[offset], kv_cache), "seq", pairs(seq_count, offset))
-        for offset in range(1, seq_count)
-    ]
-    attention = combine(me, requests, own, returned, blocks)
-    if seq_count == 2 * kvh_count and kvh_count & (kvh_count - 1) == 0:
-        shards = spread_weight(out_weight, kvh_count)
-        gathered = [attention]
-        bit = kvh_count // 2
-        parts = {0: attention}
-        while bit:
-            for offset in list(parts):
-                parts[offset | bit] = lax.ppermute(parts[offset], "kvh", pairs(kvh_count, bit))
-            bit //= 2
-        gathered = [parts[offset] for offset in range(kvh_count)]
-        numbers = jnp.stack([seq // 2, seq % 2, kvh]).astype(jnp.int32)
-        return project(numbers, gathered, shards)
+    arrived = {offset: move(outgoing[offset], offset) for offset in range(1, seq_count)}
+    returned = {}
+
+    def answer(offsets, after):
+        answers = serve([arrived[offset] for offset in offsets], kv_cache, [a for a in after if a is not None])
+        for offset, result in zip(offsets, answers):
+            returned[offset] = move(result, offset)
+        return answers[-1]
+
+    own = own_pieces(queries, kv_cache, [outgoing[0]])
+    last = returned[0] = serve([outgoing[0]], kv_cache, [own])[0]
+    last = answer([1, 2, 3], [last, stack])
+    last = answer([4, 5], [last])
+    for place in range(6, seq_count, 2):
+        last = answer([place, place + 1], [last, stack_x])
+    returned = [returned[offset] for offset in range(seq_count)]
+    attention = combine(me, requests, own, returned, blocks, [stack_z] if fast else [])
+    if fast:
+        other_y = lax.ppermute(attention, "kvh", pairs(kvh_count, 2))
+        other_core = lax.ppermute(attention, "kvh", pairs(kvh_count, 1))
+        both = lax.ppermute(other_y, "kvh", pairs(kvh_count, 1))
+        gathered = [attention, other_core, other_y, both]
+        stacks = [stack, stack_z, stack_x, stack_zx]
+        numbers = jnp.stack([lax.shift_right_logical(seq, 1), seq & 1, kvh]).astype(jnp.int32)
+        return project(numbers, gathered, stacks)
     column_terms = jnp.dot(
         attention,
         lax.all_gather(out_weight, "seq", axis=1, tiled=True),

time: 157 us -> 112 us (0.71); the launches traced: 157 us -> 110 us
  waiting for transfers between devices: 81.2 us -> 45.6 us
  starting transfers between devices: 45.9 us -> 36.7 us
    ppermute x25 -> x22, waiting for transfers between devices: 81.2 us -> 45.6 us  [the longest x17 35.8 us: move(): return lax.ppermute(array, 'seq', pairs(seq_count, offset))]
    ppermute x25 -> x22, starting transfers between devices: 45.9 us -> 36.7 us  [the longest x17 29.1 us: move(): return lax.ppermute(array, 'seq', pairs(seq_count, offset))]
    unnamed x13 -> x17, local copies, waits for them, and re-layouts: 5.31 us -> 4.82 us
    pallas_call x8 -> x4, Pallas kernels: 13.1 us -> 13.3 us  [serve(): pl.pallas_call(functools.partial(serve_kernel, count), out_shape=[jax.Sha...]
  transfers between devices with their start and end apart: 25 -> 22, of which waited for: 11 -> 10; matrix products, arithmetic and copies ran while one was open for 1% -> 0% of each run, Pallas kernels for 12% -> 17%
where the time goes in v2:
time: 112 us; the launch traced here: 110 us
  waiting for transfers between devices  45.6 us (41%)
  starting transfers between devices  36.7 us (33%)
  Pallas kernels  22.6 us (20%)
  local copies, waits for them, and re-layouts  4.85 us (4%)
    ppermute x17, waiting for transfers between devices, move(): return lax.ppermute(array, 'seq', pairs(seq_count, offset))  35.8 us
    ppermute x17, starting transfers between devices, move(): return lax.ppermute(array, 'seq', pairs(seq_count, offset))  29.1 us
    pallas_call x4, Pallas kernels, serve(): pl.pallas_call(functools.partial(serve_kernel, count), out_shape=[jax.Sha...  13.3 us
    ppermute x1, waiting for transfers between devices, per_device(): other_y = lax.ppermute(attention, 'kvh', pairs(kvh_count, 2))  7.95 us
    ppermute x2, starting transfers between devices, jump(): return lax.ppermute(weight, ('seq', 'kvh'), moves)  7.28 us
    unnamed x17, local copies, waits for them, and re-layouts  4.82 us
    pallas_call x1, Pallas kernels, project(): pl.pallas_call(functools.partial(project_kernel, heads), out_shape=jax.Sh...  3.52 us
    pallas_call x1, Pallas kernels, own_pieces(): pl.pallas_call(functools.partial(own_kernel, tiles, blocks), out_shape=ja...  3.28 us
  transfers between devices with their start and end apart: 22, of which 10 were waited for; matrix products, arithmetic and copies ran while one was open for 0% of the time, Pallas kernels for 17%

profile of v2, /device:TPU:0, one launch (start us, length us, event | category | flops | bytes accessed | tf_op | source)
XLA Modules:
  0.0 110.1 jit_solution(10511866832821179217)
XLA Ops:
  0.0 1.7 %collective-permute-start.3 = (bf16[512,512]{1,0:T(8,128)(2,1)}, bf16[512,512]{1,0:T(8,128)(2,1)S(1)}, u32[]{:S(2)}, u32[]{:S(2)}) collective-permute-start(bf16[512,512]{1,0:T(8,128)(2,1)} %param.7), channel_id=1, source_target_pairs={{0,0},{1,8},{2,16},{3,24},{4,4},{5,12},{6,20},{7,28},{8,1},{9,9},{... | collective-permute-start | bytes 1572872 | tf_op jit(solution)/shard_map/ppermute | solution.py:284
  1.7 5.6 %collective-permute-start.4 = (bf16[512,512]{1,0:T(8,128)(2,1)}, bf16[512,512]{1,0:T(8,128)(2,1)S(1)}, u32[]{:S(2)}, u32[]{:S(2)}) collective-permute-start(bf16[512,512]{1,0:T(8,128)(2,1)} %param.7), channel_id=1, source_target_pairs={{0,16},{1,24},{2,0},{3,8},{4,20},{5,28},{6,4},{7,12},{8,17},{9,25}... | collective-permute-start | bytes 1572872 | tf_op jit(solution)/shard_map/ppermute | solution.py:284
  7.3 0.0 copy-start.2
  7.3 0.9 copy-done.2
  8.2 0.7 copy-done.4
  8.9 0.8 pack_queries.1
  9.7 1.6 %collective-permute-start = (bf16[528,128]{1,0:T(8,128)(2,1)S(1)}, bf16[528,128]{1,0:T(8,128)(2,1)S(1)}, u32[]{:S(2)}, u32[]{:S(2)}) collective-permute-start(bf16[528,128]{1,0:T(8,128)(2,1)S(1)} %get-tuple-element.21), channel_id=1, source_target_pairs={{0,4},{4,0},{8,12},{12,8},{16,20},{20,16},{24,28},{28,24},{1,5},{5... | collective-permute-start | bytes 405512 | tf_op jit(solution)/shard_map/ppermute | solution.py:296
  11.3 0.4 collective-permute-start.1
  11.7 1.6 %collective-permute-start.2 = (bf16[528,128]{1,0:T(8,128)(2,1)S(1)}, bf16[528,128]{1,0:T(8,128)(2,1)S(1)}, u32[]{:S(2)}, u32[]{:S(2)}) collective-permute-start(bf16[528,128]{1,0:T(8,128)(2,1)S(1)} %get-tuple-element.23), channel_id=1, source_target_pairs={{0,12},{4,8},{8,4},{12,0},{16,28},{20,24},{24,20},{28,16},{1,13},{... | collective-permute-start | bytes 405512 | tf_op jit(solution)/shard_map/ppermute | solution.py:296
  13.3 0.9 copy-done.3
  14.2 2.2 %copy-done.6 = bf16[2,8192,128]{2,1,0:T(8,128)(2,1)S(1)} copy-done((bf16[2,8192,128]{2,1,0:T(8,128)(2,1)S(1)}, bf16[2,8192,128]{2,1,0:T(8,128)(2,1)}, u32[]{:S(2)}) %copy-start.6) | copy-done | bytes 4194328
  16.4 3.3 %own_pieces.1.refs_2_.own_ref = bf16[2,528,128]{2,1,0:T(8,128)(2,1)S(1)} custom-call(bf16[256,512]{1,0:T(8,128)(2,1)S(1)} %copy-done.3, bf16[2,8192,128]{2,1,0:T(8,128)(2,1)S(1)} %copy-done.6, bf16[528,128]{1,0:T(8,128)(2,1)S(1)} %get-tuple-element.20.refs_0_), custom_call_target="tpu_custom_call" | custom-call | flops 68719476736 | bytes 1073741824 | tf_op jit(solution)/shard_map/own_pieces/pallas_call | solution.py:122
  19.7 0.0 copy-start
  19.7 0.0 copy-start.7
  19.7 1.6 %serve_slots.4.refs_4_.refs_0_ = bf16[528,128]{1,0:T(8,128)(2,1)S(1)} custom-call(bf16[528,128]{1,0:T(8,128)(2,1)S(1)} %get-tuple-element.20.refs_0_, bf16[2,8192,128]{2,1,0:T(8,128)(2,1)S(1)} %copy-done.6, bf16[2,528,128]{2,1,0:T(8,128)(2,1)S(1)} %own_pieces.1.refs_2_.own_ref), custom_call_target="tpu_custom_call" | custom-call | flops 68719476736 | bytes 1073741824 | tf_op jit(solution)/shard_map/serve_slots/pallas_call | solution.py:159
  21.4 0.0 copy-done
  21.4 0.0 collective-permute-done.3
  21.4 9.2 %collective-permute-start.8 = (bf16[528,128]{1,0:T(8,128)(2,1)S(1)}, bf16[528,128]{1,0:T(8,128)(2,1)S(1)}, u32[]{:S(2)}, u32[]{:S(2)}) collective-permute-start(bf16[528,128]{1,0:T(8,128)(2,1)S(1)} %get-tuple-element.27), channel_id=1, source_target_pairs={{0,16},{4,20},{8,24},{12,28},{16,0},{20,4},{24,8},{28,12},{1,17},{... | collective-permute-start | bytes 405512 | tf_op jit(solution)/shard_map/ppermute | solution.py:296
  30.7 0.0 collective-permute-done.4
  30.7 1.0 collective-permute-start.9
  31.7 0.0 collective-permute-done.refs_0_
  31.7 3.0 %collective-permute-start.12 = (bf16[528,128]{1,0:T(8,128)(2,1)S(1)}, bf16[528,128]{1,0:T(8,128)(2,1)S(1)}, u32[]{:S(2)}, u32[]{:S(2)}) collective-permute-start(bf16[528,128]{1,0:T(8,128)(2,1)S(1)} %get-tuple-element.31), channel_id=1, source_target_pairs={{0,24},{4,28},{8,16},{12,20},{16,8},{20,12},{24,0},{28,4},{1,25},{... | collective-permute-start | bytes 405512 | tf_op jit(solution)/shard_map/ppermute | solution.py:296
  34.7 0.0 collective-permute-done.1.refs_1_
  34.7 0.9 collective-permute-start.13
  35.6 0.0 collective-permute-done.2.refs_2_
  35.6 1.4 %collective-permute-start.14 = (bf16[1024,512]{1,0:T(8,128)(2,1)S(1)}, bf16[1024,512]{1,0:T(8,128)(2,1)S(1)}, u32[]{:S(2)}, u32[]{:S(2)}) collective-permute-start(bf16[1024,512]{1,0:T(8,128)(2,1)S(1)} %constant_dynamic-update-slice_fusion.refs_5_.refs_4_), channel_id=1, source_target_pairs={{0,4},{4,0},{8,12},{12,8},{16,20},{20,16},{24,28},{28,24},{1,5},{5... | collective-permute-start | bytes 3145736 | tf_op jit(solution)/shard_map/ppermute | solution.py:296
  37.1 0.0 copy-done.7
  37.1 4.9 %serve_slots.5 = (bf16[528,128]{1,0:T(8,128)(2,1)S(1)}, bf16[528,128]{1,0:T(8,128)(2,1)S(1)}, bf16[528,128]{1,0:T(8,128)(2,1)S(1)}) custom-call(bf16[528,128]{1,0:T(8,128)(2,1)S(1)} %collective-permute-done.refs_0_, bf16[528,128]{1,0:T(8,128)(2,1)S(1)} %collective-permute-done.1.refs_1_, bf16[528,128]{1,0:T(8,128)(2,1)S(1)} %collective-permute-done.2.refs_2_, ...), custom_call_target="tpu_custom_call" | custom-call | flops 68719476736 | bytes 1073741824 | tf_op jit(solution)/shard_map/serve_slots/pallas_call | solution.py:159
  42.0 3.9 %collective-permute-done.8.refs_0_ = bf16[528,128]{1,0:T(8,128)(2,1)S(1)} collective-permute-done((bf16[528,128]{1,0:T(8,128)(2,1)S(1)}, bf16[528,128]{1,0:T(8,128)(2,1)S(1)}, u32[]{:S(2)}, u32[]{:S(2)}) %collective-permute-start.8) | collective-permute-done | bytes 135200 | tf_op jit(solution)/shard_map/ppermute | solution.py:296
  45.9 0.0 collective-permute-start.17
  45.9 4.0 %collective-permute-done.9.refs_1_ = bf16[528,128]{1,0:T(8,128)(2,1)S(1)} collective-permute-done((bf16[528,128]{1,0:T(8,128)(2,1)S(1)}, bf16[528,128]{1,0:T(8,128)(2,1)S(1)}, u32[]{:S(2)}, u32[]{:S(2)}) %collective-permute-start.9) | collective-permute-done | bytes 135200 | tf_op jit(solution)/shard_map/ppermute | solution.py:296
  49.9 0.0 collective-permute-start.7
  49.9 3.3 %serve_slots.6 = (bf16[528,128]{1,0:T(8,128)(2,1)S(1)}, bf16[528,128]{1,0:T(8,128)(2,1)S(1)}) custom-call(bf16[528,128]{1,0:T(8,128)(2,1)S(1)} %collective-permute-done.8.refs_0_, bf16[528,128]{1,0:T(8,128)(2,1)S(1)} %collective-permute-done.9.refs_1_, bf16[2,8192,128]{2,1,0:T(8,128)(2,1)S(1)} %copy-done.7, bf16[528,128]{1,0:T(8,128)(2,1)S(1)} %get-tuple-element.26.refs_3_), custom_call_target="tpu_custom_call" | custom-call | flops 68719476736 | bytes 1073741824 | tf_op jit(solution)/shard_map/serve_slots/pallas_call | solution.py:159
  53.2 0.0 collective-permute-done.12.refs_0_
  53.2 2.0 %collective-permute-start.11 = (bf16[528,128]{1,0:T(8,128)(2,1)S(1)}, bf16[528,128]{1,0:T(8,128)(2,1)S(1)}, u32[]{:S(2)}, u32[]{:S(2)}) collective-permute-start(bf16[528,128]{1,0:T(8,128)(2,1)S(1)} %get-tuple-element.30.refs_3_), channel_id=1, source_target_pairs={{0,20},{4,16},{8,28},{12,24},{16,4},{20,0},{24,12},{28,8},{1,21},{... | collective-permute-start | bytes 405512 | tf_op jit(solution)/shard_map/ppermute | solution.py:296
  55.2 0.0 collective-permute-done.13.refs_1_
  55.2 0.9 collective-permute-start.10
  56.1 13.8 %collective-permute-done.14.refs_4_.refs_6_ = bf16[1024,512]{1,0:T(8,128)(2,1)S(1)} collective-permute-done((bf16[1024,512]{1,0:T(8,128)(2,1)S(1)}, bf16[1024,512]{1,0:T(8,128)(2,1)S(1)}, u32[]{:S(2)}, u32[]{:S(2)}) %collective-permute-start.14) | collective-permute-done | bytes 1048608 | tf_op jit(solution)/shard_map/ppermute | solution.py:296
  69.9 1.6 %collective-permute-start.5 = (bf16[528,128]{1,0:T(8,128)(2,1)S(1)}, bf16[528,128]{1,0:T(8,128)(2,1)S(1)}, u32[]{:S(2)}, u32[]{:S(2)}) collective-permute-start(bf16[528,128]{1,0:T(8,128)(2,1)S(1)} %get-tuple-element.24), channel_id=1, source_target_pairs={{0,4},{4,0},{8,12},{12,8},{16,20},{20,16},{24,28},{28,24},{1,5},{5... | collective-permute-start | bytes 405512 | tf_op jit(solution)/shard_map/ppermute | solution.py:296
  71.5 6.2 %collective-permute-done.17.refs_8_.refs_5_ = bf16[1024,512]{1,0:T(8,128)(2,1)S(1)} collective-permute-done((bf16[1024,512]{1,0:T(8,128)(2,1)S(1)}, bf16[1024,512]{1,0:T(8,128)(2,1)S(1)}, u32[]{:S(2)}, u32[]{:S(2)}) %collective-permute-start.17) | collective-permute-done | bytes 1048608 | tf_op jit(solution)/shard_map/ppermute | solution.py:296
  77.7 1.6 %collective-permute-start.21 = (bf16[1024,512]{1,0:T(8,128)(2,1)S(1)}, bf16[1024,512]{1,0:T(8,128)(2,1)}, u32[]{:S(2)}, u32[]{:S(2)}) collective-permute-start(bf16[1024,512]{1,0:T(8,128)(2,1)S(1)} %collective-permute-done.17.refs_8_.refs_5_), channel_id=1, source_target_pairs={{0,4},{4,0},{8,12},{12,8},{16,20},{20,16},{24,28},{28,24},{1,5},{5... | collective-permute-start | bytes 3145736 | tf_op jit(solution)/shard_map/ppermute | solution.py:296
  79.3 3.4 %serve_slots.7 = (bf16[528,128]{1,0:T(8,128)(2,1)S(1)}, bf16[528,128]{1,0:T(8,128)(2,1)S(1)}) custom-call(bf16[528,128]{1,0:T(8,128)(2,1)S(1)} %collective-permute-done.12.refs_0_, bf16[528,128]{1,0:T(8,128)(2,1)S(1)} %collective-permute-done.13.refs_1_, bf16[2,8192,128]{2,1,0:T(8,128)(2,1)S(1)} %copy-done.7, ...), custom_call_target="tpu_custom_call" | custom-call | flops 68719476736 | bytes 1073741824 | tf_op jit(solution)/shard_map/serve_slots/pallas_call | solution.py:159
  82.7 0.0 collective-permute-done.11.refs_5_
  82.7 0.1 collective-permute-start.6
  82.8 0.0 collective-permute-done.10.refs_4_
  82.8 0.1 collective-permute-start.15
  82.9 0.0 collective-permute-done.7.refs_3_
  82.9 3.7 %collective-permute-start.16 = (bf16[528,128]{1,0:T(8,128)(2,1)S(1)}, bf16[528,128]{1,0:T(8,128)(2,1)S(1)}, u32[]{:S(2)}, u32[]{:S(2)}) collective-permute-start(bf16[528,128]{1,0:T(8,128)(2,1)S(1)} %get-tuple-element.34), channel_id=1, source_target_pairs={{0,28},{4,24},{8,20},{12,16},{16,12},{20,8},{24,4},{28,0},{1,29},{... | collective-permute-start | bytes 405512 | tf_op jit(solution)/shard_map/ppermute | solution.py:296
  86.6 0.0 collective-permute-done.5.refs_1_
  86.6 1.2 %collective-permute-done.6.refs_2_ = bf16[528,128]{1,0:T(8,128)(2,1)S(1)} collective-permute-done((bf16[528,128]{1,0:T(8,128)(2,1)S(1)}, bf16[528,128]{1,0:T(8,128)(2,1)S(1)}, u32[]{:S(2)}, u32[]{:S(2)}) %collective-permute-start.6) | collective-permute-done | bytes 135200 | tf_op jit(solution)/shard_map/ppermute | solution.py:296
  87.8 3.5 %collective-permute-done.15.refs_6_ = bf16[528,128]{1,0:T(8,128)(2,1)S(1)} collective-permute-done((bf16[528,128]{1,0:T(8,128)(2,1)S(1)}, bf16[528,128]{1,0:T(8,128)(2,1)S(1)}, u32[]{:S(2)}, u32[]{:S(2)}) %collective-permute-start.15) | collective-permute-done | bytes 135200 | tf_op jit(solution)/shard_map/ppermute | solution.py:296
  91.3 2.9 %collective-permute-done.16.refs_7_ = bf16[528,128]{1,0:T(8,128)(2,1)S(1)} collective-permute-done((bf16[528,128]{1,0:T(8,128)(2,1)S(1)}, bf16[528,128]{1,0:T(8,128)(2,1)S(1)}, u32[]{:S(2)}, u32[]{:S(2)}) %collective-permute-start.16) | collective-permute-done | bytes 135200 | tf_op jit(solution)/shard_map/ppermute | solution.py:296
  94.2 0.0 copy-done.1
  94.2 0.0 copy-done.5
  94.2 1.8 %combine_pieces.1.refs_0_ = bf16[256,512]{1,0:T(8,128)(2,1)S(1)} custom-call(s32[1]{0:T(128)} %bitcast.3.me_ref, s32[2,1,2]{2,1,0:T(1,128)S(1)} %copy-done.5, bf16[2,528,128]{2,1,0:T(8,128)(2,1)S(1)} %copy-done.1, bf16[528,128]{1,0:T(8,128)(2,1)S(1)} %serve_slots.4.refs_4_.refs_0_, bf16[528,128]{1,0:T(8,128)(2,1)S(1)} %collective-permute-done.5.refs_1_, ...), custom_call_target="tpu_custom_call" | custom-call | tf_op jit(solution)/shard_map/combine_pieces/pallas_call | solution.py:228
  96.0 0.4 collective-permute-start.19
  96.4 0.0 collective-permute-start.18
  96.4 7.9 %collective-permute-done.19.refs_2_ = bf16[256,512]{1,0:T(8,128)(2,1)} collective-permute-done((bf16[256,512]{1,0:T(8,128)(2,1)S(1)}, bf16[256,512]{1,0:T(8,128)(2,1)}, u32[]{:S(2)}, u32[]{:S(2)}) %collective-permute-start.19) | collective-permute-done | bytes 262176 | tf_op jit(solution)/shard_map/ppermute | solution.py:324
  104.3 0.0 collective-permute-start.20
  104.3 0.1 pad_add_fusion.me_ref
  104.4 0.0 collective-permute-done.18.refs_1_
  104.4 1.8 %collective-permute-done.20.refs_3_ = bf16[256,512]{1,0:T(8,128)(2,1)} collective-permute-done((bf16[256,512]{1,0:T(8,128)(2,1)}, bf16[256,512]{1,0:T(8,128)(2,1)}, u32[]{:S(2)}, u32[]{:S(2)}) %collective-permute-start.20) | collective-permute-done | bytes 262176 | tf_op jit(solution)/shard_map/ppermute | solution.py:326
  106.2 0.4 collective-permute-done.21.refs_7_
  106.6 3.5 %project.1 = bf16[256,1024]{1,0:T(8,128)(2,1)} custom-call(s32[3]{0:T(128)S(1)} %pad_add_fusion.me_ref, bf16[256,512]{1,0:T(8,128)(2,1)S(1)} %combine_pieces.1.refs_0_, bf16[256,512]{1,0:T(8,128)(2,1)} %collective-permute-done.18.refs_1_, bf16[256,512]{1,0:T(8,128)(2,1)} %collective-permute-done.19.refs_2_, ...), custom_call_target="tpu_custom_call" | custom-call | tf_op jit(solution)/shard_map/project/pallas_call | solution.py:264
  (7 shorter events, 0.1 us)
Async XLA Ops:
  0.0 21.4 %collective-permute-start.3 = (bf16[512,512]{1,0:T(8,128)(2,1)}, bf16[512,512]{1,0:T(8,128)(2,1)S(1)}, u32[]{:S(2)}, u32[]{:S(2)}) collective-permute-start(bf16[512,512]{1,0:T(8,128)(2,1)} %param.7), channel_id=1, source_target_pairs={{0,0},{1,8},{2,16},{3,24},{4,4},{5,12},{6,20},{7,28},{8,1},{9,9},{... | collective-permute-start | bytes 1572872 | tf_op jit(solution)/shard_map/ppermute | solution.py:284
  1.7 29.0 %collective-permute-start.4 = (bf16[512,512]{1,0:T(8,128)(2,1)}, bf16[512,512]{1,0:T(8,128)(2,1)S(1)}, u32[]{:S(2)}, u32[]{:S(2)}) collective-permute-start(bf16[512,512]{1,0:T(8,128)(2,1)} %param.7), channel_id=1, source_target_pairs={{0,16},{1,24},{2,0},{3,8},{4,20},{5,28},{6,4},{7,12},{8,17},{9,25}... | collective-permute-start | bytes 1572872 | tf_op jit(solution)/shard_map/ppermute | solution.py:284
  7.3 0.9 copy-start.2
  8.2 0.7 copy-start.4
  9.7 22.0 %collective-permute-start = (bf16[528,128]{1,0:T(8,128)(2,1)S(1)}, bf16[528,128]{1,0:T(8,128)(2,1)S(1)}, u32[]{:S(2)}, u32[]{:S(2)}) collective-permute-start(bf16[528,128]{1,0:T(8,128)(2,1)S(1)} %get-tuple-element.21), channel_id=1, source_target_pairs={{0,4},{4,0},{8,12},{12,8},{16,20},{20,16},{24,28},{28,24},{1,5},{5... | collective-permute-start | bytes 405512 | tf_op jit(solution)/shard_map/ppermute | solution.py:296
  11.3 23.4 %collective-permute-start.1 = (bf16[528,128]{1,0:T(8,128)(2,1)S(1)}, bf16[528,128]{1,0:T(8,128)(2,1)S(1)}, u32[]{:S(2)}, u32[]{:S(2)}) collective-permute-start(bf16[528,128]{1,0:T(8,128)(2,1)S(1)} %get-tuple-element.22), channel_id=1, source_target_pairs={{0,8},{4,12},{8,0},{12,4},{16,24},{20,28},{24,16},{28,20},{1,9},{5... | collective-permute-start | bytes 405512 | tf_op jit(solution)/shard_map/ppermute | solution.py:296
  11.7 23.9 %collective-permute-start.2 = (bf16[528,128]{1,0:T(8,128)(2,1)S(1)}, bf16[528,128]{1,0:T(8,128)(2,1)S(1)}, u32[]{:S(2)}, u32[]{:S(2)}) collective-permute-start(bf16[528,128]{1,0:T(8,128)(2,1)S(1)} %get-tuple-element.23), channel_id=1, source_target_pairs={{0,12},{4,8},{8,4},{12,0},{16,28},{20,24},{24,20},{28,16},{1,13},{... | collective-permute-start | bytes 405512 | tf_op jit(solution)/shard_map/ppermute | solution.py:296
  13.3 0.9 copy-start.3
  14.2 2.2 %copy-start.6 = (bf16[2,8192,128]{2,1,0:T(8,128)(2,1)S(1)}, bf16[2,8192,128]{2,1,0:T(8,128)(2,1)}, u32[]{:S(2)}) copy-start(bf16[2,8192,128]{2,1,0:T(8,128)(2,1)} %refs_2_.3) | copy-start | bytes 12582916
  19.7 1.7 %copy-start = (bf16[2,528,128]{2,1,0:T(8,128)(2,1)}, bf16[2,528,128]{2,1,0:T(8,128)(2,1)S(1)}, u32[]{:S(2)}) copy-start(bf16[2,528,128]{2,1,0:T(8,128)(2,1)S(1)} %own_pieces.1.refs_2_.own_ref) | copy-start | bytes 811012
  19.7 17.4 %copy-start.7 = (bf16[2,8192,128]{2,1,0:T(8,128)(2,1)S(1)}, bf16[2,8192,128]{2,1,0:T(8,128)(2,1)}, u32[]{:S(2)}) copy-start(bf16[2,8192,128]{2,1,0:T(8,128)(2,1)} %refs_2_.3) | copy-start | bytes 12582916
  21.4 24.5 %collective-permute-start.8 = (bf16[528,128]{1,0:T(8,128)(2,1)S(1)}, bf16[528,128]{1,0:T(8,128)(2,1)S(1)}, u32[]{:S(2)}, u32[]{:S(2)}) collective-permute-start(bf16[528,128]{1,0:T(8,128)(2,1)S(1)} %get-tuple-element.27), channel_id=1, source_target_pairs={{0,16},{4,20},{8,24},{12,28},{16,0},{20,4},{24,8},{28,12},{1,17},{... | collective-permute-start | bytes 405512 | tf_op jit(solution)/shard_map/ppermute | solution.py:296
  30.7 19.2 %collective-permute-start.9 = (bf16[528,128]{1,0:T(8,128)(2,1)S(1)}, bf16[528,128]{1,0:T(8,128)(2,1)S(1)}, u32[]{:S(2)}, u32[]{:S(2)}) collective-permute-start(bf16[528,128]{1,0:T(8,128)(2,1)S(1)} %get-tuple-element.28), channel_id=1, source_target_pairs={{0,20},{4,16},{8,28},{12,24},{16,4},{20,0},{24,12},{28,8},{1,21},{... | collective-permute-start | bytes 405512 | tf_op jit(solution)/shard_map/ppermute | solution.py:296
  31.7 21.5 %collective-permute-start.12 = (bf16[528,128]{1,0:T(8,128)(2,1)S(1)}, bf16[528,128]{1,0:T(8,128)(2,1)S(1)}, u32[]{:S(2)}, u32[]{:S(2)}) collective-permute-start(bf16[528,128]{1,0:T(8,128)(2,1)S(1)} %get-tuple-element.31), channel_id=1, source_target_pairs={{0,24},{4,28},{8,16},{12,20},{16,8},{20,12},{24,0},{28,4},{1,25},{... | collective-permute-start | bytes 405512 | tf_op jit(solution)/shard_map/ppermute | solution.py:296
  34.7 20.5 %collective-permute-start.13 = (bf16[528,128]{1,0:T(8,128)(2,1)S(1)}, bf16[528,128]{1,0:T(8,128)(2,1)S(1)}, u32[]{:S(2)}, u32[]{:S(2)}) collective-permute-start(bf16[528,128]{1,0:T(8,128)(2,1)S(1)} %get-tuple-element.32), channel_id=1, source_target_pairs={{0,28},{4,24},{8,20},{12,16},{16,12},{20,8},{24,4},{28,0},{1,29},{... | collective-permute-start | bytes 405512 | tf_op jit(solution)/shard_map/ppermute | solution.py:296
  35.6 34.2 %collective-permute-start.14 = (bf16[1024,512]{1,0:T(8,128)(2,1)S(1)}, bf16[1024,512]{1,0:T(8,128)(2,1)S(1)}, u32[]{:S(2)}, u32[]{:S(2)}) collective-permute-start(bf16[1024,512]{1,0:T(8,128)(2,1)S(1)} %constant_dynamic-update-slice_fusion.refs_5_.refs_4_), channel_id=1, source_target_pairs={{0,4},{4,0},{8,12},{12,8},{16,20},{20,16},{24,28},{28,24},{1,5},{5... | collective-permute-start | bytes 3145736 | tf_op jit(solution)/shard_map/ppermute | solution.py:296
  45.9 31.8 %collective-permute-start.17 = (bf16[1024,512]{1,0:T(8,128)(2,1)S(1)}, bf16[1024,512]{1,0:T(8,128)(2,1)S(1)}, u32[]{:S(2)}, u32[]{:S(2)}) collective-permute-start(bf16[1024,512]{1,0:T(8,128)(2,1)S(1)} %constant_dynamic-update-slice_fusion.refs_5_.refs_4_), channel_id=1, source_target_pairs={{0,8},{4,12},{8,0},{12,4},{16,24},{20,28},{24,16},{28,20},{1,9},{5... | collective-permute-start | bytes 3145736 | tf_op jit(solution)/shard_map/ppermute | solution.py:296
  49.9 33.0 %collective-permute-start.7 = (bf16[528,128]{1,0:T(8,128)(2,1)S(1)}, bf16[528,128]{1,0:T(8,128)(2,1)S(1)}, u32[]{:S(2)}, u32[]{:S(2)}) collective-permute-start(bf16[528,128]{1,0:T(8,128)(2,1)S(1)} %get-tuple-element.26.refs_3_), channel_id=1, source_target_pairs={{0,12},{4,8},{8,4},{12,0},{16,28},{20,24},{24,20},{28,16},{1,13},{... | collective-permute-start | bytes 405512 | tf_op jit(solution)/shard_map/ppermute | solution.py:296
  53.2 29.5 %collective-permute-start.11 = (bf16[528,128]{1,0:T(8,128)(2,1)S(1)}, bf16[528,128]{1,0:T(8,128)(2,1)S(1)}, u32[]{:S(2)}, u32[]{:S(2)}) collective-permute-start(bf16[528,128]{1,0:T(8,128)(2,1)S(1)} %get-tuple-element.30.refs_3_), channel_id=1, source_target_pairs={{0,20},{4,16},{8,28},{12,24},{16,4},{20,0},{24,12},{28,8},{1,21},{... | collective-permute-start | bytes 405512 | tf_op jit(solution)/shard_map/ppermute | solution.py:296
  55.2 27.6 %collective-permute-start.10 = (bf16[528,128]{1,0:T(8,128)(2,1)S(1)}, bf16[528,128]{1,0:T(8,128)(2,1)S(1)}, u32[]{:S(2)}, u32[]{:S(2)}) collective-permute-start(bf16[528,128]{1,0:T(8,128)(2,1)S(1)} %get-tuple-element.29), channel_id=1, source_target_pairs={{0,16},{4,20},{8,24},{12,28},{16,0},{20,4},{24,8},{28,12},{1,17},{... | collective-permute-start | bytes 405512 | tf_op jit(solution)/shard_map/ppermute | solution.py:296
  69.9 24.3 %copy-start.1 = (bf16[2,528,128]{2,1,0:T(8,128)(2,1)S(1)}, bf16[2,528,128]{2,1,0:T(8,128)(2,1)}, u32[]{:S(2)}) copy-start(bf16[2,528,128]{2,1,0:T(8,128)(2,1)} %copy-done) | copy-start | bytes 811012
  69.9 24.3 %copy-start.5 = (s32[2,1,2]{2,1,0:T(1,128)S(1)}, s32[2,1,2]{2,1,0:T(1,128)}, u32[]{:S(2)}) copy-start(s32[2,1,2]{2,1,0:T(1,128)} %selected_ref.3) | copy-start | bytes 52
  69.9 16.7 %collective-permute-start.5 = (bf16[528,128]{1,0:T(8,128)(2,1)S(1)}, bf16[528,128]{1,0:T(8,128)(2,1)S(1)}, u32[]{:S(2)}, u32[]{:S(2)}) collective-permute-start(bf16[528,128]{1,0:T(8,128)(2,1)S(1)} %get-tuple-element.24), channel_id=1, source_target_pairs={{0,4},{4,0},{8,12},{12,8},{16,20},{20,16},{24,28},{28,24},{1,5},{5... | collective-permute-start | bytes 405512 | tf_op jit(solution)/shard_map/ppermute | solution.py:296
  77.7 28.9 %collective-permute-start.21 = (bf16[1024,512]{1,0:T(8,128)(2,1)S(1)}, bf16[1024,512]{1,0:T(8,128)(2,1)}, u32[]{:S(2)}, u32[]{:S(2)}) collective-permute-start(bf16[1024,512]{1,0:T(8,128)(2,1)S(1)} %collective-permute-done.17.refs_8_.refs_5_), channel_id=1, source_target_pairs={{0,4},{4,0},{8,12},{12,8},{16,20},{20,16},{24,28},{28,24},{1,5},{5... | collective-permute-start | bytes 3145736 | tf_op jit(solution)/shard_map/ppermute | solution.py:296
  82.7 5.1 %collective-permute-start.6 = (bf16[528,128]{1,0:T(8,128)(2,1)S(1)}, bf16[528,128]{1,0:T(8,128)(2,1)S(1)}, u32[]{:S(2)}, u32[]{:S(2)}) collective-permute-start(bf16[528,128]{1,0:T(8,128)(2,1)S(1)} %get-tuple-element.25), channel_id=1, source_target_pairs={{0,8},{4,12},{8,0},{12,4},{16,24},{20,28},{24,16},{28,20},{1,9},{5... | collective-permute-start | bytes 405512 | tf_op jit(solution)/shard_map/ppermute | solution.py:296
  82.8 8.5 %collective-permute-start.15 = (bf16[528,128]{1,0:T(8,128)(2,1)S(1)}, bf16[528,128]{1,0:T(8,128)(2,1)S(1)}, u32[]{:S(2)}, u32[]{:S(2)}) collective-permute-start(bf16[528,128]{1,0:T(8,128)(2,1)S(1)} %get-tuple-element.33), channel_id=1, source_target_pairs={{0,24},{4,28},{8,16},{12,20},{16,8},{20,12},{24,0},{28,4},{1,25},{... | collective-permute-start | bytes 405512 | tf_op jit(solution)/shard_map/ppermute | solution.py:296
  82.9 11.3 %collective-permute-start.16 = (bf16[528,128]{1,0:T(8,128)(2,1)S(1)}, bf16[528,128]{1,0:T(8,128)(2,1)S(1)}, u32[]{:S(2)}, u32[]{:S(2)}) collective-permute-start(bf16[528,128]{1,0:T(8,128)(2,1)S(1)} %get-tuple-element.34), channel_id=1, source_target_pairs={{0,28},{4,24},{8,20},{12,16},{16,12},{20,8},{24,4},{28,0},{1,29},{... | collective-permute-start | bytes 405512 | tf_op jit(solution)/shard_map/ppermute | solution.py:296
  96.0 8.3 %collective-permute-start.19 = (bf16[256,512]{1,0:T(8,128)(2,1)S(1)}, bf16[256,512]{1,0:T(8,128)(2,1)}, u32[]{:S(2)}, u32[]{:S(2)}) collective-permute-start(bf16[256,512]{1,0:T(8,128)(2,1)S(1)} %combine_pieces.1.refs_0_), channel_id=1, source_target_pairs={{0,2},{1,3},{2,0},{3,1},{4,6},{5,7},{6,4},{7,5},{8,10},{9,11},{10,... | collective-permute-start | bytes 786440 | tf_op jit(solution)/shard_map/ppermute | solution.py:324
  96.4 8.0 %collective-permute-start.18 = (bf16[256,512]{1,0:T(8,128)(2,1)S(1)}, bf16[256,512]{1,0:T(8,128)(2,1)}, u32[]{:S(2)}, u32[]{:S(2)}) collective-permute-start(bf16[256,512]{1,0:T(8,128)(2,1)S(1)} %combine_pieces.1.refs_0_), channel_id=1, source_target_pairs={{0,1},{1,0},{2,3},{3,2},{4,5},{5,4},{6,7},{7,6},{8,9},{9,8},{10,11... | collective-permute-start | bytes 786440 | tf_op jit(solution)/shard_map/ppermute | solution.py:325
  104.3 1.9 %collective-permute-start.20 = (bf16[256,512]{1,0:T(8,128)(2,1)}, bf16[256,512]{1,0:T(8,128)(2,1)}, u32[]{:S(2)}, u32[]{:S(2)}) collective-permute-start(bf16[256,512]{1,0:T(8,128)(2,1)} %collective-permute-done.19.refs_2_), channel_id=1, source_target_pairs={{0,1},{1,0},{2,3},{3,2},{4,5},{5,4},{6,7},{7,6},{8,9},{9,8},{10,11... | collective-permute-start | bytes 786440 | tf_op jit(solution)/shard_map/ppermute | solution.py:326

commit v3 on v2

--- a/solution.py
+++ b/solution.py
@@ -15,6 +15,7 @@
 SEL = 2
 ROWS = GROUP * TILE
 SLOT = ROWS + 16
+NEAR = 4
 SCALE = HD ** (-0.5)
 LOG2E = math.log2(math.e)
 VMEM_LIMIT = 48 * 1024 * 1024
@@ -42,23 +43,28 @@
     return tile, block, filled
 
 
-def pack_kernel(tiles, blocks, me_ref, selected_ref, query_ref, *slots):
-    for offset, slot in enumerate(slots):
-        peer = me_ref[0] ^ offset
+def pack_kernel(tiles, blocks, me_ref, selected_ref, query_ref, near_ref, *far_refs):
+    def fill(slot, peer):
         tile, block, _ = route(selected_ref, me_ref[0], peer, tiles, blocks)
         rows = pl.ds(pl.multiple_of(tile * TILE, TILE), TILE)
         for head in range(GROUP):
             slot[head * TILE : (head + 1) * TILE, :] = query_ref[rows, head * HD : (head + 1) * HD]
         slot[ROWS:SLOT, :] = jnp.full((16, HD), block.astype(jnp.float32)).astype(jnp.bfloat16)
 
+    for place in range(NEAR):
+        fill(near_ref.at[place], (me_ref[0] & ~(NEAR - 1)) + place)
+    for index, slot in enumerate(far_refs):
+        fill(slot, me_ref[0] ^ (NEAR + index))
+
 
 def pack(me, selected, queries, seq_count, blocks):
     tiles = queries.shape[0] // TILE
     return pl.pallas_call(
         functools.partial(pack_kernel, tiles, blocks),
-        out_shape=[jax.ShapeDtypeStruct((SLOT, HD), jnp.bfloat16)] * seq_count,
+        out_shape=[jax.ShapeDtypeStruct((NEAR, SLOT, HD), jnp.bfloat16)]
+        + [jax.ShapeDtypeStruct((SLOT, HD), jnp.bfloat16)] * (seq_count - NEAR),
         in_specs=[smem, smem, vmem],
-        out_specs=[vmem] * seq_count,
+        out_specs=[vmem] * (seq_count - NEAR + 1),
         compiler_params=params(),
         name="pack_queries",
     )(me, selected, queries)
@@ -172,17 +178,57 @@
     )(*slots, kv_cache, *after)
 
 
+def serve_group_kernel(slots_ref, kv_ref, *refs):
+    out_ref, keys, values, sems = refs[-4:]
+    copies = []
+    for place in range(NEAR):
+        number = jnp.max(slots_ref[place, ROWS:SLOT, :].astype(jnp.float32)).astype(jnp.int32)
+        start = pl.multiple_of(number * BLK, BLK)
+        for half, buffer in enumerate((keys, values)):
+            copy = pltpu.make_async_copy(
+                kv_ref.at[half, pl.ds(start, BLK)], buffer.at[place], sems.at[half, place]
+            )
+            copy.start()
+            copies.append(copy)
+    for place in range(NEAR):
+        copies[2 * place].wait()
+        copies[2 * place + 1].wait()
+        attend(slots_ref[place, 0:ROWS, :], keys[place], values[place], None, out_ref.at[place])
+
+
+def serve_group(slots, kv_cache, after):
+    return pl.pallas_call(
+        serve_group_kernel,
+        out_shape=jax.ShapeDtypeStruct((NEAR, SLOT, HD), jnp.bfloat16),
+        in_specs=[vmem, hbm] + [anywhere] * len(after),
+        out_specs=vmem,
+        scratch_shapes=[
+            pltpu.VMEM((NEAR, BLK, HD), jnp.bfloat16),
+            pltpu.VMEM((NEAR, BLK, HD), jnp.bfloat16),
+            pltpu.SemaphoreType.DMA((2, NEAR)),
+        ],
+        compiler_params=params(),
+        cost_estimate=pl.CostEstimate(flops=1 << 36, bytes_accessed=1 << 30, transcendentals=1),
+        name="serve_group",
+    )(slots, kv_cache, *after)
+
+
 def levels_of(parts):
     parts = parts.astype(jnp.float32)
     return parts[0:GROUP] + parts[GROUP : 2 * GROUP] + parts[2 * GROUP : 3 * GROUP]
 
 
-def combine_kernel(tiles, blocks, seq_count, me_ref, selected_ref, own_ref, *refs):
-    slots, out_ref, blend = refs[:seq_count], refs[-2], refs[-1]
-    routes = [
-        route(selected_ref, me_ref[0], me_ref[0] ^ offset, tiles, blocks)
-        for offset in range(seq_count)
-    ]
+def combine_kernel(tiles, blocks, seq_count, me_ref, selected_ref, own_ref, near_ref, *refs):
+    far_refs, out_ref, blend = refs[: seq_count - NEAR], refs[-2], refs[-1]
+    slots, routes = [], []
+    for place in range(NEAR):
+        slots.append(near_ref.at[place])
+        routes.append(
+            route(selected_ref, me_ref[0], (me_ref[0] & ~(NEAR - 1)) + place, tiles, blocks)
+        )
+    for index, slot in enumerate(far_refs):
+        slots.append(slot)
+        routes.append(route(selected_ref, me_ref[0], me_ref[0] ^ (NEAR + index), tiles, blocks))
     slot_levels = [levels_of(slot[ROWS:SLOT, :]) for slot in slots]
     for tile in range(tiles):
         own_level = levels_of(own_ref[tile, ROWS:SLOT, :])
@@ -222,24 +268,25 @@
             ].astype(jnp.bfloat16)
 
 
-def combine(me, selected, own, slots, blocks, after):
-    tiles = own.shape[0]
-    seq_count = len(slots)
+def combine(me, selected, own, near, far, blocks, after):
+    tiles, seq_count = own.shape[0], NEAR + len(far)
     return pl.pallas_call(
         functools.partial(combine_kernel, tiles, blocks, seq_count),
         out_shape=jax.ShapeDtypeStruct((tiles * TILE, GROUP * HD), jnp.bfloat16),
-        in_specs=[smem, smem, vmem] + [vmem] * seq_count + [anywhere] * len(after),
+        in_specs=[smem, smem, vmem, vmem] + [vmem] * len(far) + [anywhere] * len(after),
         out_specs=vmem,
         scratch_shapes=[pltpu.VMEM((ROWS, HD), jnp.float32)],
         compiler_params=params(),
+        cost_estimate=pl.CostEstimate(flops=1 << 36, bytes_accessed=1 << 30, transcendentals=1),
         name="combine_pieces",
-    )(me, selected, own, *slots, *after)
+    )(me, selected, own, near, *far, *after)
 
 
 def project_kernel(heads, me_ref, *refs):
-    attentions, stacks, out_ref = refs[:heads], refs[heads:-1], refs[-1]
-    depth, width = attentions[0].shape[1], stacks[0].shape[1]
-    z, x, h = me_ref[0], me_ref[1], me_ref[2]
+    attentions = refs[:heads]
+    stack, stack_z, stack_x, whole_ref, share_ref, rest_ref = refs[heads:]
+    depth = attentions[0].shape[1]
+    z, h = me_ref[0], me_ref[2]
     lefts = []
     for index in range(heads):
         place = (z ^ index) ^ h
@@ -247,28 +294,65 @@
         for other in range(1, heads):
             left = jnp.where(place == other, attentions[other][...], left)
         lefts.append(left)
-    for side in range(2):
-        total = None
-        for index in range(heads):
-            stack = stacks[2 * side + (index & 1)]
-            part = slice((index >> 1) * depth, ((index >> 1) + 1) * depth)
-            term = jnp.dot(lefts[index], stack[part, :], preferred_element_type=jnp.float32)
-            total = term if total is None else total + term
-        start = pl.multiple_of((x ^ side) * width, width)
-        out_ref[:, pl.ds(start, width)] = total.astype(jnp.bfloat16)
+    near, rest = jnp.concatenate(lefts[0::2], axis=1), jnp.concatenate(lefts[1::2], axis=1)
+    rest_ref[...] = rest
+    share_ref[...] = jnp.dot(near, stack_x[...], preferred_element_type=jnp.float32)
+    whole_ref[...] = (
+        jnp.dot(near, stack[...], preferred_element_type=jnp.float32)
+        + jnp.dot(rest, stack_z[...], preferred_element_type=jnp.float32)
+    ).astype(jnp.bfloat16)
+
+
+def finish_kernel(me_ref, rest_ref, stack_ref, share_ref, whole_ref, out_ref):
+    width = whole_ref.shape[1]
+    x = me_ref[1]
+    total = share_ref[...] + jnp.dot(
+        rest_ref[...], stack_ref[...], preferred_element_type=jnp.float32
+    )
+    out_ref[:, pl.ds(pl.multiple_of(x * width, width), width)] = whole_ref[...]
+    out_ref[:, pl.ds(pl.multiple_of((x ^ 1) * width, width), width)] = total.astype(jnp.bfloat16)
 
 
 def project(numbers, attentions, stacks):
     rows, width = attentions[0].shape[0], stacks[0].shape[1]
     heads = len(attentions)
-    return pl.pallas_call(
+    whole, share, rest = pl.pallas_call(
         functools.partial(project_kernel, heads),
+        out_shape=[
+            jax.ShapeDtypeStruct((rows, width), jnp.bfloat16),
+            jax.ShapeDtypeStruct((rows, width), jnp.float32),
+            jax.ShapeDtypeStruct((rows, stacks[3].shape[0]), jnp.bfloat16),
+        ],
+        in_specs=[smem] + [vmem] * (heads + 3),
+        out_specs=[vmem] * 3,
+        compiler_params=params(),
+        name="project",
+    )(numbers, *attentions, *stacks[:3])
+    return pl.pallas_call(
+        finish_kernel,
         out_shape=jax.ShapeDtypeStruct((rows, 2 * width), jnp.bfloat16),
-        in_specs=[smem] + [vmem] * (heads + len(stacks)),
+        in_specs=[smem] + [vmem] * 4,
         out_specs=vmem,
         compiler_params=params(),
-        name="project",
-    )(numbers, *attentions, *stacks)
+        name="finish",
+    )(numbers, rest, stacks[3], share, whole)
+
+
+def gate_kernel(*refs):
+    del refs
+
+
+def gate(array, *after):
+    return pl.pallas_call(
+        gate_kernel,
+        out_shape=jax.ShapeDtypeStruct(array.shape, array.dtype),
+        in_specs=[anywhere] * (1 + len(after)),
+        out_specs=anywhere,
+        input_output_aliases={0: 0},
+        compiler_params=params(),
+        cost_estimate=pl.CostEstimate(flops=1 << 36, bytes_accessed=1 << 30, transcendentals=1),
+        name="gate",
+    )(array, *after)
 
 
 def pairs(count, offset):
@@ -298,28 +382,39 @@
     stack = stack_z = stack_x = stack_zx = None
     if fast:
         jumps = [jump(out_weight, kvh_count, 0), jump(out_weight, kvh_count, 2)]
+    if fast:
         stack = jnp.concatenate(jumps, axis=0)
         stack_z = move(stack, 2)
         stack_x = move(stack, 1)
-        stack_zx = move(stack_z, 1)
-    outgoing = pack(me, requests, queries, seq_count, blocks)
-    arrived = {offset: move(outgoing[offset], offset) for offset in range(1, seq_count)}
+    groups = [list(range(base, base + NEAR)) for base in range(0, seq_count, NEAR)]
+
+    def swap(array):
+        return lax.all_to_all(
+            array, "seq", split_axis=0, concat_axis=0, axis_index_groups=groups, tiled=True
+        )
+
+    near, *far = pack(me, requests, queries, seq_count, blocks)
+    arrived = {NEAR + index: move(slot, NEAR + index) for index, slot in enumerate(far)}
     returned = {}
 
     def answer(offsets, after):
-        answers = serve([arrived[offset] for offset in offsets], kv_cache, [a for a in after if a is not None])
+        answers = serve([arrived[offset] for offset in offsets], kv_cache, after)
         for offset, result in zip(offsets, answers):
             returned[offset] = move(result, offset)
         return answers[-1]
 
-    own = own_pieces(queries, kv_cache, [outgoing[0]])
-    last = returned[0] = serve([outgoing[0]], kv_cache, [own])[0]
-    last = answer([1, 2, 3], [last, stack])
-    last = answer([4, 5], [last])
-    for place in range(6, seq_count, 2):
-        last = answer([place, place + 1], [last, stack_x])
-    returned = [returned[offset] for offset in range(seq_count)]
-    attention = combine(me, requests, own, returned, blocks, [stack_z] if fast else [])
+    own = own_pieces(queries, kv_cache, [near])
+    near_answers = serve_group(swap(near), kv_cache, [own] + [])
+    returned_near = swap(near_answers)
+    half = (seq_count + NEAR) // 2
+    first = answer(list(range(NEAR, half)), [own] + ([stack] if fast else []))
+    last = answer(list(range(half, seq_count)), [first] + [])
+    if fast:
+        stack_z = gate(stack_z, last)
+        stack_zx = move(stack_z, 1)
+    tick = gate(last, returned_near, *[returned[offset] for offset in range(NEAR, half)], *([stack_x] if fast else []))
+    far = [returned[offset] for offset in range(NEAR, seq_count)]
+    attention = combine(me, requests, own, returned_near, far, blocks, [tick] + [])
     if fast:
         other_y = lax.ppermute(attention, "kvh", pairs(kvh_count, 2))
         other_core = lax.ppermute(attention, "kvh", pairs(kvh_count, 1))

time: 112 us -> 110 us (0.982); the launches traced: 110 us -> 110 us
  waiting for transfers between devices: 45.6 us -> 24.6 us
  starting transfers between devices: 36.7 us -> 49 us
  Pallas kernels: 22.6 us -> 27.2 us
  local copies, waits for them, and re-layouts: 4.85 us -> 8.63 us
    ppermute x17 -> x11, waiting for transfers between devices: 35.8 us -> 14.3 us  [move(): return lax.ppermute(array, 'seq', pairs(seq_count, offset))]
    pallas_call x1 -> x5, Pallas kernels: 3.52 us -> 13 us  [the longest x1 8.37 us: serve_group(): pl.pallas_call(serve_group_kernel, out_shape=jax.ShapeDtypeStruct((NEAR,...]
    all_to_all x0 -> x2, starting transfers between devices: none -> 7.8 us  [swap(): lax.all_to_all(array, 'seq', split_axis=0, concat_axis=0, axis_index_grou...]
    pallas_call x4 -> x2, Pallas kernels: 13.3 us -> 7.2 us  [serve(): pl.pallas_call(functools.partial(serve_kernel, count), out_shape=[jax.Sha...]
    all_to_all x0 -> x2, waiting for transfers between devices: none -> 4.16 us  [swap(): lax.all_to_all(array, 'seq', split_axis=0, concat_axis=0, axis_index_grou...]
    ppermute x1, waiting for transfers between devices: 7.95 us -> 4.6 us  [per_device(): other_y = lax.ppermute(attention, 'kvh', pairs(kvh_count, 2))]
    ppermute x17 -> x11, starting transfers between devices: 29.1 us -> 32.1 us  [move(): return lax.ppermute(array, 'seq', pairs(seq_count, offset))]
    unnamed x17 -> x15, local copies, waits for them, and re-layouts: 4.82 us -> 7.8 us
  transfers between devices with their start and end apart: 22 -> 18, of which waited for: 10 -> 7; matrix products, arithmetic and copies ran while one was open for 0% -> 2% of each run, Pallas kernels for 17% -> 23%
where the time goes in v3:
time: 110 us
  starting transfers between devices  49 us (45%)
  Pallas kernels  27.2 us (25%)
  waiting for transfers between devices  24.6 us (22%)
  local copies, waits for them, and re-layouts  8.63 us (8%)
    ppermute x11, starting transfers between devices, move(): return lax.ppermute(array, 'seq', pairs(seq_count, offset))  32.1 us
    ppermute x11, waiting for transfers between devices, move(): return lax.ppermute(array, 'seq', pairs(seq_count, offset))  14.3 us
    pallas_call x1, Pallas kernels, serve_group(): pl.pallas_call(serve_group_kernel, out_shape=jax.ShapeDtypeStruct((NEAR,...  8.37 us
    unnamed x15, local copies, waits for them, and re-layouts  7.8 us
    all_to_all x2, starting transfers between devices, swap(): lax.all_to_all(array, 'seq', split_axis=0, concat_axis=0, axis_index_grou...  7.8 us
    ppermute x2, starting transfers between devices, jump(): return lax.ppermute(weight, ('seq', 'kvh'), moves)  7.28 us
    pallas_call x2, Pallas kernels, serve(): pl.pallas_call(functools.partial(serve_kernel, count), out_shape=[jax.Sha...  7.2 us
    ppermute x1, waiting for transfers between devices, per_device(): other_y = lax.ppermute(attention, 'kvh', pairs(kvh_count, 2))  4.6 us
  transfers between devices with their start and end apart: 18, of which 7 were waited for; matrix products, arithmetic and copies ran while one was open for 2% of the time, Pallas kernels for 23%

profile of v3, /device:TPU:0, one launch (start us, length us, event | category | flops | bytes accessed | tf_op | source)
XLA Modules:
  0.0 109.6 jit_solution(4656502138563854857)
XLA Ops:
  0.0 1.7 %collective-permute-start.2 = (bf16[512,512]{1,0:T(8,128)(2,1)}, bf16[512,512]{1,0:T(8,128)(2,1)S(1)}, u32[]{:S(2)}, u32[]{:S(2)}) collective-permute-start(bf16[512,512]{1,0:T(8,128)(2,1)} %param.7), channel_id=1, source_target_pairs={{0,0},{1,8},{2,16},{3,24},{4,4},{5,12},{6,20},{7,28},{8,1},{9,9},{... | collective-permute-start | bytes 1572872 | tf_op jit(solution)/shard_map/ppermute | solution.py:368
  1.7 5.6 %collective-permute-start.3 = (bf16[512,512]{1,0:T(8,128)(2,1)}, bf16[512,512]{1,0:T(8,128)(2,1)S(1)}, u32[]{:S(2)}, u32[]{:S(2)}) collective-permute-start(bf16[512,512]{1,0:T(8,128)(2,1)} %param.7), channel_id=1, source_target_pairs={{0,16},{1,24},{2,0},{3,8},{4,20},{5,28},{6,4},{7,12},{8,17},{9,25}... | collective-permute-start | bytes 1572872 | tf_op jit(solution)/shard_map/ppermute | solution.py:368
  7.3 0.0 copy-start
  7.3 0.9 copy-done
  8.2 0.0 copy-start.2
  8.2 0.7 copy-done.2
  8.9 1.6 %pack_queries.1 = (bf16[4,528,128]{2,1,0:T(8,128)(2,1)}, bf16[528,128]{1,0:T(8,128)(2,1)S(1)}, bf16[528,128]{1,0:T(8,128)(2,1)S(1)}, bf16[528,128]{1,0:T(8,128)(2,1)S(1)}, bf16[528,128]{1,0:T(8,128)(2,1)S(1)}) custom-call(s32[1]{0:T(128)} %bitcast.3.me_ref, s32[2,1,2]{2,1,0:T(1,128)S(1)} %copy-done.2, bf16[256,512]{1,0:T(8,128)(2,1)S(1)} %copy-done), custom_call_target="tpu_custom_call" | custom-call | tf_op jit(solution)/shard_map/pack_queries/pallas_call | solution.py:62
  10.5 0.0 collective-permute-start
  10.5 3.8 %collective-permute-start.1 = (bf16[528,128]{1,0:T(8,128)(2,1)S(1)}, bf16[528,128]{1,0:T(8,128)(2,1)S(1)}, u32[]{:S(2)}, u32[]{:S(2)}) collective-permute-start(bf16[528,128]{1,0:T(8,128)(2,1)S(1)} %get-tuple-element.19), channel_id=1, source_target_pairs={{0,20},{4,16},{8,28},{12,24},{16,4},{20,0},{24,12},{28,8},{1,21},{... | collective-permute-start | bytes 405512 | tf_op jit(solution)/shard_map/ppermute | solution.py:380
  14.4 2.4 %collective-permute-start.6 = (bf16[528,128]{1,0:T(8,128)(2,1)S(1)}, bf16[528,128]{1,0:T(8,128)(2,1)S(1)}, u32[]{:S(2)}, u32[]{:S(2)}) collective-permute-start(bf16[528,128]{1,0:T(8,128)(2,1)S(1)} %get-tuple-element.22), channel_id=1, source_target_pairs={{0,24},{4,28},{8,16},{12,20},{16,8},{20,12},{24,0},{28,4},{1,25},{... | collective-permute-start | bytes 405512 | tf_op jit(solution)/shard_map/ppermute | solution.py:380
  16.8 4.1 %all-to-all-start = ((bf16[4,528,128]{2,1,0:T(8,128)(2,1)}), bf16[4,528,128]{2,1,0:T(8,128)(2,1)}, u32[]{:S(2)}, u32[]{:S(2)}) async-start(bf16[4,528,128]{2,1,0:T(8,128)(2,1)} %get-tuple-element.17.refs_0_), calls=%async_computation | async-start | bytes 1081344 | tf_op jit(solution)/shard_map/all_to_all | solution.py:392
  20.9 0.0 copy-start.1
  20.9 0.9 copy-done.1
  21.9 0.0 copy-start.4
  21.9 2.2 %copy-done.4 = bf16[2,8192,128]{2,1,0:T(8,128)(2,1)S(1)} copy-done((bf16[2,8192,128]{2,1,0:T(8,128)(2,1)S(1)}, bf16[2,8192,128]{2,1,0:T(8,128)(2,1)}, u32[]{:S(2)}) %copy-start.4) | copy-done | bytes 4194328
  24.1 0.0 copy-start.5
  24.1 3.3 %own_pieces.1.refs_0_.refs_3_.own_ref = bf16[2,528,128]{2,1,0:T(8,128)(2,1)S(1)} custom-call(bf16[256,512]{1,0:T(8,128)(2,1)S(1)} %copy-done.1, bf16[2,8192,128]{2,1,0:T(8,128)(2,1)S(1)} %copy-done.4, bf16[4,528,128]{2,1,0:T(8,128)(2,1)} %get-tuple-element.17.refs_0_), custom_call_target="tpu_custom_call" | custom-call | flops 68719476736 | bytes 1073741824 | tf_op jit(solution)/shard_map/own_pieces/pallas_call | solution.py:128
  27.4 0.0 collective-permute-done.2
  27.4 1.8 %collective-permute-start.7 = (bf16[528,128]{1,0:T(8,128)(2,1)S(1)}, bf16[528,128]{1,0:T(8,128)(2,1)S(1)}, u32[]{:S(2)}, u32[]{:S(2)}) collective-permute-start(bf16[528,128]{1,0:T(8,128)(2,1)S(1)} %get-tuple-element.23), channel_id=1, source_target_pairs={{0,28},{4,24},{8,20},{12,16},{16,12},{20,8},{24,4},{28,0},{1,29},{... | collective-permute-start | bytes 405512 | tf_op jit(solution)/shard_map/ppermute | solution.py:380
  29.2 0.8 constant_dynamic-update-slice_fusion.1
  30.0 0.0 collective-permute-done.3
  30.0 0.8 constant_dynamic-update-slice_fusion.refs_4_
  30.9 12.0 %collective-permute-start.14 = (bf16[1024,512]{1,0:T(8,128)(2,1)}, bf16[1024,512]{1,0:T(8,128)(2,1)}, u32[]{:S(2)}, u32[]{:S(2)}) collective-permute-start(bf16[1024,512]{1,0:T(8,128)(2,1)} %constant_dynamic-update-slice_fusion.refs_4_), channel_id=1, source_target_pairs={{0,8},{4,12},{8,0},{12,4},{16,24},{20,28},{24,16},{28,20},{1,9},{5... | collective-permute-start | bytes 3145736 | tf_op jit(solution)/shard_map/ppermute | solution.py:380
  42.8 3.1 %collective-permute-done.refs_0_ = bf16[528,128]{1,0:T(8,128)(2,1)S(1)} collective-permute-done((bf16[528,128]{1,0:T(8,128)(2,1)S(1)}, bf16[528,128]{1,0:T(8,128)(2,1)S(1)}, u32[]{:S(2)}, u32[]{:S(2)}) %collective-permute-start) | collective-permute-done | bytes 135200 | tf_op jit(solution)/shard_map/ppermute | solution.py:380
  45.9 1.5 %collective-permute-start.10 = (bf16[1024,512]{1,0:T(8,128)(2,1)}, bf16[1024,512]{1,0:T(8,128)(2,1)}, u32[]{:S(2)}, u32[]{:S(2)}) collective-permute-start(bf16[1024,512]{1,0:T(8,128)(2,1)} %constant_dynamic-update-slice_fusion.refs_4_), channel_id=1, source_target_pairs={{0,4},{4,0},{8,12},{12,8},{16,20},{20,16},{24,28},{28,24},{1,5},{5... | collective-permute-start | bytes 3145736 | tf_op jit(solution)/shard_map/ppermute | solution.py:380
  47.4 2.3 %collective-permute-done.1.refs_1_ = bf16[528,128]{1,0:T(8,128)(2,1)S(1)} collective-permute-done((bf16[528,128]{1,0:T(8,128)(2,1)S(1)}, bf16[528,128]{1,0:T(8,128)(2,1)S(1)}, u32[]{:S(2)}, u32[]{:S(2)}) %collective-permute-start.1) | collective-permute-done | bytes 135200 | tf_op jit(solution)/shard_map/ppermute | solution.py:380
  49.7 0.0 copy-done.5
  49.7 3.9 %serve_slots.2 = (bf16[528,128]{1,0:T(8,128)(2,1)S(1)}, bf16[528,128]{1,0:T(8,128)(2,1)}) custom-call(bf16[528,128]{1,0:T(8,128)(2,1)S(1)} %collective-permute-done.refs_0_, bf16[528,128]{1,0:T(8,128)(2,1)S(1)} %collective-permute-done.1.refs_1_, bf16[2,8192,128]{2,1,0:T(8,128)(2,1)S(1)} %copy-done.5, ...), custom_call_target="tpu_custom_call" | custom-call | flops 68719476736 | bytes 1073741824 | tf_op jit(solution)/shard_map/serve_slots/pallas_call | solution.py:165
  53.6 0.1 collective-permute-start.5
  53.7 0.0 collective-permute-done.6.refs_0_
  53.7 0.0 collective-permute-done.7.refs_1_
  53.7 3.3 %serve_slots.3 = (bf16[528,128]{1,0:T(8,128)(2,1)S(1)}, bf16[528,128]{1,0:T(8,128)(2,1)S(1)}) custom-call(bf16[528,128]{1,0:T(8,128)(2,1)S(1)} %collective-permute-done.6.refs_0_, bf16[528,128]{1,0:T(8,128)(2,1)S(1)} %collective-permute-done.7.refs_1_, bf16[2,8192,128]{2,1,0:T(8,128)(2,1)S(1)} %copy-done.5, bf16[528,128]{1,0:T(8,128)(2,1)} %get-tuple-element.21.refs_3_), custom_call_target="tpu_custom_call" | custom-call | flops 68719476736 | bytes 1073741824 | tf_op jit(solution)/shard_map/serve_slots/pallas_call | solution.py:165
  57.0 3.0 %collective-permute-start.9 = (bf16[528,128]{1,0:T(8,128)(2,1)S(1)}, bf16[528,128]{1,0:T(8,128)(2,1)S(1)}, u32[]{:S(2)}, u32[]{:S(2)}) collective-permute-start(bf16[528,128]{1,0:T(8,128)(2,1)S(1)} %get-tuple-element.25.refs_0_.refs_1_), channel_id=1, source_target_pairs={{0,28},{4,24},{8,20},{12,16},{16,12},{20,8},{24,4},{28,0},{1,29},{... | collective-permute-start | bytes 405512 | tf_op jit(solution)/shard_map/ppermute | solution.py:380
  60.0 2.9 %collective-permute-start.4 = (bf16[528,128]{1,0:T(8,128)(2,1)S(1)}, bf16[528,128]{1,0:T(8,128)(2,1)S(1)}, u32[]{:S(2)}, u32[]{:S(2)}) collective-permute-start(bf16[528,128]{1,0:T(8,128)(2,1)S(1)} %get-tuple-element.20), channel_id=1, source_target_pairs={{0,16},{4,20},{8,24},{12,28},{16,0},{20,4},{24,8},{28,12},{1,17},{... | collective-permute-start | bytes 405512 | tf_op jit(solution)/shard_map/ppermute | solution.py:380
  62.9 0.0 all-to-all-done.slots_ref
  62.9 0.0 copy-start.6
  62.9 2.2 %copy-done.6 = bf16[2,8192,128]{2,1,0:T(8,128)(2,1)S(1)} copy-done((bf16[2,8192,128]{2,1,0:T(8,128)(2,1)S(1)}, bf16[2,8192,128]{2,1,0:T(8,128)(2,1)}, u32[]{:S(2)}) %copy-start.6) | copy-done | bytes 4194328
  65.1 8.4 %serve_group.1 = bf16[4,528,128]{2,1,0:T(8,128)(2,1)} custom-call(bf16[4,528,128]{2,1,0:T(8,128)(2,1)} %all-to-all-done.slots_ref, bf16[2,8192,128]{2,1,0:T(8,128)(2,1)S(1)} %copy-done.6, bf16[2,528,128]{2,1,0:T(8,128)(2,1)S(1)} %own_pieces.1.refs_0_.refs_3_.own_ref), custom_call_target="tpu_custom_call" | custom-call | flops 68719476736 | bytes 1073741824 | tf_op jit(solution)/shard_map/serve_group/pallas_call | solution.py:200
  73.5 3.7 %all-to-all-start.1 = ((bf16[4,528,128]{2,1,0:T(8,128)(2,1)}), bf16[4,528,128]{2,1,0:T(8,128)(2,1)S(1)}, u32[]{:S(2)}, u32[]{:S(2)}) async-start(bf16[4,528,128]{2,1,0:T(8,128)(2,1)} %serve_group.1), calls=%async_computation.1 | async-start | bytes 1081344 | tf_op jit(solution)/shard_map/all_to_all | solution.py:392
  77.1 2.4 %collective-permute-done.14.refs_0_ = bf16[1024,512]{1,0:T(8,128)(2,1)} collective-permute-done((bf16[1024,512]{1,0:T(8,128)(2,1)}, bf16[1024,512]{1,0:T(8,128)(2,1)}, u32[]{:S(2)}, u32[]{:S(2)}) %collective-permute-start.14) | collective-permute-done | bytes 1048608 | tf_op jit(solution)/shard_map/ppermute | solution.py:380
  79.5 3.1 %collective-permute-start.8 = (bf16[528,128]{1,0:T(8,128)(2,1)S(1)}, bf16[528,128]{1,0:T(8,128)(2,1)S(1)}, u32[]{:S(2)}, u32[]{:S(2)}) collective-permute-start(bf16[528,128]{1,0:T(8,128)(2,1)S(1)} %get-tuple-element.24), channel_id=1, source_target_pairs={{0,24},{4,28},{8,16},{12,20},{16,8},{20,12},{24,0},{28,4},{1,25},{... | collective-permute-start | bytes 405512 | tf_op jit(solution)/shard_map/ppermute | solution.py:380
  82.6 0.0 copy-start.3
  82.6 0.0 collective-permute-done.9.refs_3_
  82.6 1.5 %collective-permute-start.15 = (bf16[1024,512]{1,0:T(8,128)(2,1)}, bf16[1024,512]{1,0:T(8,128)(2,1)S(1)}, u32[]{:S(2)}, u32[]{:S(2)}) collective-permute-start(bf16[1024,512]{1,0:T(8,128)(2,1)} %gate.3.refs_5_), channel_id=1, source_target_pairs={{0,4},{4,0},{8,12},{12,8},{16,20},{20,16},{24,28},{28,24},{1,5},{5... | collective-permute-start | bytes 3145736 | tf_op jit(solution)/shard_map/ppermute | solution.py:380
  84.1 0.0 collective-permute-done.5.refs_3_.refs_1_
  84.1 0.0 collective-permute-done.4.refs_2_.refs_0_
  84.1 0.0 collective-permute-done.10.refs_4_.refs_6_
  84.1 4.2 %all-to-all-done.1.refs_1_.near_ref = bf16[4,528,128]{2,1,0:T(8,128)(2,1)S(1)} async-done(((bf16[4,528,128]{2,1,0:T(8,128)(2,1)}), bf16[4,528,128]{2,1,0:T(8,128)(2,1)S(1)}, u32[]{:S(2)}, u32[]{:S(2)}) %all-to-all-start.1) | async-done | bytes 540704 | tf_op jit(solution)/shard_map/all_to_all | solution.py:392
  88.2 0.0 collective-permute-done.8.refs_2_
  88.2 0.0 copy-done.3
  88.3 2.1 %combine_pieces.1.refs_0_ = bf16[256,512]{1,0:T(8,128)(2,1)S(1)} custom-call(s32[1]{0:T(128)} %bitcast.3.me_ref, s32[2,1,2]{2,1,0:T(1,128)S(1)} %copy-done.3, bf16[2,528,128]{2,1,0:T(8,128)(2,1)S(1)} %own_pieces.1.refs_0_.refs_3_.own_ref, bf16[4,528,128]{2,1,0:T(8,128)(2,1)S(1)} %all-to-all-done.1.refs_1_.near_ref, ...), custom_call_target="tpu_custom_call" | custom-call | flops 68719476736 | bytes 1073741824 | tf_op jit(solution)/shard_map/combine_pieces/pallas_call | solution.py:273
  90.4 1.8 %collective-permute-start.12 = (bf16[256,512]{1,0:T(8,128)(2,1)S(1)}, bf16[256,512]{1,0:T(8,128)(2,1)S(1)}, u32[]{:S(2)}, u32[]{:S(2)}) collective-permute-start(bf16[256,512]{1,0:T(8,128)(2,1)S(1)} %combine_pieces.1.refs_0_), channel_id=1, source_target_pairs={{0,2},{1,3},{2,0},{3,1},{4,6},{5,7},{6,4},{7,5},{8,10},{9,11},{10,... | collective-permute-start | bytes 786440 | tf_op jit(solution)/shard_map/ppermute | solution.py:419
  92.2 0.0 collective-permute-start.11
  92.2 4.6 %collective-permute-done.12.refs_2_ = bf16[256,512]{1,0:T(8,128)(2,1)S(1)} collective-permute-done((bf16[256,512]{1,0:T(8,128)(2,1)S(1)}, bf16[256,512]{1,0:T(8,128)(2,1)S(1)}, u32[]{:S(2)}, u32[]{:S(2)}) %collective-permute-start.12) | collective-permute-done | bytes 262176 | tf_op jit(solution)/shard_map/ppermute | solution.py:419
  96.8 0.0 collective-permute-start.13
  96.8 0.1 pad_add_fusion.me_ref
  96.9 0.0 collective-permute-done.11.refs_1_
  96.9 1.5 %collective-permute-done.13.refs_3_ = bf16[256,512]{1,0:T(8,128)(2,1)S(1)} collective-permute-done((bf16[256,512]{1,0:T(8,128)(2,1)S(1)}, bf16[256,512]{1,0:T(8,128)(2,1)S(1)}, u32[]{:S(2)}, u32[]{:S(2)}) %collective-permute-start.13) | collective-permute-done | bytes 262176 | tf_op jit(solution)/shard_map/ppermute | solution.py:421
  98.3 2.8 %project.1 = (bf16[256,512]{1,0:T(8,128)(2,1)S(1)}, f32[256,512]{1,0:T(8,128)S(1)}, bf16[256,1024]{1,0:T(8,128)(2,1)S(1)}) custom-call(s32[3]{0:T(128)S(1)} %pad_add_fusion.me_ref, bf16[256,512]{1,0:T(8,128)(2,1)S(1)} %combine_pieces.1.refs_0_, bf16[256,512]{1,0:T(8,128)(2,1)S(1)} %collective-permute-done.11.refs_1_, ...), custom_call_target="tpu_custom_call" | custom-call | tf_op jit(solution)/shard_map/project/pallas_call | solution.py:319
  101.2 6.6 %collective-permute-done.15.stack_ref = bf16[1024,512]{1,0:T(8,128)(2,1)S(1)} collective-permute-done((bf16[1024,512]{1,0:T(8,128)(2,1)}, bf16[1024,512]{1,0:T(8,128)(2,1)S(1)}, u32[]{:S(2)}, u32[]{:S(2)}) %collective-permute-start.15) | collective-permute-done | bytes 1048608 | tf_op jit(solution)/shard_map/ppermute | solution.py:380
  107.8 1.8 %finish.1 = bf16[256,1024]{1,0:T(8,128)(2,1)} custom-call(s32[3]{0:T(128)S(1)} %pad_add_fusion.me_ref, bf16[256,1024]{1,0:T(8,128)(2,1)S(1)} %get-tuple-element.26.rest_ref, bf16[1024,512]{1,0:T(8,128)(2,1)S(1)} %collective-permute-done.15.stack_ref, f32[256,512]{1,0:T(8,128)S(1)} %get-tuple-element.27.share_ref, ...), custom_call_target="tpu_custom_call" | custom-call | tf_op jit(solution)/shard_map/finish/pallas_call | solution.py:331
  (2 shorter events, 0.0 us)
Async XLA Ops:
  0.0 27.4 %collective-permute-start.2 = (bf16[512,512]{1,0:T(8,128)(2,1)}, bf16[512,512]{1,0:T(8,128)(2,1)S(1)}, u32[]{:S(2)}, u32[]{:S(2)}) collective-permute-start(bf16[512,512]{1,0:T(8,128)(2,1)} %param.7), channel_id=1, source_target_pairs={{0,0},{1,8},{2,16},{3,24},{4,4},{5,12},{6,20},{7,28},{8,1},{9,9},{... | collective-permute-start | bytes 1572872 | tf_op jit(solution)/shard_map/ppermute | solution.py:368
  1.7 28.3 %collective-permute-start.3 = (bf16[512,512]{1,0:T(8,128)(2,1)}, bf16[512,512]{1,0:T(8,128)(2,1)S(1)}, u32[]{:S(2)}, u32[]{:S(2)}) collective-permute-start(bf16[512,512]{1,0:T(8,128)(2,1)} %param.7), channel_id=1, source_target_pairs={{0,16},{1,24},{2,0},{3,8},{4,20},{5,28},{6,4},{7,12},{8,17},{9,25}... | collective-permute-start | bytes 1572872 | tf_op jit(solution)/shard_map/ppermute | solution.py:368
  7.3 0.9 copy-start
  8.2 0.7 copy-start.2
  10.5 35.4 %collective-permute-start = (bf16[528,128]{1,0:T(8,128)(2,1)S(1)}, bf16[528,128]{1,0:T(8,128)(2,1)S(1)}, u32[]{:S(2)}, u32[]{:S(2)}) collective-permute-start(bf16[528,128]{1,0:T(8,128)(2,1)S(1)} %get-tuple-element.18), channel_id=1, source_target_pairs={{0,16},{4,20},{8,24},{12,28},{16,0},{20,4},{24,8},{28,12},{1,17},{... | collective-permute-start | bytes 405512 | tf_op jit(solution)/shard_map/ppermute | solution.py:380
  10.5 39.1 %collective-permute-start.1 = (bf16[528,128]{1,0:T(8,128)(2,1)S(1)}, bf16[528,128]{1,0:T(8,128)(2,1)S(1)}, u32[]{:S(2)}, u32[]{:S(2)}) collective-permute-start(bf16[528,128]{1,0:T(8,128)(2,1)S(1)} %get-tuple-element.19), channel_id=1, source_target_pairs={{0,20},{4,16},{8,28},{12,24},{16,4},{20,0},{24,12},{28,8},{1,21},{... | collective-permute-start | bytes 405512 | tf_op jit(solution)/shard_map/ppermute | solution.py:380
  14.4 39.3 %collective-permute-start.6 = (bf16[528,128]{1,0:T(8,128)(2,1)S(1)}, bf16[528,128]{1,0:T(8,128)(2,1)S(1)}, u32[]{:S(2)}, u32[]{:S(2)}) collective-permute-start(bf16[528,128]{1,0:T(8,128)(2,1)S(1)} %get-tuple-element.22), channel_id=1, source_target_pairs={{0,24},{4,28},{8,16},{12,20},{16,8},{20,12},{24,0},{28,4},{1,25},{... | collective-permute-start | bytes 405512 | tf_op jit(solution)/shard_map/ppermute | solution.py:380
  16.8 46.1 %all-to-all-start = ((bf16[4,528,128]{2,1,0:T(8,128)(2,1)}), bf16[4,528,128]{2,1,0:T(8,128)(2,1)}, u32[]{:S(2)}, u32[]{:S(2)}) async-start(bf16[4,528,128]{2,1,0:T(8,128)(2,1)} %get-tuple-element.17.refs_0_), calls=%async_computation | async-start | bytes 1081344 | tf_op jit(solution)/shard_map/all_to_all | solution.py:392
  20.9 1.0 copy-start.1
  21.9 2.2 %copy-start.4 = (bf16[2,8192,128]{2,1,0:T(8,128)(2,1)S(1)}, bf16[2,8192,128]{2,1,0:T(8,128)(2,1)}, u32[]{:S(2)}) copy-start(bf16[2,8192,128]{2,1,0:T(8,128)(2,1)} %refs_2_.3) | copy-start | bytes 12582916
  24.1 25.6 %copy-start.5 = (bf16[2,8192,128]{2,1,0:T(8,128)(2,1)S(1)}, bf16[2,8192,128]{2,1,0:T(8,128)(2,1)}, u32[]{:S(2)}) copy-start(bf16[2,8192,128]{2,1,0:T(8,128)(2,1)} %refs_2_.3) | copy-start | bytes 12582916
  27.4 26.3 %collective-permute-start.7 = (bf16[528,128]{1,0:T(8,128)(2,1)S(1)}, bf16[528,128]{1,0:T(8,128)(2,1)S(1)}, u32[]{:S(2)}, u32[]{:S(2)}) collective-permute-start(bf16[528,128]{1,0:T(8,128)(2,1)S(1)} %get-tuple-element.23), channel_id=1, source_target_pairs={{0,28},{4,24},{8,20},{12,16},{16,12},{20,8},{24,4},{28,0},{1,29},{... | collective-permute-start | bytes 405512 | tf_op jit(solution)/shard_map/ppermute | solution.py:380
  30.9 48.7 %collective-permute-start.14 = (bf16[1024,512]{1,0:T(8,128)(2,1)}, bf16[1024,512]{1,0:T(8,128)(2,1)}, u32[]{:S(2)}, u32[]{:S(2)}) collective-permute-start(bf16[1024,512]{1,0:T(8,128)(2,1)} %constant_dynamic-update-slice_fusion.refs_4_), channel_id=1, source_target_pairs={{0,8},{4,12},{8,0},{12,4},{16,24},{20,28},{24,16},{28,20},{1,9},{5... | collective-permute-start | bytes 3145736 | tf_op jit(solution)/shard_map/ppermute | solution.py:380
  45.9 38.2 %collective-permute-start.10 = (bf16[1024,512]{1,0:T(8,128)(2,1)}, bf16[1024,512]{1,0:T(8,128)(2,1)}, u32[]{:S(2)}, u32[]{:S(2)}) collective-permute-start(bf16[1024,512]{1,0:T(8,128)(2,1)} %constant_dynamic-update-slice_fusion.refs_4_), channel_id=1, source_target_pairs={{0,4},{4,0},{8,12},{12,8},{16,20},{20,16},{24,28},{28,24},{1,5},{5... | collective-permute-start | bytes 3145736 | tf_op jit(solution)/shard_map/ppermute | solution.py:380
  53.6 30.5 %collective-permute-start.5 = (bf16[528,128]{1,0:T(8,128)(2,1)}, bf16[528,128]{1,0:T(8,128)(2,1)}, u32[]{:S(2)}, u32[]{:S(2)}) collective-permute-start(bf16[528,128]{1,0:T(8,128)(2,1)} %get-tuple-element.21.refs_3_), channel_id=1, source_target_pairs={{0,20},{4,16},{8,28},{12,24},{16,4},{20,0},{24,12},{28,8},{1,21},{... | collective-permute-start | bytes 405512 | tf_op jit(solution)/shard_map/ppermute | solution.py:380
  57.0 25.6 %collective-permute-start.9 = (bf16[528,128]{1,0:T(8,128)(2,1)S(1)}, bf16[528,128]{1,0:T(8,128)(2,1)S(1)}, u32[]{:S(2)}, u32[]{:S(2)}) collective-permute-start(bf16[528,128]{1,0:T(8,128)(2,1)S(1)} %get-tuple-element.25.refs_0_.refs_1_), channel_id=1, source_target_pairs={{0,28},{4,24},{8,20},{12,16},{16,12},{20,8},{24,4},{28,0},{1,29},{... | collective-permute-start | bytes 405512 | tf_op jit(solution)/shard_map/ppermute | solution.py:380
  60.0 24.1 %collective-permute-start.4 = (bf16[528,128]{1,0:T(8,128)(2,1)S(1)}, bf16[528,128]{1,0:T(8,128)(2,1)S(1)}, u32[]{:S(2)}, u32[]{:S(2)}) collective-permute-start(bf16[528,128]{1,0:T(8,128)(2,1)S(1)} %get-tuple-element.20), channel_id=1, source_target_pairs={{0,16},{4,20},{8,24},{12,28},{16,0},{20,4},{24,8},{28,12},{1,17},{... | collective-permute-start | bytes 405512 | tf_op jit(solution)/shard_map/ppermute | solution.py:380
  62.9 2.2 %copy-start.6 = (bf16[2,8192,128]{2,1,0:T(8,128)(2,1)S(1)}, bf16[2,8192,128]{2,1,0:T(8,128)(2,1)}, u32[]{:S(2)}) copy-start(bf16[2,8192,128]{2,1,0:T(8,128)(2,1)} %refs_2_.3) | copy-start | bytes 12582916
  73.5 14.8 %all-to-all-start.1 = ((bf16[4,528,128]{2,1,0:T(8,128)(2,1)}), bf16[4,528,128]{2,1,0:T(8,128)(2,1)S(1)}, u32[]{:S(2)}, u32[]{:S(2)}) async-start(bf16[4,528,128]{2,1,0:T(8,128)(2,1)} %serve_group.1), calls=%async_computation.1 | async-start | bytes 1081344 | tf_op jit(solution)/shard_map/all_to_all | solution.py:392
  79.5 8.7 %collective-permute-start.8 = (bf16[528,128]{1,0:T(8,128)(2,1)S(1)}, bf16[528,128]{1,0:T(8,128)(2,1)S(1)}, u32[]{:S(2)}, u32[]{:S(2)}) collective-permute-start(bf16[528,128]{1,0:T(8,128)(2,1)S(1)} %get-tuple-element.24), channel_id=1, source_target_pairs={{0,24},{4,28},{8,16},{12,20},{16,8},{20,12},{24,0},{28,4},{1,25},{... | collective-permute-start | bytes 405512 | tf_op jit(solution)/shard_map/ppermute | solution.py:380
  82.6 5.7 %copy-start.3 = (s32[2,1,2]{2,1,0:T(1,128)S(1)}, s32[2,1,2]{2,1,0:T(1,128)}, u32[]{:S(2)}) copy-start(s32[2,1,2]{2,1,0:T(1,128)} %selected_ref.3) | copy-start | bytes 52
  82.6 25.2 %collective-permute-start.15 = (bf16[1024,512]{1,0:T(8,128)(2,1)}, bf16[1024,512]{1,0:T(8,128)(2,1)S(1)}, u32[]{:S(2)}, u32[]{:S(2)}) collective-permute-start(bf16[1024,512]{1,0:T(8,128)(2,1)} %gate.3.refs_5_), channel_id=1, source_target_pairs={{0,4},{4,0},{8,12},{12,8},{16,20},{20,16},{24,28},{28,24},{1,5},{5... | collective-permute-start | bytes 3145736 | tf_op jit(solution)/shard_map/ppermute | solution.py:380
  90.4 6.4 %collective-permute-start.12 = (bf16[256,512]{1,0:T(8,128)(2,1)S(1)}, bf16[256,512]{1,0:T(8,128)(2,1)S(1)}, u32[]{:S(2)}, u32[]{:S(2)}) collective-permute-start(bf16[256,512]{1,0:T(8,128)(2,1)S(1)} %combine_pieces.1.refs_0_), channel_id=1, source_target_pairs={{0,2},{1,3},{2,0},{3,1},{4,6},{5,7},{6,4},{7,5},{8,10},{9,11},{10,... | collective-permute-start | bytes 786440 | tf_op jit(solution)/shard_map/ppermute | solution.py:419
  92.2 4.7 %collective-permute-start.11 = (bf16[256,512]{1,0:T(8,128)(2,1)S(1)}, bf16[256,512]{1,0:T(8,128)(2,1)S(1)}, u32[]{:S(2)}, u32[]{:S(2)}) collective-permute-start(bf16[256,512]{1,0:T(8,128)(2,1)S(1)} %combine_pieces.1.refs_0_), channel_id=1, source_target_pairs={{0,1},{1,0},{2,3},{3,2},{4,5},{5,4},{6,7},{7,6},{8,9},{9,8},{10,11... | collective-permute-start | bytes 786440 | tf_op jit(solution)/shard_map/ppermute | solution.py:420
  96.8 1.5 %collective-permute-start.13 = (bf16[256,512]{1,0:T(8,128)(2,1)S(1)}, bf16[256,512]{1,0:T(8,128)(2,1)S(1)}, u32[]{:S(2)}, u32[]{:S(2)}) collective-permute-start(bf16[256,512]{1,0:T(8,128)(2,1)S(1)} %collective-permute-done.12.refs_2_), channel_id=1, source_target_pairs={{0,1},{1,0},{2,3},{3,2},{4,5},{5,4},{6,7},{7,6},{8,9},{9,8},{10,11... | collective-permute-start | bytes 786440 | tf_op jit(solution)/shard_map/ppermute | solution.py:421

commit v4 on v3

--- a/solution.py
+++ b/solution.py
@@ -303,11 +303,13 @@
     ).astype(jnp.bfloat16)
 
 
-def finish_kernel(me_ref, rest_ref, stack_ref, share_ref, whole_ref, out_ref):
-    width = whole_ref.shape[1]
+def finish_kernel(me_ref, rest_ref, first_ref, second_ref, share_ref, whole_ref, out_ref):
+    depth, width = first_ref.shape
     x = me_ref[1]
-    total = share_ref[...] + jnp.dot(
-        rest_ref[...], stack_ref[...], preferred_element_type=jnp.float32
+    total = (
+        share_ref[...]
+        + jnp.dot(rest_ref[:, :depth], first_ref[...], preferred_element_type=jnp.float32)
+        + jnp.dot(rest_ref[:, depth:], second_ref[...], preferred_element_type=jnp.float32)
     )
     out_ref[:, pl.ds(pl.multiple_of(x * width, width), width)] = whole_ref[...]
     out_ref[:, pl.ds(pl.multiple_of((x ^ 1) * width, width), width)] = total.astype(jnp.bfloat16)
@@ -321,7 +323,7 @@
         out_shape=[
             jax.ShapeDtypeStruct((rows, width), jnp.bfloat16),
             jax.ShapeDtypeStruct((rows, width), jnp.float32),
-            jax.ShapeDtypeStruct((rows, stacks[3].shape[0]), jnp.bfloat16),
+            jax.ShapeDtypeStruct((rows, 2 * stacks[3].shape[0]), jnp.bfloat16),
         ],
         in_specs=[smem] + [vmem] * (heads + 3),
         out_specs=[vmem] * 3,
@@ -331,11 +333,11 @@
     return pl.pallas_call(
         finish_kernel,
         out_shape=jax.ShapeDtypeStruct((rows, 2 * width), jnp.bfloat16),
-        in_specs=[smem] + [vmem] * 4,
+        in_specs=[smem] + [vmem] * 5,
         out_specs=vmem,
         compiler_params=params(),
         name="finish",
-    )(numbers, rest, stacks[3], share, whole)
+    )(numbers, rest, stacks[3], stacks[4], share, whole)
 
 
 def gate_kernel(*refs):
@@ -379,7 +381,7 @@
     def move(array, offset):
         return lax.ppermute(array, "seq", pairs(seq_count, offset))
 
-    stack = stack_z = stack_x = stack_zx = None
+    stack = stack_z = stack_x = None
     if fast:
         jumps = [jump(out_weight, kvh_count, 0), jump(out_weight, kvh_count, 2)]
     if fast:
@@ -410,8 +412,9 @@
     first = answer(list(range(NEAR, half)), [own] + ([stack] if fast else []))
     last = answer(list(range(half, seq_count)), [first] + [])
     if fast:
-        stack_z = gate(stack_z, last)
-        stack_zx = move(stack_z, 1)
+        depth = out_weight.shape[0]
+        first_zx = move(gate(stack_z[:depth], near_answers), 1)
+        second_zx = move(gate(stack_x[depth:], near_answers), 2)
     tick = gate(last, returned_near, *[returned[offset] for offset in range(NEAR, half)], *([stack_x] if fast else []))
     far = [returned[offset] for offset in range(NEAR, seq_count)]
     attention = combine(me, requests, own, returned_near, far, blocks, [tick] + [])
@@ -420,7 +423,7 @@
         other_core = lax.ppermute(attention, "kvh", pairs(kvh_count, 1))
         both = lax.ppermute(other_y, "kvh", pairs(kvh_count, 1))
         gathered = [attention, other_core, other_y, both]
-        stacks = [stack, stack_z, stack_x, stack_zx]
+        stacks = [stack, stack_z, stack_x, first_zx, second_zx]
         numbers = jnp.stack([lax.shift_right_logical(seq, 1), seq & 1, kvh]).astype(jnp.int32)
         return project(numbers, gathered, stacks)
     column_terms = jnp.dot(

time: 110 us -> 107 us (0.973)
  starting transfers between devices: 49 us -> 35.9 us
  waiting for transfers between devices: 24.6 us -> 30.8 us
  local copies, waits for them, and re-layouts: 8.63 us -> 11.6 us
    ppermute x11 -> x12, starting transfers between devices: 32.1 us -> 18.4 us  [move(): return lax.ppermute(array, 'seq', pairs(seq_count, offset))]
    ppermute x11 -> x12, waiting for transfers between devices: 14.3 us -> 19.2 us  [move(): return lax.ppermute(array, 'seq', pairs(seq_count, offset))]
    all_to_all x2, waiting for transfers between devices: 4.16 us -> 7.5 us  [swap(): lax.all_to_all(array, 'seq', split_axis=0, concat_axis=0, axis_index_grou...]
    slice x0 -> x2, local copies, waits for them, and re-layouts: none -> 2.94 us  [the longest x1 1.87 us: per_device(): second_zx = move(gate(stack_x[depth:], near_answers), 2)]
    ppermute x1, waiting for transfers between devices: 4.6 us -> 2.59 us  [per_device(): other_y = lax.ppermute(attention, 'kvh', pairs(kvh_count, 2))]
  transfers between devices with their start and end apart: 18 -> 19, of which waited for: 7 -> 7; matrix products, arithmetic and copies ran while one was open for 2% -> 4% of each run, Pallas kernels for 23% -> 24%
where the time goes in v4:
time: 107 us; the launch traced here: 106 us
  starting transfers between devices  35.9 us (34%)
  waiting for transfers between devices  30.8 us (29%)
  Pallas kernels  27.7 us (26%)
  local copies, waits for them, and re-layouts  11.6 us (11%)
    ppermute x12, waiting for transfers between devices, move(): return lax.ppermute(array, 'seq', pairs(seq_count, offset))  19.2 us
    ppermute x12, starting transfers between devices, move(): return lax.ppermute(array, 'seq', pairs(seq_count, offset))  18.4 us
    pallas_call x1, Pallas kernels, serve_group(): pl.pallas_call(serve_group_kernel, out_shape=jax.ShapeDtypeStruct((NEAR,...  8.38 us
    all_to_all x2, starting transfers between devices, swap(): lax.all_to_all(array, 'seq', split_axis=0, concat_axis=0, axis_index_grou...  7.8 us
    unnamed x15, local copies, waits for them, and re-layouts  7.8 us
    all_to_all x2, waiting for transfers between devices, swap(): lax.all_to_all(array, 'seq', split_axis=0, concat_axis=0, axis_index_grou...  7.5 us
    ppermute x2, starting transfers between devices, jump(): return lax.ppermute(weight, ('seq', 'kvh'), moves)  7.28 us
    pallas_call x2, Pallas kernels, serve(): pl.pallas_call(functools.partial(serve_kernel, count), out_shape=[jax.Sha...  7.2 us
  transfers between devices with their start and end apart: 19, of which 7 were waited for; matrix products, arithmetic and copies ran while one was open for 4% of the time, Pallas kernels for 24%

profile of v4, /device:TPU:0, one launch (start us, length us, event | category | flops | bytes accessed | tf_op | source)
XLA Modules:
  0.0 106.1 jit_solution(10981812337226425932)
XLA Ops:
  0.0 1.7 %collective-permute-start.2 = (bf16[512,512]{1,0:T(8,128)(2,1)}, bf16[512,512]{1,0:T(8,128)(2,1)S(1)}, u32[]{:S(2)}, u32[]{:S(2)}) collective-permute-start(bf16[512,512]{1,0:T(8,128)(2,1)} %param.7), channel_id=1, source_target_pairs={{0,0},{1,8},{2,16},{3,24},{4,4},{5,12},{6,20},{7,28},{8,1},{9,9},{... | collective-permute-start | bytes 1572872 | tf_op jit(solution)/shard_map/ppermute | solution.py:370
  1.7 5.6 %collective-permute-start.3 = (bf16[512,512]{1,0:T(8,128)(2,1)}, bf16[512,512]{1,0:T(8,128)(2,1)S(1)}, u32[]{:S(2)}, u32[]{:S(2)}) collective-permute-start(bf16[512,512]{1,0:T(8,128)(2,1)} %param.7), channel_id=1, source_target_pairs={{0,16},{1,24},{2,0},{3,8},{4,20},{5,28},{6,4},{7,12},{8,17},{9,25}... | collective-permute-start | bytes 1572872 | tf_op jit(solution)/shard_map/ppermute | solution.py:370
  7.3 0.0 copy-start
  7.3 0.9 copy-done
  8.2 0.0 copy-start.2
  8.2 0.7 copy-done.2
  8.9 1.6 %pack_queries.1 = (bf16[4,528,128]{2,1,0:T(8,128)(2,1)}, bf16[528,128]{1,0:T(8,128)(2,1)S(1)}, bf16[528,128]{1,0:T(8,128)(2,1)S(1)}, bf16[528,128]{1,0:T(8,128)(2,1)S(1)}, bf16[528,128]{1,0:T(8,128)(2,1)S(1)}) custom-call(s32[1]{0:T(128)} %bitcast.3.me_ref, s32[2,1,2]{2,1,0:T(1,128)S(1)} %copy-done.2, bf16[256,512]{1,0:T(8,128)(2,1)S(1)} %copy-done), custom_call_target="tpu_custom_call" | custom-call | tf_op jit(solution)/shard_map/pack_queries/pallas_call | solution.py:62
  10.5 0.0 collective-permute-start
  10.5 3.8 %collective-permute-start.1 = (bf16[528,128]{1,0:T(8,128)(2,1)S(1)}, bf16[528,128]{1,0:T(8,128)(2,1)S(1)}, u32[]{:S(2)}, u32[]{:S(2)}) collective-permute-start(bf16[528,128]{1,0:T(8,128)(2,1)S(1)} %get-tuple-element.19), channel_id=1, source_target_pairs={{0,20},{4,16},{8,28},{12,24},{16,4},{20,0},{24,12},{28,8},{1,21},{... | collective-permute-start | bytes 405512 | tf_op jit(solution)/shard_map/ppermute | solution.py:382
  14.4 2.4 %collective-permute-start.6 = (bf16[528,128]{1,0:T(8,128)(2,1)S(1)}, bf16[528,128]{1,0:T(8,128)(2,1)S(1)}, u32[]{:S(2)}, u32[]{:S(2)}) collective-permute-start(bf16[528,128]{1,0:T(8,128)(2,1)S(1)} %get-tuple-element.22), channel_id=1, source_target_pairs={{0,24},{4,28},{8,16},{12,20},{16,8},{20,12},{24,0},{28,4},{1,25},{... | collective-permute-start | bytes 405512 | tf_op jit(solution)/shard_map/ppermute | solution.py:382
  16.8 4.1 %all-to-all-start = ((bf16[4,528,128]{2,1,0:T(8,128)(2,1)}), bf16[4,528,128]{2,1,0:T(8,128)(2,1)}, u32[]{:S(2)}, u32[]{:S(2)}) async-start(bf16[4,528,128]{2,1,0:T(8,128)(2,1)} %get-tuple-element.17.refs_0_), calls=%async_computation | async-start | bytes 1081344 | tf_op jit(solution)/shard_map/all_to_all | solution.py:394
  20.9 0.0 copy-start.1
  21.0 0.9 copy-done.1
  21.9 0.0 copy-start.4
  21.9 2.2 %copy-done.4 = bf16[2,8192,128]{2,1,0:T(8,128)(2,1)S(1)} copy-done((bf16[2,8192,128]{2,1,0:T(8,128)(2,1)S(1)}, bf16[2,8192,128]{2,1,0:T(8,128)(2,1)}, u32[]{:S(2)}) %copy-start.4) | copy-done | bytes 4194328
  24.1 0.0 copy-start.5
  24.1 3.3 %own_pieces.1.refs_0_.refs_3_.own_ref = bf16[2,528,128]{2,1,0:T(8,128)(2,1)S(1)} custom-call(bf16[256,512]{1,0:T(8,128)(2,1)S(1)} %copy-done.1, bf16[2,8192,128]{2,1,0:T(8,128)(2,1)S(1)} %copy-done.4, bf16[4,528,128]{2,1,0:T(8,128)(2,1)} %get-tuple-element.17.refs_0_), custom_call_target="tpu_custom_call" | custom-call | flops 68719476736 | bytes 1073741824 | tf_op jit(solution)/shard_map/own_pieces/pallas_call | solution.py:128
  27.4 0.0 collective-permute-done.2
  27.4 1.8 %collective-permute-start.7 = (bf16[528,128]{1,0:T(8,128)(2,1)S(1)}, bf16[528,128]{1,0:T(8,128)(2,1)S(1)}, u32[]{:S(2)}, u32[]{:S(2)}) collective-permute-start(bf16[528,128]{1,0:T(8,128)(2,1)S(1)} %get-tuple-element.23), channel_id=1, source_target_pairs={{0,28},{4,24},{8,20},{12,16},{16,12},{20,8},{24,4},{28,0},{1,29},{... | collective-permute-start | bytes 405512 | tf_op jit(solution)/shard_map/ppermute | solution.py:382
  29.2 0.8 constant_dynamic-update-slice_fusion.1
  30.0 0.0 collective-permute-done.3
  30.0 0.8 constant_dynamic-update-slice_fusion.refs_4_
  30.9 1.1 %collective-permute-start.10 = (bf16[1024,512]{1,0:T(8,128)(2,1)}, bf16[1024,512]{1,0:T(8,128)(2,1)}, u32[]{:S(2)}, u32[]{:S(2)}) collective-permute-start(bf16[1024,512]{1,0:T(8,128)(2,1)} %constant_dynamic-update-slice_fusion.refs_4_), channel_id=1, source_target_pairs={{0,4},{4,0},{8,12},{12,8},{16,20},{20,16},{24,28},{28,24},{1,5},{5... | collective-permute-start | bytes 3145736 | tf_op jit(solution)/shard_map/ppermute | solution.py:382
  32.0 13.8 %collective-permute-done.refs_0_ = bf16[528,128]{1,0:T(8,128)(2,1)S(1)} collective-permute-done((bf16[528,128]{1,0:T(8,128)(2,1)S(1)}, bf16[528,128]{1,0:T(8,128)(2,1)S(1)}, u32[]{:S(2)}, u32[]{:S(2)}) %collective-permute-start) | collective-permute-done | bytes 135200 | tf_op jit(solution)/shard_map/ppermute | solution.py:382
  45.8 0.0 collective-permute-start.14
  45.8 3.8 %collective-permute-done.1.refs_1_ = bf16[528,128]{1,0:T(8,128)(2,1)S(1)} collective-permute-done((bf16[528,128]{1,0:T(8,128)(2,1)S(1)}, bf16[528,128]{1,0:T(8,128)(2,1)S(1)}, u32[]{:S(2)}, u32[]{:S(2)}) %collective-permute-start.1) | collective-permute-done | bytes 135200 | tf_op jit(solution)/shard_map/ppermute | solution.py:382
  49.6 0.0 copy-done.5
  49.6 3.9 %serve_slots.2 = (bf16[528,128]{1,0:T(8,128)(2,1)S(1)}, bf16[528,128]{1,0:T(8,128)(2,1)}) custom-call(bf16[528,128]{1,0:T(8,128)(2,1)S(1)} %collective-permute-done.refs_0_, bf16[528,128]{1,0:T(8,128)(2,1)S(1)} %collective-permute-done.1.refs_1_, bf16[2,8192,128]{2,1,0:T(8,128)(2,1)S(1)} %copy-done.5, ...), custom_call_target="tpu_custom_call" | custom-call | flops 68719476736 | bytes 1073741824 | tf_op jit(solution)/shard_map/serve_slots/pallas_call | solution.py:165
  53.6 0.7 collective-permute-start.5
  54.2 0.0 collective-permute-done.6.refs_0_
  54.2 0.0 collective-permute-done.7.refs_1_
  54.2 3.3 %serve_slots.3 = (bf16[528,128]{1,0:T(8,128)(2,1)S(1)}, bf16[528,128]{1,0:T(8,128)(2,1)S(1)}) custom-call(bf16[528,128]{1,0:T(8,128)(2,1)S(1)} %collective-permute-done.6.refs_0_, bf16[528,128]{1,0:T(8,128)(2,1)S(1)} %collective-permute-done.7.refs_1_, bf16[2,8192,128]{2,1,0:T(8,128)(2,1)S(1)} %copy-done.5, bf16[528,128]{1,0:T(8,128)(2,1)} %get-tuple-element.21.refs_3_), custom_call_target="tpu_custom_call" | custom-call | flops 68719476736 | bytes 1073741824 | tf_op jit(solution)/shard_map/serve_slots/pallas_call | solution.py:165
  57.5 2.4 %collective-permute-start.9 = (bf16[528,128]{1,0:T(8,128)(2,1)S(1)}, bf16[528,128]{1,0:T(8,128)(2,1)S(1)}, u32[]{:S(2)}, u32[]{:S(2)}) collective-permute-start(bf16[528,128]{1,0:T(8,128)(2,1)S(1)} %get-tuple-element.25.refs_0_), channel_id=1, source_target_pairs={{0,28},{4,24},{8,20},{12,16},{16,12},{20,8},{24,4},{28,0},{1,29},{... | collective-permute-start | bytes 405512 | tf_op jit(solution)/shard_map/ppermute | solution.py:382
  60.0 2.9 %collective-permute-start.4 = (bf16[528,128]{1,0:T(8,128)(2,1)S(1)}, bf16[528,128]{1,0:T(8,128)(2,1)S(1)}, u32[]{:S(2)}, u32[]{:S(2)}) collective-permute-start(bf16[528,128]{1,0:T(8,128)(2,1)S(1)} %get-tuple-element.20), channel_id=1, source_target_pairs={{0,16},{4,20},{8,24},{12,28},{16,0},{20,4},{24,8},{28,12},{1,17},{... | collective-permute-start | bytes 405512 | tf_op jit(solution)/shard_map/ppermute | solution.py:382
  62.8 0.0 all-to-all-done.slots_ref
  62.8 2.2 %copy-done.6 = bf16[2,8192,128]{2,1,0:T(8,128)(2,1)S(1)} copy-done((bf16[2,8192,128]{2,1,0:T(8,128)(2,1)S(1)}, bf16[2,8192,128]{2,1,0:T(8,128)(2,1)}, u32[]{:S(2)}) %copy-start.6) | copy-done | bytes 4194328
  65.0 8.4 %serve_group.1.refs_1_ = bf16[4,528,128]{2,1,0:T(8,128)(2,1)} custom-call(bf16[4,528,128]{2,1,0:T(8,128)(2,1)} %all-to-all-done.slots_ref, bf16[2,8192,128]{2,1,0:T(8,128)(2,1)S(1)} %copy-done.6, bf16[2,528,128]{2,1,0:T(8,128)(2,1)S(1)} %own_pieces.1.refs_0_.refs_3_.own_ref), custom_call_target="tpu_custom_call" | custom-call | flops 68719476736 | bytes 1073741824 | tf_op jit(solution)/shard_map/serve_group/pallas_call | solution.py:200
  73.4 3.7 %all-to-all-start.1 = ((bf16[4,528,128]{2,1,0:T(8,128)(2,1)}), bf16[4,528,128]{2,1,0:T(8,128)(2,1)S(1)}, u32[]{:S(2)}, u32[]{:S(2)}) async-start(bf16[4,528,128]{2,1,0:T(8,128)(2,1)} %serve_group.1.refs_1_), calls=%async_computation.1 | async-start | bytes 1081344 | tf_op jit(solution)/shard_map/all_to_all | solution.py:394
  77.1 0.0 collective-permute-done.10.refs_4_.refs_6_
  77.1 1.3 %collective-permute-start.8 = (bf16[528,128]{1,0:T(8,128)(2,1)S(1)}, bf16[528,128]{1,0:T(8,128)(2,1)S(1)}, u32[]{:S(2)}, u32[]{:S(2)}) collective-permute-start(bf16[528,128]{1,0:T(8,128)(2,1)S(1)} %get-tuple-element.24), channel_id=1, source_target_pairs={{0,24},{4,28},{8,16},{12,20},{16,8},{20,12},{24,0},{28,4},{1,25},{... | collective-permute-start | bytes 405512 | tf_op jit(solution)/shard_map/ppermute | solution.py:382
  78.4 1.9 %slice.9.refs_0_ = bf16[512,512]{1,0:T(8,128)(2,1)} slice(bf16[1024,512]{1,0:T(8,128)(2,1)} %collective-permute-done.10.refs_4_.refs_6_), slice={[512:1024], [0:512]} | slice | bytes 1048576 | tf_op jit(solution)/shard_map/slice | solution.py:417
  80.3 0.3 collective-permute-done.14.refs_5_
  80.6 0.2 collective-permute-start.16
  80.8 1.1 %slice.8.refs_0_ = bf16[512,512]{1,0:T(8,128)(2,1)S(1)} slice(bf16[1024,512]{1,0:T(8,128)(2,1)} %collective-permute-done.14.refs_5_), slice={[0:512], [0:512]} | slice | bytes 1048576 | tf_op jit(solution)/shard_map/slice | solution.py:416
  81.9 0.0 copy-start.3
  81.9 0.0 collective-permute-done.9.refs_3_
  81.9 0.0 collective-permute-done.5.refs_3_.refs_1_
  81.9 0.0 collective-permute-done.4.refs_2_.refs_0_
  81.9 7.5 %all-to-all-done.1.refs_1_.near_ref = bf16[4,528,128]{2,1,0:T(8,128)(2,1)S(1)} async-done(((bf16[4,528,128]{2,1,0:T(8,128)(2,1)}), bf16[4,528,128]{2,1,0:T(8,128)(2,1)S(1)}, u32[]{:S(2)}, u32[]{:S(2)}) %all-to-all-start.1) | async-done | bytes 540704 | tf_op jit(solution)/shard_map/all_to_all | solution.py:394
  89.4 0.0 collective-permute-done.8.refs_2_
  89.4 0.0 copy-done.3
  89.4 2.1 %combine_pieces.1.refs_0_ = bf16[256,512]{1,0:T(8,128)(2,1)S(1)} custom-call(s32[1]{0:T(128)} %bitcast.3.me_ref, s32[2,1,2]{2,1,0:T(1,128)S(1)} %copy-done.3, bf16[2,528,128]{2,1,0:T(8,128)(2,1)S(1)} %own_pieces.1.refs_0_.refs_3_.own_ref, bf16[4,528,128]{2,1,0:T(8,128)(2,1)S(1)} %all-to-all-done.1.refs_1_.near_ref, ...), custom_call_target="tpu_custom_call" | custom-call | flops 68719476736 | bytes 1073741824 | tf_op jit(solution)/shard_map/combine_pieces/pallas_call | solution.py:273
  91.5 2.4 %collective-permute-start.12 = (bf16[256,512]{1,0:T(8,128)(2,1)S(1)}, bf16[256,512]{1,0:T(8,128)(2,1)S(1)}, u32[]{:S(2)}, u32[]{:S(2)}) collective-permute-start(bf16[256,512]{1,0:T(8,128)(2,1)S(1)} %combine_pieces.1.refs_0_), channel_id=1, source_target_pairs={{0,2},{1,3},{2,0},{3,1},{4,6},{5,7},{6,4},{7,5},{8,10},{9,11},{10,... | collective-permute-start | bytes 786440 | tf_op jit(solution)/shard_map/ppermute | solution.py:422
  93.9 1.8 %collective-permute-start.15 = (bf16[512,512]{1,0:T(8,128)(2,1)S(1)}, bf16[512,512]{1,0:T(8,128)(2,1)S(1)}, u32[]{:S(2)}, u32[]{:S(2)}) collective-permute-start(bf16[512,512]{1,0:T(8,128)(2,1)S(1)} %gate.4), channel_id=1, source_target_pairs={{0,4},{4,0},{8,12},{12,8},{16,20},{20,16},{24,28},{28,24},{1,5},{5... | collective-permute-start | bytes 1572872 | tf_op jit(solution)/shard_map/ppermute | solution.py:382
  95.6 0.0 collective-permute-start.11
  95.6 2.6 %collective-permute-done.12.refs_2_ = bf16[256,512]{1,0:T(8,128)(2,1)S(1)} collective-permute-done((bf16[256,512]{1,0:T(8,128)(2,1)S(1)}, bf16[256,512]{1,0:T(8,128)(2,1)S(1)}, u32[]{:S(2)}, u32[]{:S(2)}) %collective-permute-start.12) | collective-permute-done | bytes 262176 | tf_op jit(solution)/shard_map/ppermute | solution.py:422
  98.2 0.0 collective-permute-start.13
  98.2 0.1 pad_add_fusion.me_ref
  98.3 0.0 collective-permute-done.11.refs_1_
  98.3 1.5 %collective-permute-done.13.refs_3_ = bf16[256,512]{1,0:T(8,128)(2,1)S(1)} collective-permute-done((bf16[256,512]{1,0:T(8,128)(2,1)S(1)}, bf16[256,512]{1,0:T(8,128)(2,1)S(1)}, u32[]{:S(2)}, u32[]{:S(2)}) %collective-permute-start.13) | collective-permute-done | bytes 262176 | tf_op jit(solution)/shard_map/ppermute | solution.py:424
  99.8 2.8 %project.1 = (bf16[256,512]{1,0:T(8,128)(2,1)S(1)}, f32[256,512]{1,0:T(8,128)S(1)}, bf16[256,1024]{1,0:T(8,128)(2,1)S(1)}) custom-call(s32[3]{0:T(128)S(1)} %pad_add_fusion.me_ref, bf16[256,512]{1,0:T(8,128)(2,1)S(1)} %combine_pieces.1.refs_0_, bf16[256,512]{1,0:T(8,128)(2,1)S(1)} %collective-permute-done.11.refs_1_, ...), custom_call_target="tpu_custom_call" | custom-call | tf_op jit(solution)/shard_map/project/pallas_call | solution.py:321
  102.6 0.0 collective-permute-done.16.second_ref
  102.6 1.2 %collective-permute-done.15.first_ref = bf16[512,512]{1,0:T(8,128)(2,1)S(1)} collective-permute-done((bf16[512,512]{1,0:T(8,128)(2,1)S(1)}, bf16[512,512]{1,0:T(8,128)(2,1)S(1)}, u32[]{:S(2)}, u32[]{:S(2)}) %collective-permute-start.15) | collective-permute-done | bytes 524320 | tf_op jit(solution)/shard_map/ppermute | solution.py:382
  103.8 2.3 %finish.1 = bf16[256,1024]{1,0:T(8,128)(2,1)} custom-call(s32[3]{0:T(128)S(1)} %pad_add_fusion.me_ref, bf16[256,1024]{1,0:T(8,128)(2,1)S(1)} %get-tuple-element.26.rest_ref, bf16[512,512]{1,0:T(8,128)(2,1)S(1)} %collective-permute-done.15.first_ref, bf16[512,512]{1,0:T(8,128)(2,1)} %collective-permute-done.16.second_ref, ...), custom_call_target="tpu_custom_call" | custom-call | tf_op jit(solution)/shard_map/finish/pallas_call | solution.py:333
  (4 shorter events, 0.0 us)
Async XLA Ops:
  0.0 27.4 %collective-permute-start.2 = (bf16[512,512]{1,0:T(8,128)(2,1)}, bf16[512,512]{1,0:T(8,128)(2,1)S(1)}, u32[]{:S(2)}, u32[]{:S(2)}) collective-permute-start(bf16[512,512]{1,0:T(8,128)(2,1)} %param.7), channel_id=1, source_target_pairs={{0,0},{1,8},{2,16},{3,24},{4,4},{5,12},{6,20},{7,28},{8,1},{9,9},{... | collective-permute-start | bytes 1572872 | tf_op jit(solution)/shard_map/ppermute | solution.py:370
  1.7 28.4 %collective-permute-start.3 = (bf16[512,512]{1,0:T(8,128)(2,1)}, bf16[512,512]{1,0:T(8,128)(2,1)S(1)}, u32[]{:S(2)}, u32[]{:S(2)}) collective-permute-start(bf16[512,512]{1,0:T(8,128)(2,1)} %param.7), channel_id=1, source_target_pairs={{0,16},{1,24},{2,0},{3,8},{4,20},{5,28},{6,4},{7,12},{8,17},{9,25}... | collective-permute-start | bytes 1572872 | tf_op jit(solution)/shard_map/ppermute | solution.py:370
  7.3 0.9 copy-start
  8.2 0.7 copy-start.2
  10.5 35.3 %collective-permute-start = (bf16[528,128]{1,0:T(8,128)(2,1)S(1)}, bf16[528,128]{1,0:T(8,128)(2,1)S(1)}, u32[]{:S(2)}, u32[]{:S(2)}) collective-permute-start(bf16[528,128]{1,0:T(8,128)(2,1)S(1)} %get-tuple-element.18), channel_id=1, source_target_pairs={{0,16},{4,20},{8,24},{12,28},{16,0},{20,4},{24,8},{28,12},{1,17},{... | collective-permute-start | bytes 405512 | tf_op jit(solution)/shard_map/ppermute | solution.py:382
  10.5 39.1 %collective-permute-start.1 = (bf16[528,128]{1,0:T(8,128)(2,1)S(1)}, bf16[528,128]{1,0:T(8,128)(2,1)S(1)}, u32[]{:S(2)}, u32[]{:S(2)}) collective-permute-start(bf16[528,128]{1,0:T(8,128)(2,1)S(1)} %get-tuple-element.19), channel_id=1, source_target_pairs={{0,20},{4,16},{8,28},{12,24},{16,4},{20,0},{24,12},{28,8},{1,21},{... | collective-permute-start | bytes 405512 | tf_op jit(solution)/shard_map/ppermute | solution.py:382
  14.4 39.9 %collective-permute-start.6 = (bf16[528,128]{1,0:T(8,128)(2,1)S(1)}, bf16[528,128]{1,0:T(8,128)(2,1)S(1)}, u32[]{:S(2)}, u32[]{:S(2)}) collective-permute-start(bf16[528,128]{1,0:T(8,128)(2,1)S(1)} %get-tuple-element.22), channel_id=1, source_target_pairs={{0,24},{4,28},{8,16},{12,20},{16,8},{20,12},{24,0},{28,4},{1,25},{... | collective-permute-start | bytes 405512 | tf_op jit(solution)/shard_map/ppermute | solution.py:382
  16.8 46.1 %all-to-all-start = ((bf16[4,528,128]{2,1,0:T(8,128)(2,1)}), bf16[4,528,128]{2,1,0:T(8,128)(2,1)}, u32[]{:S(2)}, u32[]{:S(2)}) async-start(bf16[4,528,128]{2,1,0:T(8,128)(2,1)} %get-tuple-element.17.refs_0_), calls=%async_computation | async-start | bytes 1081344 | tf_op jit(solution)/shard_map/all_to_all | solution.py:394
  20.9 1.0 copy-start.1
  21.9 2.2 %copy-start.4 = (bf16[2,8192,128]{2,1,0:T(8,128)(2,1)S(1)}, bf16[2,8192,128]{2,1,0:T(8,128)(2,1)}, u32[]{:S(2)}) copy-start(bf16[2,8192,128]{2,1,0:T(8,128)(2,1)} %refs_2_.3) | copy-start | bytes 12582916
  24.1 25.6 %copy-start.5 = (bf16[2,8192,128]{2,1,0:T(8,128)(2,1)S(1)}, bf16[2,8192,128]{2,1,0:T(8,128)(2,1)}, u32[]{:S(2)}) copy-start(bf16[2,8192,128]{2,1,0:T(8,128)(2,1)} %refs_2_.3) | copy-start | bytes 12582916
  27.4 26.9 %collective-permute-start.7 = (bf16[528,128]{1,0:T(8,128)(2,1)S(1)}, bf16[528,128]{1,0:T(8,128)(2,1)S(1)}, u32[]{:S(2)}, u32[]{:S(2)}) collective-permute-start(bf16[528,128]{1,0:T(8,128)(2,1)S(1)} %get-tuple-element.23), channel_id=1, source_target_pairs={{0,28},{4,24},{8,20},{12,16},{16,12},{20,8},{24,4},{28,0},{1,29},{... | collective-permute-start | bytes 405512 | tf_op jit(solution)/shard_map/ppermute | solution.py:382
  30.9 46.2 %collective-permute-start.10 = (bf16[1024,512]{1,0:T(8,128)(2,1)}, bf16[1024,512]{1,0:T(8,128)(2,1)}, u32[]{:S(2)}, u32[]{:S(2)}) collective-permute-start(bf16[1024,512]{1,0:T(8,128)(2,1)} %constant_dynamic-update-slice_fusion.refs_4_), channel_id=1, source_target_pairs={{0,4},{4,0},{8,12},{12,8},{16,20},{20,16},{24,28},{28,24},{1,5},{5... | collective-permute-start | bytes 3145736 | tf_op jit(solution)/shard_map/ppermute | solution.py:382
  45.8 34.8 %collective-permute-start.14 = (bf16[1024,512]{1,0:T(8,128)(2,1)}, bf16[1024,512]{1,0:T(8,128)(2,1)}, u32[]{:S(2)}, u32[]{:S(2)}) collective-permute-start(bf16[1024,512]{1,0:T(8,128)(2,1)} %constant_dynamic-update-slice_fusion.refs_4_), channel_id=1, source_target_pairs={{0,8},{4,12},{8,0},{12,4},{16,24},{20,28},{24,16},{28,20},{1,9},{5... | collective-permute-start | bytes 3145736 | tf_op jit(solution)/shard_map/ppermute | solution.py:382
  53.6 28.3 %collective-permute-start.5 = (bf16[528,128]{1,0:T(8,128)(2,1)}, bf16[528,128]{1,0:T(8,128)(2,1)}, u32[]{:S(2)}, u32[]{:S(2)}) collective-permute-start(bf16[528,128]{1,0:T(8,128)(2,1)} %get-tuple-element.21.refs_3_), channel_id=1, source_target_pairs={{0,20},{4,16},{8,28},{12,24},{16,4},{20,0},{24,12},{28,8},{1,21},{... | collective-permute-start | bytes 405512 | tf_op jit(solution)/shard_map/ppermute | solution.py:382
  57.5 24.4 %collective-permute-start.9 = (bf16[528,128]{1,0:T(8,128)(2,1)S(1)}, bf16[528,128]{1,0:T(8,128)(2,1)S(1)}, u32[]{:S(2)}, u32[]{:S(2)}) collective-permute-start(bf16[528,128]{1,0:T(8,128)(2,1)S(1)} %get-tuple-element.25.refs_0_), channel_id=1, source_target_pairs={{0,28},{4,24},{8,20},{12,16},{16,12},{20,8},{24,4},{28,0},{1,29},{... | collective-permute-start | bytes 405512 | tf_op jit(solution)/shard_map/ppermute | solution.py:382
  60.0 21.9 %collective-permute-start.4 = (bf16[528,128]{1,0:T(8,128)(2,1)S(1)}, bf16[528,128]{1,0:T(8,128)(2,1)S(1)}, u32[]{:S(2)}, u32[]{:S(2)}) collective-permute-start(bf16[528,128]{1,0:T(8,128)(2,1)S(1)} %get-tuple-element.20), channel_id=1, source_target_pairs={{0,16},{4,20},{8,24},{12,28},{16,0},{20,4},{24,8},{28,12},{1,17},{... | collective-permute-start | bytes 405512 | tf_op jit(solution)/shard_map/ppermute | solution.py:382
  62.8 2.2 %copy-start.6 = (bf16[2,8192,128]{2,1,0:T(8,128)(2,1)S(1)}, bf16[2,8192,128]{2,1,0:T(8,128)(2,1)}, u32[]{:S(2)}) copy-start(bf16[2,8192,128]{2,1,0:T(8,128)(2,1)} %refs_2_.3) | copy-start | bytes 12582916
  73.4 16.0 %all-to-all-start.1 = ((bf16[4,528,128]{2,1,0:T(8,128)(2,1)}), bf16[4,528,128]{2,1,0:T(8,128)(2,1)S(1)}, u32[]{:S(2)}, u32[]{:S(2)}) async-start(bf16[4,528,128]{2,1,0:T(8,128)(2,1)} %serve_group.1.refs_1_), calls=%async_computation.1 | async-start | bytes 1081344 | tf_op jit(solution)/shard_map/all_to_all | solution.py:394
  77.1 12.3 %collective-permute-start.8 = (bf16[528,128]{1,0:T(8,128)(2,1)S(1)}, bf16[528,128]{1,0:T(8,128)(2,1)S(1)}, u32[]{:S(2)}, u32[]{:S(2)}) collective-permute-start(bf16[528,128]{1,0:T(8,128)(2,1)S(1)} %get-tuple-element.24), channel_id=1, source_target_pairs={{0,24},{4,28},{8,16},{12,20},{16,8},{20,12},{24,0},{28,4},{1,25},{... | collective-permute-start | bytes 405512 | tf_op jit(solution)/shard_map/ppermute | solution.py:382
  80.6 22.0 %collective-permute-start.16 = (bf16[512,512]{1,0:T(8,128)(2,1)}, bf16[512,512]{1,0:T(8,128)(2,1)}, u32[]{:S(2)}, u32[]{:S(2)}) collective-permute-start(bf16[512,512]{1,0:T(8,128)(2,1)} %gate.5), channel_id=1, source_target_pairs={{0,8},{4,12},{8,0},{12,4},{16,24},{20,28},{24,16},{28,20},{1,9},{5... | collective-permute-start | bytes 1572872 | tf_op jit(solution)/shard_map/ppermute | solution.py:382
  81.9 7.5 %copy-start.3 = (s32[2,1,2]{2,1,0:T(1,128)S(1)}, s32[2,1,2]{2,1,0:T(1,128)}, u32[]{:S(2)}) copy-start(s32[2,1,2]{2,1,0:T(1,128)} %selected_ref.3) | copy-start | bytes 52
  91.5 6.7 %collective-permute-start.12 = (bf16[256,512]{1,0:T(8,128)(2,1)S(1)}, bf16[256,512]{1,0:T(8,128)(2,1)S(1)}, u32[]{:S(2)}, u32[]{:S(2)}) collective-permute-start(bf16[256,512]{1,0:T(8,128)(2,1)S(1)} %combine_pieces.1.refs_0_), channel_id=1, source_target_pairs={{0,2},{1,3},{2,0},{3,1},{4,6},{5,7},{6,4},{7,5},{8,10},{9,11},{10,... | collective-permute-start | bytes 786440 | tf_op jit(solution)/shard_map/ppermute | solution.py:422
  93.9 9.9 %collective-permute-start.15 = (bf16[512,512]{1,0:T(8,128)(2,1)S(1)}, bf16[512,512]{1,0:T(8,128)(2,1)S(1)}, u32[]{:S(2)}, u32[]{:S(2)}) collective-permute-start(bf16[512,512]{1,0:T(8,128)(2,1)S(1)} %gate.4), channel_id=1, source_target_pairs={{0,4},{4,0},{8,12},{12,8},{16,20},{20,16},{24,28},{28,24},{1,5},{5... | collective-permute-start | bytes 1572872 | tf_op jit(solution)/shard_map/ppermute | solution.py:382
  95.6 2.7 %collective-permute-start.11 = (bf16[256,512]{1,0:T(8,128)(2,1)S(1)}, bf16[256,512]{1,0:T(8,128)(2,1)S(1)}, u32[]{:S(2)}, u32[]{:S(2)}) collective-permute-start(bf16[256,512]{1,0:T(8,128)(2,1)S(1)} %combine_pieces.1.refs_0_), channel_id=1, source_target_pairs={{0,1},{1,0},{2,3},{3,2},{4,5},{5,4},{6,7},{7,6},{8,9},{9,8},{10,11... | collective-permute-start | bytes 786440 | tf_op jit(solution)/shard_map/ppermute | solution.py:423
  98.2 1.5 %collective-permute-start.13 = (bf16[256,512]{1,0:T(8,128)(2,1)S(1)}, bf16[256,512]{1,0:T(8,128)(2,1)S(1)}, u32[]{:S(2)}, u32[]{:S(2)}) collective-permute-start(bf16[256,512]{1,0:T(8,128)(2,1)S(1)} %collective-permute-done.12.refs_2_), channel_id=1, source_target_pairs={{0,1},{1,0},{2,3},{3,2},{4,5},{5,4},{6,7},{7,6},{8,9},{9,8},{10,11... | collective-permute-start | bytes 786440 | tf_op jit(solution)/shard_map/ppermute | solution.py:424

commit v5 on v4

--- a/solution.py
+++ b/solution.py
@@ -71,21 +71,25 @@
 
 
 def attend(query, keys, values, first_offset, out_ref):
-    scores = lax.dot_general(
-        query, keys, (((1,), (1,)), ((), ())), preferred_element_type=jnp.float32
-    )
-    if first_offset is not None:
-        offsets = first_offset + lax.rem(
-            lax.broadcasted_iota(jnp.int32, (ROWS, BLK), 0), jnp.int32(TILE)
-        )
-        seen = lax.broadcasted_iota(jnp.int32, (ROWS, BLK), 1) <= offsets
-        scores = jnp.where(seen, scores, -jnp.inf)
-    top = jnp.max(scores, axis=1, keepdims=True)
-    weights = jnp.exp2((scores - top) * (SCALE * LOG2E))
-    total = jnp.sum(weights, axis=1, keepdims=True)
-    summed = jnp.dot(weights.astype(jnp.bfloat16), values, preferred_element_type=jnp.float32)
-    out_ref[0:ROWS, :] = (summed / total).astype(jnp.bfloat16)
-    level = top * SCALE + jnp.log(total)
+    levels = []
+    step = ROWS // 2
+    for base in range(0, ROWS, step):
+        scores = lax.dot_general(
+            query[base : base + step], keys, (((1,), (1,)), ((), ())), preferred_element_type=jnp.float32
+        )
+        if first_offset is not None:
+            offsets = first_offset + lax.rem(
+                lax.broadcasted_iota(jnp.int32, (step, BLK), 0), jnp.int32(TILE)
+            )
+            seen = lax.broadcasted_iota(jnp.int32, (step, BLK), 1) <= offsets
+            scores = jnp.where(seen, scores, -jnp.inf)
+        top = jnp.max(scores, axis=1, keepdims=True)
+        weights = jnp.exp2((scores - top) * (SCALE * LOG2E))
+        total = jnp.sum(weights, axis=1, keepdims=True)
+        summed = jnp.dot(weights.astype(jnp.bfloat16), values, preferred_element_type=jnp.float32)
+        out_ref[base : base + step, :] = (summed / total).astype(jnp.bfloat16)
+        levels.append(top * SCALE + jnp.log(total))
+    level = jnp.concatenate(levels, axis=0)
     lane = lax.rem(lax.broadcasted_iota(jnp.int32, (TILE, TILE), 1), jnp.int32(GROUP))
     spread = jnp.zeros((TILE, TILE), jnp.float32)
     for head in range(GROUP):
@@ -282,62 +286,71 @@
     )(me, selected, own, near, *far, *after)
 
 
-def project_kernel(heads, me_ref, *refs):
-    attentions = refs[:heads]
-    stack, stack_z, stack_x, whole_ref, share_ref, rest_ref = refs[heads:]
-    depth = attentions[0].shape[1]
-    z, h = me_ref[0], me_ref[2]
-    lefts = []
-    for index in range(heads):
-        place = (z ^ index) ^ h
-        left = attentions[0][...]
-        for other in range(1, heads):
-            left = jnp.where(place == other, attentions[other][...], left)
-        lefts.append(left)
-    near, rest = jnp.concatenate(lefts[0::2], axis=1), jnp.concatenate(lefts[1::2], axis=1)
-    rest_ref[...] = rest
-    share_ref[...] = jnp.dot(near, stack_x[...], preferred_element_type=jnp.float32)
-    whole_ref[...] = (
-        jnp.dot(near, stack[...], preferred_element_type=jnp.float32)
-        + jnp.dot(rest, stack_z[...], preferred_element_type=jnp.float32)
-    ).astype(jnp.bfloat16)
-
-
-def finish_kernel(me_ref, rest_ref, first_ref, second_ref, share_ref, whole_ref, out_ref):
+def halves(numbers_ref, first, second):
+    even = ((numbers_ref[0] ^ numbers_ref[2]) & 1) == 0
+    return jnp.where(even, first, second), jnp.where(even, second, first)
+
+
+def project_kernel(numbers_ref, own_ref, core_ref, stack, stack_z, stack_x, whole_ref, share_ref):
+    depth = own_ref.shape[1]
+    part = lax.shift_right_logical(numbers_ref[0] ^ numbers_ref[2], 1)
+    rows = pl.ds(pl.multiple_of(part * depth, depth), depth)
+    even, odd = halves(numbers_ref, own_ref[...], core_ref[...])
+    whole_ref[...] = jnp.dot(even, stack[rows, :], preferred_element_type=jnp.float32) + jnp.dot(
+        odd, stack_z[rows, :], preferred_element_type=jnp.float32
+    )
+    share_ref[...] = jnp.dot(even, stack_x[rows, :], preferred_element_type=jnp.float32)
+
+
+def finish_kernel(numbers_ref, own_ref, core_ref, y_ref, both_ref, *refs):
+    stack, stack_z, stack_x, first_ref, second_ref, whole_ref, share_ref, out_ref = refs
     depth, width = first_ref.shape
-    x = me_ref[1]
-    total = (
+    x = numbers_ref[1]
+    part = lax.shift_right_logical(numbers_ref[0] ^ numbers_ref[2], 1)
+    rows = pl.ds(pl.multiple_of((1 - part) * depth, depth), depth)
+    _, near_odd = halves(numbers_ref, own_ref[...], core_ref[...])
+    even, odd = halves(numbers_ref, y_ref[...], both_ref[...])
+    whole = (
+        whole_ref[...]
+        + jnp.dot(even, stack[rows, :], preferred_element_type=jnp.float32)
+        + jnp.dot(odd, stack_z[rows, :], preferred_element_type=jnp.float32)
+    )
+    share = (
         share_ref[...]
-        + jnp.dot(rest_ref[:, :depth], first_ref[...], preferred_element_type=jnp.float32)
-        + jnp.dot(rest_ref[:, depth:], second_ref[...], preferred_element_type=jnp.float32)
-    )
-    out_ref[:, pl.ds(pl.multiple_of(x * width, width), width)] = whole_ref[...]
-    out_ref[:, pl.ds(pl.multiple_of((x ^ 1) * width, width), width)] = total.astype(jnp.bfloat16)
+        + jnp.dot(even, stack_x[rows, :], preferred_element_type=jnp.float32)
+        + jnp.dot(
+            jnp.where(part == 0, near_odd, odd), first_ref[...], preferred_element_type=jnp.float32
+        )
+        + jnp.dot(
+            jnp.where(part == 0, odd, near_odd), second_ref[...], preferred_element_type=jnp.float32
+        )
+    )
+    out_ref[:, pl.ds(pl.multiple_of(x * width, width), width)] = whole.astype(jnp.bfloat16)
+    out_ref[:, pl.ds(pl.multiple_of((x ^ 1) * width, width), width)] = share.astype(jnp.bfloat16)
 
 
 def project(numbers, attentions, stacks):
     rows, width = attentions[0].shape[0], stacks[0].shape[1]
-    heads = len(attentions)
-    whole, share, rest = pl.pallas_call(
-        functools.partial(project_kernel, heads),
-        out_shape=[
-            jax.ShapeDtypeStruct((rows, width), jnp.bfloat16),
-            jax.ShapeDtypeStruct((rows, width), jnp.float32),
-            jax.ShapeDtypeStruct((rows, 2 * stacks[3].shape[0]), jnp.bfloat16),
-        ],
-        in_specs=[smem] + [vmem] * (heads + 3),
-        out_specs=[vmem] * 3,
+    return pl.pallas_call(
+        project_kernel,
+        out_shape=[jax.ShapeDtypeStruct((rows, width), jnp.float32)] * 2,
+        in_specs=[smem] + [vmem] * 5,
+        out_specs=[vmem] * 2,
         compiler_params=params(),
         name="project",
-    )(numbers, *attentions, *stacks[:3])
+    )(numbers, *attentions, *stacks)
+
+
+def finish(numbers, attentions, stacks, whole, share):
+    rows, width = attentions[0].shape[0], stacks[0].shape[1]
     return pl.pallas_call(
         finish_kernel,
         out_shape=jax.ShapeDtypeStruct((rows, 2 * width), jnp.bfloat16),
-        in_specs=[smem] + [vmem] * 5,
+        in_specs=[smem] + [vmem] * 11,
         out_specs=vmem,
         compiler_params=params(),
         name="finish",
-    )(numbers, rest, stacks[3], stacks[4], share, whole)
+    )(numbers, *attentions, *stacks, whole, share)
 
 
 def gate_kernel(*refs):
@@ -421,11 +434,13 @@
     if fast:
         other_y = lax.ppermute(attention, "kvh", pairs(kvh_count, 2))
         other_core = lax.ppermute(attention, "kvh", pairs(kvh_count, 1))
+        numbers = jnp.stack([lax.shift_right_logical(seq, 1), seq & 1, kvh]).astype(jnp.int32)
+        stacks = [stack, stack_z, stack_x]
+        whole, share = project(numbers, [attention, other_core], stacks)
+        other_y = gate(other_y, whole, first_zx, second_zx)
         both = lax.ppermute(other_y, "kvh", pairs(kvh_count, 1))
-        gathered = [attention, other_core, other_y, both]
-        stacks = [stack, stack_z, stack_x, first_zx, second_zx]
-        numbers = jnp.stack([lax.shift_right_logical(seq, 1), seq & 1, kvh]).astype(jnp.int32)
-        return project(numbers, gathered, stacks)
+        attentions = [attention, other_core, other_y, both]
+        return finish(numbers, attentions, [*stacks, first_zx, second_zx], whole, share)
     column_terms = jnp.dot(
         attention,
         lax.all_gather(out_weight, "seq", axis=1, tiled=True),

time: 107 us -> 106 us (level)
  starting transfers between devices: 35.9 us -> 47.5 us
  waiting for transfers between devices: 30.8 us -> 19.7 us
    ppermute x12, starting transfers between devices: 18.4 us -> 31.8 us  [move(): return lax.ppermute(array, 'seq', pairs(seq_count, offset))]
    ppermute x12, waiting for transfers between devices: 19.2 us -> 8.95 us  [move(): return lax.ppermute(array, 'seq', pairs(seq_count, offset))]
    all_to_all x2, waiting for transfers between devices: 7.5 us -> 3.61 us  [swap(): lax.all_to_all(array, 'seq', split_axis=0, concat_axis=0, axis_index_grou...]
    ppermute x1, starting transfers between devices: 2.35 us -> 0.2 us  [per_device(): other_y = lax.ppermute(attention, 'kvh', pairs(kvh_count, 2))]
    ppermute x1, waiting for transfers between devices: 2.59 us -> 4.68 us  [per_device(): other_y = lax.ppermute(attention, 'kvh', pairs(kvh_count, 2))]
    ppermute x2, starting transfers between devices: 7.28 us -> 5.72 us  [jump(): return lax.ppermute(weight, ('seq', 'kvh'), moves)]
    unnamed x15 -> x19, local copies, waits for them, and re-layouts: 7.8 us -> 7.81 us
  transfers between devices with their start and end apart: 19 -> 19, of which waited for: 7 -> 8; matrix products, arithmetic and copies ran while one was open for 4% -> 4% of each run, Pallas kernels for 24% -> 22%
where the time goes in v5:
time: 106 us; the launch traced here: 105 us
  starting transfers between devices  47.5 us (45%)
  Pallas kernels  27.1 us (26%)
  waiting for transfers between devices  19.7 us (19%)
  local copies, waits for them, and re-layouts  10.8 us (10%)
    ppermute x12, starting transfers between devices, move(): return lax.ppermute(array, 'seq', pairs(seq_count, offset))  31.8 us
    ppermute x12, waiting for transfers between devices, move(): return lax.ppermute(array, 'seq', pairs(seq_count, offset))  8.95 us
    all_to_all x2, starting transfers between devices, swap(): lax.all_to_all(array, 'seq', split_axis=0, concat_axis=0, axis_index_grou...  8.66 us
    unnamed x19, local copies, waits for them, and re-layouts  7.81 us
    pallas_call x1, Pallas kernels, serve_group(): pl.pallas_call(serve_group_kernel, out_shape=jax.ShapeDtypeStruct((NEAR,...  7.43 us
    pallas_call x2, Pallas kernels, serve(): pl.pallas_call(functools.partial(serve_kernel, count), out_shape=[jax.Sha...  6.93 us
    ppermute x2, starting transfers between devices, jump(): return lax.ppermute(weight, ('seq', 'kvh'), moves)  5.72 us
    ppermute x1, waiting for transfers between devices, per_device(): other_y = lax.ppermute(attention, 'kvh', pairs(kvh_count, 2))  4.68 us
  transfers between devices with their start and end apart: 19, of which 8 were waited for; matrix products, arithmetic and copies ran while one was open for 4% of the time, Pallas kernels for 22%

profile of v5, /device:TPU:0, one launch (start us, length us, event | category | flops | bytes accessed | tf_op | source)
XLA Modules:
  0.0 105.4 jit_solution(9836533071170911682)
XLA Ops:
  0.0 4.0 %collective-permute-start.3 = (bf16[512,512]{1,0:T(8,128)(2,1)}, bf16[512,512]{1,0:T(8,128)(2,1)S(1)}, u32[]{:S(2)}, u32[]{:S(2)}) collective-permute-start(bf16[512,512]{1,0:T(8,128)(2,1)} %param.7), channel_id=1, source_target_pairs={{0,16},{1,24},{2,0},{3,8},{4,20},{5,28},{6,4},{7,12},{8,17},{9,25}... | collective-permute-start | bytes 1572872 | tf_op jit(solution)/shard_map/ppermute | solution.py:383
  4.0 1.7 %collective-permute-start.2 = (bf16[512,512]{1,0:T(8,128)(2,1)}, bf16[512,512]{1,0:T(8,128)(2,1)S(1)}, u32[]{:S(2)}, u32[]{:S(2)}) collective-permute-start(bf16[512,512]{1,0:T(8,128)(2,1)} %param.7), channel_id=1, source_target_pairs={{0,0},{1,8},{2,16},{3,24},{4,4},{5,12},{6,20},{7,28},{8,1},{9,9},{... | collective-permute-start | bytes 1572872 | tf_op jit(solution)/shard_map/ppermute | solution.py:383
  5.7 0.0 copy-start
  5.7 0.9 copy-done
  6.7 0.7 copy-done.2
  7.4 1.6 %pack_queries.1 = (bf16[4,528,128]{2,1,0:T(8,128)(2,1)}, bf16[528,128]{1,0:T(8,128)(2,1)S(1)}, bf16[528,128]{1,0:T(8,128)(2,1)S(1)}, bf16[528,128]{1,0:T(8,128)(2,1)S(1)}, bf16[528,128]{1,0:T(8,128)(2,1)S(1)}) custom-call(s32[1]{0:T(128)} %bitcast.3.me_ref, s32[2,1,2]{2,1,0:T(1,128)S(1)} %copy-done.2, bf16[256,512]{1,0:T(8,128)(2,1)S(1)} %copy-done), custom_call_target="tpu_custom_call" | custom-call | tf_op jit(solution)/shard_map/pack_queries/pallas_call | solution.py:62
  9.0 5.2 %all-to-all-start = ((bf16[4,528,128]{2,1,0:T(8,128)(2,1)}), bf16[4,528,128]{2,1,0:T(8,128)(2,1)}, u32[]{:S(2)}, u32[]{:S(2)}) async-start(bf16[4,528,128]{2,1,0:T(8,128)(2,1)} %get-tuple-element.16.refs_0_), calls=%async_computation | async-start | bytes 1081344 | tf_op jit(solution)/shard_map/all_to_all | solution.py:407
  14.1 1.2 %collective-permute-start = (bf16[528,128]{1,0:T(8,128)(2,1)S(1)}, bf16[528,128]{1,0:T(8,128)(2,1)S(1)}, u32[]{:S(2)}, u32[]{:S(2)}) collective-permute-start(bf16[528,128]{1,0:T(8,128)(2,1)S(1)} %get-tuple-element.17), channel_id=1, source_target_pairs={{0,16},{4,20},{8,24},{12,28},{16,0},{20,4},{24,8},{28,12},{1,17},{... | collective-permute-start | bytes 405512 | tf_op jit(solution)/shard_map/ppermute | solution.py:395
  15.4 3.1 %collective-permute-start.1 = (bf16[528,128]{1,0:T(8,128)(2,1)S(1)}, bf16[528,128]{1,0:T(8,128)(2,1)S(1)}, u32[]{:S(2)}, u32[]{:S(2)}) collective-permute-start(bf16[528,128]{1,0:T(8,128)(2,1)S(1)} %get-tuple-element.18), channel_id=1, source_target_pairs={{0,20},{4,16},{8,28},{12,24},{16,4},{20,0},{24,12},{28,8},{1,21},{... | collective-permute-start | bytes 405512 | tf_op jit(solution)/shard_map/ppermute | solution.py:395
  18.5 2.2 %collective-permute-start.6 = (bf16[528,128]{1,0:T(8,128)(2,1)S(1)}, bf16[528,128]{1,0:T(8,128)(2,1)S(1)}, u32[]{:S(2)}, u32[]{:S(2)}) collective-permute-start(bf16[528,128]{1,0:T(8,128)(2,1)S(1)} %get-tuple-element.21), channel_id=1, source_target_pairs={{0,24},{4,28},{8,16},{12,20},{16,8},{20,12},{24,0},{28,4},{1,25},{... | collective-permute-start | bytes 405512 | tf_op jit(solution)/shard_map/ppermute | solution.py:395
  20.7 0.9 copy-done.1
  21.6 2.2 %copy-done.4 = bf16[2,8192,128]{2,1,0:T(8,128)(2,1)S(1)} copy-done((bf16[2,8192,128]{2,1,0:T(8,128)(2,1)S(1)}, bf16[2,8192,128]{2,1,0:T(8,128)(2,1)}, u32[]{:S(2)}) %copy-start.4) | copy-done | bytes 4194328
  23.8 2.7 %own_pieces.1.refs_0_.refs_3_.own_ref = bf16[2,528,128]{2,1,0:T(8,128)(2,1)S(1)} custom-call(bf16[256,512]{1,0:T(8,128)(2,1)S(1)} %copy-done.1, bf16[2,8192,128]{2,1,0:T(8,128)(2,1)S(1)} %copy-done.4, bf16[4,528,128]{2,1,0:T(8,128)(2,1)} %get-tuple-element.16.refs_0_), custom_call_target="tpu_custom_call" | custom-call | flops 68719476736 | bytes 1073741824 | tf_op jit(solution)/shard_map/own_pieces/pallas_call | solution.py:132
  26.6 0.0 copy-start.7
  26.6 0.0 collective-permute-done.2
  26.6 2.7 %collective-permute-start.7 = (bf16[528,128]{1,0:T(8,128)(2,1)S(1)}, bf16[528,128]{1,0:T(8,128)(2,1)S(1)}, u32[]{:S(2)}, u32[]{:S(2)}) collective-permute-start(bf16[528,128]{1,0:T(8,128)(2,1)S(1)} %get-tuple-element.22), channel_id=1, source_target_pairs={{0,28},{4,24},{8,20},{12,16},{16,12},{20,8},{24,4},{28,0},{1,29},{... | collective-permute-start | bytes 405512 | tf_op jit(solution)/shard_map/ppermute | solution.py:395
  29.3 0.8 constant_dynamic-update-slice_fusion.1
  30.2 0.0 collective-permute-done.3
  30.2 0.8 constant_dynamic-update-slice_fusion.refs_4_.stack.refs_0_
  31.0 13.6 %collective-permute-start.13 = (bf16[1024,512]{1,0:T(8,128)(2,1)}, bf16[1024,512]{1,0:T(8,128)(2,1)}, u32[]{:S(2)}, u32[]{:S(2)}) collective-permute-start(bf16[1024,512]{1,0:T(8,128)(2,1)} %constant_dynamic-update-slice_fusion.refs_4_.stack.refs_0_), channel_id=1, source_target_pairs={{0,8},{4,12},{8,0},{12,4},{16,24},{20,28},{24,16},{28,20},{1,9},{5... | collective-permute-start | bytes 3145736 | tf_op jit(solution)/shard_map/ppermute | solution.py:395
  44.6 0.0 collective-permute-done.refs_0_
  44.6 1.6 %collective-permute-start.10 = (bf16[1024,512]{1,0:T(8,128)(2,1)}, bf16[1024,512]{1,0:T(8,128)(2,1)}, u32[]{:S(2)}, u32[]{:S(2)}) collective-permute-start(bf16[1024,512]{1,0:T(8,128)(2,1)} %constant_dynamic-update-slice_fusion.refs_4_.stack.refs_0_), channel_id=1, source_target_pairs={{0,4},{4,0},{8,12},{12,8},{16,20},{20,16},{24,28},{28,24},{1,5},{5... | collective-permute-start | bytes 3145736 | tf_op jit(solution)/shard_map/ppermute | solution.py:395
  46.2 4.0 %collective-permute-done.1.refs_1_ = bf16[528,128]{1,0:T(8,128)(2,1)S(1)} collective-permute-done((bf16[528,128]{1,0:T(8,128)(2,1)S(1)}, bf16[528,128]{1,0:T(8,128)(2,1)S(1)}, u32[]{:S(2)}, u32[]{:S(2)}) %collective-permute-start.1) | collective-permute-done | bytes 135200 | tf_op jit(solution)/shard_map/ppermute | solution.py:395
  50.2 0.0 copy-done.5
  50.2 3.5 %serve_slots.2 = (bf16[528,128]{1,0:T(8,128)(2,1)S(1)}, bf16[528,128]{1,0:T(8,128)(2,1)}) custom-call(bf16[528,128]{1,0:T(8,128)(2,1)S(1)} %collective-permute-done.refs_0_, bf16[528,128]{1,0:T(8,128)(2,1)S(1)} %collective-permute-done.1.refs_1_, bf16[2,8192,128]{2,1,0:T(8,128)(2,1)S(1)} %copy-done.5, ...), custom_call_target="tpu_custom_call" | custom-call | flops 68719476736 | bytes 1073741824 | tf_op jit(solution)/shard_map/serve_slots/pallas_call | solution.py:169
  53.7 0.1 collective-permute-start.5
  53.8 0.0 collective-permute-done.6.refs_0_
  53.8 0.0 collective-permute-done.7.refs_1_
  53.8 3.4 %serve_slots.3 = (bf16[528,128]{1,0:T(8,128)(2,1)}, bf16[528,128]{1,0:T(8,128)(2,1)}) custom-call(bf16[528,128]{1,0:T(8,128)(2,1)S(1)} %collective-permute-done.6.refs_0_, bf16[528,128]{1,0:T(8,128)(2,1)S(1)} %collective-permute-done.7.refs_1_, bf16[2,8192,128]{2,1,0:T(8,128)(2,1)S(1)} %copy-done.5, bf16[528,128]{1,0:T(8,128)(2,1)} %get-tuple-element.20.refs_3_), custom_call_target="tpu_custom_call" | custom-call | flops 68719476736 | bytes 1073741824 | tf_op jit(solution)/shard_map/serve_slots/pallas_call | solution.py:169
  57.2 0.1 collective-permute-start.8
  57.3 3.5 %collective-permute-start.9 = (bf16[528,128]{1,0:T(8,128)(2,1)}, bf16[528,128]{1,0:T(8,128)(2,1)}, u32[]{:S(2)}, u32[]{:S(2)}) collective-permute-start(bf16[528,128]{1,0:T(8,128)(2,1)} %get-tuple-element.24.refs_0_), channel_id=1, source_target_pairs={{0,28},{4,24},{8,20},{12,16},{16,12},{20,8},{24,4},{28,0},{1,29},{... | collective-permute-start | bytes 405512 | tf_op jit(solution)/shard_map/ppermute | solution.py:395
  60.8 0.0 all-to-all-done.slots_ref
  60.8 0.0 copy-done.7
  60.8 2.2 %copy-done.6 = bf16[2,8192,128]{2,1,0:T(8,128)(2,1)S(1)} copy-done((bf16[2,8192,128]{2,1,0:T(8,128)(2,1)S(1)}, bf16[2,8192,128]{2,1,0:T(8,128)(2,1)}, u32[]{:S(2)}) %copy-start.6) | copy-done | bytes 4194328
  63.0 7.4 %serve_group.1.refs_1_ = bf16[4,528,128]{2,1,0:T(8,128)(2,1)} custom-call(bf16[4,528,128]{2,1,0:T(8,128)(2,1)} %all-to-all-done.slots_ref, bf16[2,8192,128]{2,1,0:T(8,128)(2,1)S(1)} %copy-done.6, bf16[2,528,128]{2,1,0:T(8,128)(2,1)S(1)} %own_pieces.1.refs_0_.refs_3_.own_ref), custom_call_target="tpu_custom_call" | custom-call | flops 68719476736 | bytes 1073741824 | tf_op jit(solution)/shard_map/serve_group/pallas_call | solution.py:204
  70.4 3.5 %all-to-all-start.1 = ((bf16[4,528,128]{2,1,0:T(8,128)(2,1)}), bf16[4,528,128]{2,1,0:T(8,128)(2,1)S(1)}, u32[]{:S(2)}, u32[]{:S(2)}) async-start(bf16[4,528,128]{2,1,0:T(8,128)(2,1)} %serve_group.1.refs_1_), calls=%async_computation.1 | async-start | bytes 1081344 | tf_op jit(solution)/shard_map/all_to_all | solution.py:407
  73.9 2.6 %collective-permute-done.10.refs_4_.stack_x.refs_2_ = bf16[1024,512]{1,0:T(8,128)(2,1)} collective-permute-done((bf16[1024,512]{1,0:T(8,128)(2,1)}, bf16[1024,512]{1,0:T(8,128)(2,1)}, u32[]{:S(2)}, u32[]{:S(2)}) %collective-permute-start.10) | collective-permute-done | bytes 1048608 | tf_op jit(solution)/shard_map/ppermute | solution.py:395
  76.5 0.3 collective-permute-start.4
  76.8 1.1 %slice.9.refs_0_ = bf16[512,512]{1,0:T(8,128)(2,1)S(1)} slice(bf16[1024,512]{1,0:T(8,128)(2,1)} %collective-permute-done.10.refs_4_.stack_x.refs_2_), slice={[512:1024], [0:512]} | slice | bytes 1048576 | tf_op jit(solution)/shard_map/slice | solution.py:430
  77.9 2.0 %collective-permute-done.13.stack_z.refs_1_ = bf16[1024,512]{1,0:T(8,128)(2,1)} collective-permute-done((bf16[1024,512]{1,0:T(8,128)(2,1)}, bf16[1024,512]{1,0:T(8,128)(2,1)}, u32[]{:S(2)}, u32[]{:S(2)}) %collective-permute-start.13) | collective-permute-done | bytes 1048608 | tf_op jit(solution)/shard_map/ppermute | solution.py:395
  79.8 1.1 %slice.8.refs_0_ = bf16[512,512]{1,0:T(8,128)(2,1)S(1)} slice(bf16[1024,512]{1,0:T(8,128)(2,1)} %collective-permute-done.13.stack_z.refs_1_), slice={[0:512], [0:512]} | slice | bytes 1048576 | tf_op jit(solution)/shard_map/slice | solution.py:429
  80.9 0.0 copy-start.3
  80.9 0.0 copy-start.8
  81.0 3.5 %collective-permute-start.14 = (bf16[512,512]{1,0:T(8,128)(2,1)S(1)}, bf16[512,512]{1,0:T(8,128)(2,1)S(1)}, u32[]{:S(2)}, u32[]{:S(2)}) collective-permute-start(bf16[512,512]{1,0:T(8,128)(2,1)S(1)} %gate.5), channel_id=1, source_target_pairs={{0,4},{4,0},{8,12},{12,8},{16,20},{20,16},{24,28},{28,24},{1,5},{5... | collective-permute-start | bytes 1572872 | tf_op jit(solution)/shard_map/ppermute | solution.py:395
  84.4 0.0 collective-permute-done.9.refs_3_
  84.4 0.0 collective-permute-start.15
  84.4 0.4 collective-permute-done.4.refs_2_.refs_0_
  84.8 0.0 collective-permute-done.5.refs_3_.refs_1_
  84.8 3.6 %all-to-all-done.1.refs_1_.near_ref = bf16[4,528,128]{2,1,0:T(8,128)(2,1)S(1)} async-done(((bf16[4,528,128]{2,1,0:T(8,128)(2,1)}), bf16[4,528,128]{2,1,0:T(8,128)(2,1)S(1)}, u32[]{:S(2)}, u32[]{:S(2)}) %all-to-all-start.1) | async-done | bytes 540704 | tf_op jit(solution)/shard_map/all_to_all | solution.py:407
  88.4 0.0 collective-permute-done.8.refs_2_
  88.4 0.0 copy-done.3
  88.4 0.0 copy-done.8
  88.4 2.5 %combine_pieces.1.own_ref = bf16[256,512]{1,0:T(8,128)(2,1)S(1)} custom-call(s32[1]{0:T(128)} %bitcast.3.me_ref, s32[2,1,2]{2,1,0:T(1,128)S(1)} %copy-done.3, bf16[2,528,128]{2,1,0:T(8,128)(2,1)S(1)} %copy-done.8, bf16[4,528,128]{2,1,0:T(8,128)(2,1)S(1)} %all-to-all-done.1.refs_1_.near_ref, bf16[528,128]{1,0:T(8,128)(2,1)S(1)} %collective-permute-done.4.refs_2_.refs_0_, ...), custom_call_target="tpu_custom_call" | custom-call | flops 68719476736 | bytes 1073741824 | tf_op jit(solution)/shard_map/combine_pieces/pallas_call | solution.py:277
  90.9 1.0 collective-permute-start.11
  91.9 0.2 collective-permute-start.12
  92.2 0.1 pad_add_fusion.numbers_ref
  92.2 0.9 collective-permute-done.11.core_ref
  93.1 2.4 %project.1 = (f32[256,512]{1,0:T(8,128)S(1)}, f32[256,512]{1,0:T(8,128)S(1)}) custom-call(s32[3]{0:T(128)S(1)} %pad_add_fusion.numbers_ref, bf16[256,512]{1,0:T(8,128)(2,1)S(1)} %combine_pieces.1.own_ref, bf16[256,512]{1,0:T(8,128)(2,1)S(1)} %collective-permute-done.11.core_ref, bf16[1024,512]{1,0:T(8,128)(2,1)} %constant_dynamic-update-slice_fusion.refs_4_.stack.refs_0_, ...), custom_call_target="tpu_custom_call" | custom-call | tf_op jit(solution)/shard_map/project/pallas_call | solution.py:334
  95.6 4.7 %collective-permute-done.12.refs_0_ = bf16[256,512]{1,0:T(8,128)(2,1)S(1)} collective-permute-done((bf16[256,512]{1,0:T(8,128)(2,1)S(1)}, bf16[256,512]{1,0:T(8,128)(2,1)S(1)}, u32[]{:S(2)}, u32[]{:S(2)}) %collective-permute-start.12) | collective-permute-done | bytes 262176 | tf_op jit(solution)/shard_map/ppermute | solution.py:435
  100.2 0.0 collective-permute-done.14.refs_2_.refs_3_
  100.2 0.0 collective-permute-done.15.refs_3_.refs_4_
  100.2 0.1 collective-permute-start.16
  100.3 1.5 %collective-permute-done.16.both_ref = bf16[256,512]{1,0:T(8,128)(2,1)S(1)} collective-permute-done((bf16[256,512]{1,0:T(8,128)(2,1)S(1)}, bf16[256,512]{1,0:T(8,128)(2,1)S(1)}, u32[]{:S(2)}, u32[]{:S(2)}) %collective-permute-start.16) | collective-permute-done | bytes 262176 | tf_op jit(solution)/shard_map/ppermute | solution.py:441
  101.8 3.5 %finish.1 = bf16[256,1024]{1,0:T(8,128)(2,1)} custom-call(s32[3]{0:T(128)S(1)} %pad_add_fusion.numbers_ref, bf16[256,512]{1,0:T(8,128)(2,1)S(1)} %combine_pieces.1.own_ref, bf16[256,512]{1,0:T(8,128)(2,1)S(1)} %collective-permute-done.11.core_ref, bf16[256,512]{1,0:T(8,128)(2,1)S(1)} %gate.7.y_ref, bf16[256,512]{1,0:T(8,128)(2,1)S(1)} %collective-permute-done.16.both_ref, ...), custom_call_target="tpu_custom_call" | custom-call | tf_op jit(solution)/shard_map/finish/pallas_call | solution.py:346
  (9 shorter events, 0.0 us)
Async XLA Ops:
  0.0 30.2 %collective-permute-start.3 = (bf16[512,512]{1,0:T(8,128)(2,1)}, bf16[512,512]{1,0:T(8,128)(2,1)S(1)}, u32[]{:S(2)}, u32[]{:S(2)}) collective-permute-start(bf16[512,512]{1,0:T(8,128)(2,1)} %param.7), channel_id=1, source_target_pairs={{0,16},{1,24},{2,0},{3,8},{4,20},{5,28},{6,4},{7,12},{8,17},{9,25}... | collective-permute-start | bytes 1572872 | tf_op jit(solution)/shard_map/ppermute | solution.py:383
  4.0 22.5 %collective-permute-start.2 = (bf16[512,512]{1,0:T(8,128)(2,1)}, bf16[512,512]{1,0:T(8,128)(2,1)S(1)}, u32[]{:S(2)}, u32[]{:S(2)}) collective-permute-start(bf16[512,512]{1,0:T(8,128)(2,1)} %param.7), channel_id=1, source_target_pairs={{0,0},{1,8},{2,16},{3,24},{4,4},{5,12},{6,20},{7,28},{8,1},{9,9},{... | collective-permute-start | bytes 1572872 | tf_op jit(solution)/shard_map/ppermute | solution.py:383
  5.7 0.9 copy-start
  6.7 0.7 copy-start.2
  9.0 51.8 %all-to-all-start = ((bf16[4,528,128]{2,1,0:T(8,128)(2,1)}), bf16[4,528,128]{2,1,0:T(8,128)(2,1)}, u32[]{:S(2)}, u32[]{:S(2)}) async-start(bf16[4,528,128]{2,1,0:T(8,128)(2,1)} %get-tuple-element.16.refs_0_), calls=%async_computation | async-start | bytes 1081344 | tf_op jit(solution)/shard_map/all_to_all | solution.py:407
  14.1 30.5 %collective-permute-start = (bf16[528,128]{1,0:T(8,128)(2,1)S(1)}, bf16[528,128]{1,0:T(8,128)(2,1)S(1)}, u32[]{:S(2)}, u32[]{:S(2)}) collective-permute-start(bf16[528,128]{1,0:T(8,128)(2,1)S(1)} %get-tuple-element.17), channel_id=1, source_target_pairs={{0,16},{4,20},{8,24},{12,28},{16,0},{20,4},{24,8},{28,12},{1,17},{... | collective-permute-start | bytes 405512 | tf_op jit(solution)/shard_map/ppermute | solution.py:395
  15.4 34.8 %collective-permute-start.1 = (bf16[528,128]{1,0:T(8,128)(2,1)S(1)}, bf16[528,128]{1,0:T(8,128)(2,1)S(1)}, u32[]{:S(2)}, u32[]{:S(2)}) collective-permute-start(bf16[528,128]{1,0:T(8,128)(2,1)S(1)} %get-tuple-element.18), channel_id=1, source_target_pairs={{0,20},{4,16},{8,28},{12,24},{16,4},{20,0},{24,12},{28,8},{1,21},{... | collective-permute-start | bytes 405512 | tf_op jit(solution)/shard_map/ppermute | solution.py:395
  18.5 35.2 %collective-permute-start.6 = (bf16[528,128]{1,0:T(8,128)(2,1)S(1)}, bf16[528,128]{1,0:T(8,128)(2,1)S(1)}, u32[]{:S(2)}, u32[]{:S(2)}) collective-permute-start(bf16[528,128]{1,0:T(8,128)(2,1)S(1)} %get-tuple-element.21), channel_id=1, source_target_pairs={{0,24},{4,28},{8,16},{12,20},{16,8},{20,12},{24,0},{28,4},{1,25},{... | collective-permute-start | bytes 405512 | tf_op jit(solution)/shard_map/ppermute | solution.py:395
  20.7 0.9 copy-start.1
  21.6 2.2 %copy-start.4 = (bf16[2,8192,128]{2,1,0:T(8,128)(2,1)S(1)}, bf16[2,8192,128]{2,1,0:T(8,128)(2,1)}, u32[]{:S(2)}) copy-start(bf16[2,8192,128]{2,1,0:T(8,128)(2,1)} %refs_2_.3) | copy-start | bytes 12582916
  23.8 26.4 %copy-start.5 = (bf16[2,8192,128]{2,1,0:T(8,128)(2,1)S(1)}, bf16[2,8192,128]{2,1,0:T(8,128)(2,1)}, u32[]{:S(2)}) copy-start(bf16[2,8192,128]{2,1,0:T(8,128)(2,1)} %refs_2_.3) | copy-start | bytes 12582916
  26.6 34.2 %copy-start.7 = (bf16[2,528,128]{2,1,0:T(8,128)(2,1)}, bf16[2,528,128]{2,1,0:T(8,128)(2,1)S(1)}, u32[]{:S(2)}) copy-start(bf16[2,528,128]{2,1,0:T(8,128)(2,1)S(1)} %own_pieces.1.refs_0_.refs_3_.own_ref) | copy-start | bytes 811012
  26.6 27.2 %collective-permute-start.7 = (bf16[528,128]{1,0:T(8,128)(2,1)S(1)}, bf16[528,128]{1,0:T(8,128)(2,1)S(1)}, u32[]{:S(2)}, u32[]{:S(2)}) collective-permute-start(bf16[528,128]{1,0:T(8,128)(2,1)S(1)} %get-tuple-element.22), channel_id=1, source_target_pairs={{0,28},{4,24},{8,20},{12,16},{16,12},{20,8},{24,4},{28,0},{1,29},{... | collective-permute-start | bytes 405512 | tf_op jit(solution)/shard_map/ppermute | solution.py:395
  31.0 48.8 %collective-permute-start.13 = (bf16[1024,512]{1,0:T(8,128)(2,1)}, bf16[1024,512]{1,0:T(8,128)(2,1)}, u32[]{:S(2)}, u32[]{:S(2)}) collective-permute-start(bf16[1024,512]{1,0:T(8,128)(2,1)} %constant_dynamic-update-slice_fusion.refs_4_.stack.refs_0_), channel_id=1, source_target_pairs={{0,8},{4,12},{8,0},{12,4},{16,24},{20,28},{24,16},{28,20},{1,9},{5... | collective-permute-start | bytes 3145736 | tf_op jit(solution)/shard_map/ppermute | solution.py:395
  44.6 31.9 %collective-permute-start.10 = (bf16[1024,512]{1,0:T(8,128)(2,1)}, bf16[1024,512]{1,0:T(8,128)(2,1)}, u32[]{:S(2)}, u32[]{:S(2)}) collective-permute-start(bf16[1024,512]{1,0:T(8,128)(2,1)} %constant_dynamic-update-slice_fusion.refs_4_.stack.refs_0_), channel_id=1, source_target_pairs={{0,4},{4,0},{8,12},{12,8},{16,20},{20,16},{24,28},{28,24},{1,5},{5... | collective-permute-start | bytes 3145736 | tf_op jit(solution)/shard_map/ppermute | solution.py:395
  53.7 31.1 %collective-permute-start.5 = (bf16[528,128]{1,0:T(8,128)(2,1)}, bf16[528,128]{1,0:T(8,128)(2,1)}, u32[]{:S(2)}, u32[]{:S(2)}) collective-permute-start(bf16[528,128]{1,0:T(8,128)(2,1)} %get-tuple-element.20.refs_3_), channel_id=1, source_target_pairs={{0,20},{4,16},{8,28},{12,24},{16,4},{20,0},{24,12},{28,8},{1,21},{... | collective-permute-start | bytes 405512 | tf_op jit(solution)/shard_map/ppermute | solution.py:395
  57.2 31.2 %collective-permute-start.8 = (bf16[528,128]{1,0:T(8,128)(2,1)}, bf16[528,128]{1,0:T(8,128)(2,1)}, u32[]{:S(2)}, u32[]{:S(2)}) collective-permute-start(bf16[528,128]{1,0:T(8,128)(2,1)} %get-tuple-element.23), channel_id=1, source_target_pairs={{0,24},{4,28},{8,16},{12,20},{16,8},{20,12},{24,0},{28,4},{1,25},{... | collective-permute-start | bytes 405512 | tf_op jit(solution)/shard_map/ppermute | solution.py:395
  57.3 27.1 %collective-permute-start.9 = (bf16[528,128]{1,0:T(8,128)(2,1)}, bf16[528,128]{1,0:T(8,128)(2,1)}, u32[]{:S(2)}, u32[]{:S(2)}) collective-permute-start(bf16[528,128]{1,0:T(8,128)(2,1)} %get-tuple-element.24.refs_0_), channel_id=1, source_target_pairs={{0,28},{4,24},{8,20},{12,16},{16,12},{20,8},{24,4},{28,0},{1,29},{... | collective-permute-start | bytes 405512 | tf_op jit(solution)/shard_map/ppermute | solution.py:395
  60.8 2.2 %copy-start.6 = (bf16[2,8192,128]{2,1,0:T(8,128)(2,1)S(1)}, bf16[2,8192,128]{2,1,0:T(8,128)(2,1)}, u32[]{:S(2)}) copy-start(bf16[2,8192,128]{2,1,0:T(8,128)(2,1)} %refs_2_.3) | copy-start | bytes 12582916
  70.4 18.0 %all-to-all-start.1 = ((bf16[4,528,128]{2,1,0:T(8,128)(2,1)}), bf16[4,528,128]{2,1,0:T(8,128)(2,1)S(1)}, u32[]{:S(2)}, u32[]{:S(2)}) async-start(bf16[4,528,128]{2,1,0:T(8,128)(2,1)} %serve_group.1.refs_1_), calls=%async_computation.1 | async-start | bytes 1081344 | tf_op jit(solution)/shard_map/all_to_all | solution.py:407
  76.5 8.3 %collective-permute-start.4 = (bf16[528,128]{1,0:T(8,128)(2,1)S(1)}, bf16[528,128]{1,0:T(8,128)(2,1)S(1)}, u32[]{:S(2)}, u32[]{:S(2)}) collective-permute-start(bf16[528,128]{1,0:T(8,128)(2,1)S(1)} %get-tuple-element.19), channel_id=1, source_target_pairs={{0,16},{4,20},{8,24},{12,28},{16,0},{20,4},{24,8},{28,12},{1,17},{... | collective-permute-start | bytes 405512 | tf_op jit(solution)/shard_map/ppermute | solution.py:395
  80.9 7.5 %copy-start.3 = (s32[2,1,2]{2,1,0:T(1,128)S(1)}, s32[2,1,2]{2,1,0:T(1,128)}, u32[]{:S(2)}) copy-start(s32[2,1,2]{2,1,0:T(1,128)} %selected_ref.3) | copy-start | bytes 52
  80.9 7.5 %copy-start.8 = (bf16[2,528,128]{2,1,0:T(8,128)(2,1)S(1)}, bf16[2,528,128]{2,1,0:T(8,128)(2,1)}, u32[]{:S(2)}) copy-start(bf16[2,528,128]{2,1,0:T(8,128)(2,1)} %copy-done.7) | copy-start | bytes 811012
  81.0 19.3 %collective-permute-start.14 = (bf16[512,512]{1,0:T(8,128)(2,1)S(1)}, bf16[512,512]{1,0:T(8,128)(2,1)S(1)}, u32[]{:S(2)}, u32[]{:S(2)}) collective-permute-start(bf16[512,512]{1,0:T(8,128)(2,1)S(1)} %gate.5), channel_id=1, source_target_pairs={{0,4},{4,0},{8,12},{12,8},{16,20},{20,16},{24,28},{28,24},{1,5},{5... | collective-permute-start | bytes 1572872 | tf_op jit(solution)/shard_map/ppermute | solution.py:395
  84.4 15.8 %collective-permute-start.15 = (bf16[512,512]{1,0:T(8,128)(2,1)S(1)}, bf16[512,512]{1,0:T(8,128)(2,1)S(1)}, u32[]{:S(2)}, u32[]{:S(2)}) collective-permute-start(bf16[512,512]{1,0:T(8,128)(2,1)S(1)} %gate.6), channel_id=1, source_target_pairs={{0,8},{4,12},{8,0},{12,4},{16,24},{20,28},{24,16},{28,20},{1,9},{5... | collective-permute-start | bytes 1572872 | tf_op jit(solution)/shard_map/ppermute | solution.py:395
  90.9 2.2 %collective-permute-start.11 = (bf16[256,512]{1,0:T(8,128)(2,1)S(1)}, bf16[256,512]{1,0:T(8,128)(2,1)S(1)}, u32[]{:S(2)}, u32[]{:S(2)}) collective-permute-start(bf16[256,512]{1,0:T(8,128)(2,1)S(1)} %combine_pieces.1.own_ref), channel_id=1, source_target_pairs={{0,1},{1,0},{2,3},{3,2},{4,5},{5,4},{6,7},{7,6},{8,9},{9,8},{10,11... | collective-permute-start | bytes 786440 | tf_op jit(solution)/shard_map/ppermute | solution.py:436
  91.9 8.3 %collective-permute-start.12 = (bf16[256,512]{1,0:T(8,128)(2,1)S(1)}, bf16[256,512]{1,0:T(8,128)(2,1)S(1)}, u32[]{:S(2)}, u32[]{:S(2)}) collective-permute-start(bf16[256,512]{1,0:T(8,128)(2,1)S(1)} %combine_pieces.1.own_ref), channel_id=1, source_target_pairs={{0,2},{1,3},{2,0},{3,1},{4,6},{5,7},{6,4},{7,5},{8,10},{9,11},{10,... | collective-permute-start | bytes 786440 | tf_op jit(solution)/shard_map/ppermute | solution.py:435
  100.2 1.6 %collective-permute-start.16 = (bf16[256,512]{1,0:T(8,128)(2,1)S(1)}, bf16[256,512]{1,0:T(8,128)(2,1)S(1)}, u32[]{:S(2)}, u32[]{:S(2)}) collective-permute-start(bf16[256,512]{1,0:T(8,128)(2,1)S(1)} %gate.7.y_ref), channel_id=1, source_target_pairs={{0,1},{1,0},{2,3},{3,2},{4,5},{5,4},{6,7},{7,6},{8,9},{9,8},{10,11... | collective-permute-start | bytes 786440 | tf_op jit(solution)/shard_map/ppermute | solution.py:441

commit v6 on v5

--- a/solution.py
+++ b/solution.py
@@ -43,7 +43,7 @@
     return tile, block, filled
 
 
-def pack_kernel(tiles, blocks, me_ref, selected_ref, query_ref, near_ref, *far_refs):
+def pack_kernel(tiles, blocks, me_ref, selected_ref, query_ref, near_ref, self_ref, *far_refs):
     def fill(slot, peer):
         tile, block, _ = route(selected_ref, me_ref[0], peer, tiles, blocks)
         rows = pl.ds(pl.multiple_of(tile * TILE, TILE), TILE)
@@ -53,6 +53,7 @@
 
     for place in range(NEAR):
         fill(near_ref.at[place], (me_ref[0] & ~(NEAR - 1)) + place)
+    fill(self_ref, me_ref[0])
     for index, slot in enumerate(far_refs):
         fill(slot, me_ref[0] ^ (NEAR + index))
 
@@ -62,9 +63,9 @@
     return pl.pallas_call(
         functools.partial(pack_kernel, tiles, blocks),
         out_shape=[jax.ShapeDtypeStruct((NEAR, SLOT, HD), jnp.bfloat16)]
-        + [jax.ShapeDtypeStruct((SLOT, HD), jnp.bfloat16)] * (seq_count - NEAR),
+        + [jax.ShapeDtypeStruct((SLOT, HD), jnp.bfloat16)] * (seq_count - NEAR + 1),
         in_specs=[smem, smem, vmem],
-        out_specs=[vmem] * (seq_count - NEAR + 1),
+        out_specs=[vmem] * (seq_count - NEAR + 2),
         compiler_params=params(),
         name="pack_queries",
     )(me, selected, queries)
@@ -182,39 +183,43 @@
     )(*slots, kv_cache, *after)
 
 
-def serve_group_kernel(slots_ref, kv_ref, *refs):
+def serve_group_kernel(me_ref, slots_ref, kv_ref, *refs):
     out_ref, keys, values, sems = refs[-4:]
+    own_place = me_ref[0] & (NEAR - 1)
     copies = []
-    for place in range(NEAR):
+    for index in range(NEAR - 1):
+        place = own_place ^ (index + 1)
         number = jnp.max(slots_ref[place, ROWS:SLOT, :].astype(jnp.float32)).astype(jnp.int32)
         start = pl.multiple_of(number * BLK, BLK)
         for half, buffer in enumerate((keys, values)):
             copy = pltpu.make_async_copy(
-                kv_ref.at[half, pl.ds(start, BLK)], buffer.at[place], sems.at[half, place]
+                kv_ref.at[half, pl.ds(start, BLK)], buffer.at[index], sems.at[half, index]
             )
             copy.start()
             copies.append(copy)
-    for place in range(NEAR):
-        copies[2 * place].wait()
-        copies[2 * place + 1].wait()
-        attend(slots_ref[place, 0:ROWS, :], keys[place], values[place], None, out_ref.at[place])
-
-
-def serve_group(slots, kv_cache, after):
+    out_ref[own_place] = jnp.zeros((SLOT, HD), jnp.bfloat16)
+    for index in range(NEAR - 1):
+        place = own_place ^ (index + 1)
+        copies[2 * index].wait()
+        copies[2 * index + 1].wait()
+        attend(slots_ref[place, 0:ROWS, :], keys[index], values[index], None, out_ref.at[place])
+
+
+def serve_group(me, slots, kv_cache, after):
     return pl.pallas_call(
         serve_group_kernel,
         out_shape=jax.ShapeDtypeStruct((NEAR, SLOT, HD), jnp.bfloat16),
-        in_specs=[vmem, hbm] + [anywhere] * len(after),
+        in_specs=[smem, vmem, hbm] + [anywhere] * len(after),
         out_specs=vmem,
         scratch_shapes=[
-            pltpu.VMEM((NEAR, BLK, HD), jnp.bfloat16),
-            pltpu.VMEM((NEAR, BLK, HD), jnp.bfloat16),
-            pltpu.SemaphoreType.DMA((2, NEAR)),
+            pltpu.VMEM((NEAR - 1, BLK, HD), jnp.bfloat16),
+            pltpu.VMEM((NEAR - 1, BLK, HD), jnp.bfloat16),
+            pltpu.SemaphoreType.DMA((2, NEAR - 1)),
         ],
         compiler_params=params(),
         cost_estimate=pl.CostEstimate(flops=1 << 36, bytes_accessed=1 << 30, transcendentals=1),
         name="serve_group",
-    )(slots, kv_cache, *after)
+    )(me, slots, kv_cache, *after)
 
 
 def levels_of(parts):
@@ -222,17 +227,16 @@
     return parts[0:GROUP] + parts[GROUP : 2 * GROUP] + parts[2 * GROUP : 3 * GROUP]
 
 
-def combine_kernel(tiles, blocks, seq_count, me_ref, selected_ref, own_ref, near_ref, *refs):
+def combine_kernel(
+    tiles, blocks, seq_count, me_ref, selected_ref, own_ref, self_ref, near_ref, *refs
+):
     far_refs, out_ref, blend = refs[: seq_count - NEAR], refs[-2], refs[-1]
-    slots, routes = [], []
-    for place in range(NEAR):
-        slots.append(near_ref.at[place])
-        routes.append(
-            route(selected_ref, me_ref[0], (me_ref[0] & ~(NEAR - 1)) + place, tiles, blocks)
-        )
-    for index, slot in enumerate(far_refs):
-        slots.append(slot)
-        routes.append(route(selected_ref, me_ref[0], me_ref[0] ^ (NEAR + index), tiles, blocks))
+    own_place = me_ref[0] & (NEAR - 1)
+    slots = [self_ref, *[near_ref.at[own_place ^ offset] for offset in range(1, NEAR)], *far_refs]
+    routes = [
+        route(selected_ref, me_ref[0], me_ref[0] ^ offset, tiles, blocks)
+        for offset in range(seq_count)
+    ]
     slot_levels = [levels_of(slot[ROWS:SLOT, :]) for slot in slots]
     for tile in range(tiles):
         own_level = levels_of(own_ref[tile, ROWS:SLOT, :])
@@ -272,18 +276,18 @@
             ].astype(jnp.bfloat16)
 
 
-def combine(me, selected, own, near, far, blocks, after):
+def combine(me, selected, own, self_answer, near, far, blocks, after):
     tiles, seq_count = own.shape[0], NEAR + len(far)
     return pl.pallas_call(
         functools.partial(combine_kernel, tiles, blocks, seq_count),
         out_shape=jax.ShapeDtypeStruct((tiles * TILE, GROUP * HD), jnp.bfloat16),
-        in_specs=[smem, smem, vmem, vmem] + [vmem] * len(far) + [anywhere] * len(after),
+        in_specs=[smem, smem, vmem, vmem, vmem] + [vmem] * len(far) + [anywhere] * len(after),
         out_specs=vmem,
         scratch_shapes=[pltpu.VMEM((ROWS, HD), jnp.float32)],
         compiler_params=params(),
         cost_estimate=pl.CostEstimate(flops=1 << 36, bytes_accessed=1 << 30, transcendentals=1),
         name="combine_pieces",
-    )(me, selected, own, near, *far, *after)
+    )(me, selected, own, self_answer, near, *far, *after)
 
 
 def halves(numbers_ref, first, second):
@@ -408,7 +412,7 @@
             array, "seq", split_axis=0, concat_axis=0, axis_index_groups=groups, tiled=True
         )
 
-    near, *far = pack(me, requests, queries, seq_count, blocks)
+    near, mine, *far = pack(me, requests, queries, seq_count, blocks)
     arrived = {NEAR + index: move(slot, NEAR + index) for index, slot in enumerate(far)}
     returned = {}
 
@@ -419,18 +423,19 @@
         return answers[-1]
 
     own = own_pieces(queries, kv_cache, [near])
-    near_answers = serve_group(swap(near), kv_cache, [own] + [])
+    near_answers = serve_group(me, swap(near), kv_cache, [own] + [])
     returned_near = swap(near_answers)
     half = (seq_count + NEAR) // 2
-    first = answer(list(range(NEAR, half)), [own] + ([stack] if fast else []))
+    self_answer = serve([mine], kv_cache, [own] + ([stack] if fast else []))[0]
+    first = answer(list(range(NEAR, half)), [self_answer] + ([stack] if fast else []))
     last = answer(list(range(half, seq_count)), [first] + [])
     if fast:
         depth = out_weight.shape[0]
-        first_zx = move(gate(stack_z[:depth], near_answers), 1)
-        second_zx = move(gate(stack_x[depth:], near_answers), 2)
+        first_zx = move(gate(stack_z[:depth], last), 1)
+        second_zx = move(gate(stack_x[depth:], last), 2)
     tick = gate(last, returned_near, *[returned[offset] for offset in range(NEAR, half)], *([stack_x] if fast else []))
     far = [returned[offset] for offset in range(NEAR, seq_count)]
-    attention = combine(me, requests, own, returned_near, far, blocks, [tick] + [])
+    attention = combine(me, requests, own, self_answer, returned_near, far, blocks, [tick] + [])
     if fast:
         other_y = lax.ppermute(attention, "kvh", pairs(kvh_count, 2))
         other_core = lax.ppermute(attention, "kvh", pairs(kvh_count, 1))

time: 106 us -> 106 us (level)
  waiting for transfers between devices: 19.7 us -> 18.5 us
    pallas_call x2 -> x3, Pallas kernels: 6.93 us -> 9.2 us  [serve(): pl.pallas_call(functools.partial(serve_kernel, count), out_shape=[jax.Sha...]
    pallas_call x1, Pallas kernels: 7.43 us -> 6.07 us  [serve_group(): pl.pallas_call(serve_group_kernel, out_shape=jax.ShapeDtypeStruct((NEAR,...]
    unnamed x19 -> x23, local copies, waits for them, and re-layouts: 7.81 us -> 7.83 us
  transfers between devices with their start and end apart: 19 -> 19, of which waited for: 8 -> 8; matrix products, arithmetic and copies ran while one was open for 4% -> 4% of each run, Pallas kernels for 22% -> 23%
where the time goes in v6:
time: 106 us; the launch traced here: 105 us
  starting transfers between devices  47.7 us (45%)
  Pallas kernels  27.9 us (26%)
  waiting for transfers between devices  18.5 us (17%)
  local copies, waits for them, and re-layouts  10.8 us (10%)
    ppermute x12, starting transfers between devices, move(): return lax.ppermute(array, 'seq', pairs(seq_count, offset))  31.6 us
    pallas_call x3, Pallas kernels, serve(): pl.pallas_call(functools.partial(serve_kernel, count), out_shape=[jax.Sha...  9.2 us
    all_to_all x2, starting transfers between devices, swap(): lax.all_to_all(array, 'seq', split_axis=0, concat_axis=0, axis_index_grou...  8.84 us
    ppermute x12, waiting for transfers between devices, move(): return lax.ppermute(array, 'seq', pairs(seq_count, offset))  7.99 us
    unnamed x23, local copies, waits for them, and re-layouts  7.83 us
    pallas_call x1, Pallas kernels, serve_group(): pl.pallas_call(serve_group_kernel, out_shape=jax.ShapeDtypeStruct((NEAR,...  6.07 us
    ppermute x2, starting transfers between devices, jump(): return lax.ppermute(weight, ('seq', 'kvh'), moves)  5.72 us
    ppermute x1, waiting for transfers between devices, per_device(): other_y = lax.ppermute(attention, 'kvh', pairs(kvh_count, 2))  4.68 us
  transfers between devices with their start and end apart: 19, of which 8 were waited for; matrix products, arithmetic and copies ran while one was open for 4% of the time, Pallas kernels for 23%

profile of v6, /device:TPU:0, one launch (start us, length us, event | category | flops | bytes accessed | tf_op | source)
XLA Modules:
  0.0 105.2 jit_solution(4980237096199750668)
XLA Ops:
  0.0 4.0 %collective-permute-start.1 = (bf16[512,512]{1,0:T(8,128)(2,1)}, bf16[512,512]{1,0:T(8,128)(2,1)S(1)}, u32[]{:S(2)}, u32[]{:S(2)}) collective-permute-start(bf16[512,512]{1,0:T(8,128)(2,1)} %param.7), channel_id=1, source_target_pairs={{0,16},{1,24},{2,0},{3,8},{4,20},{5,28},{6,4},{7,12},{8,17},{9,25}... | collective-permute-start | bytes 1572872 | tf_op jit(solution)/shard_map/ppermute | solution.py:387
  4.0 1.7 %collective-permute-start = (bf16[512,512]{1,0:T(8,128)(2,1)}, bf16[512,512]{1,0:T(8,128)(2,1)S(1)}, u32[]{:S(2)}, u32[]{:S(2)}) collective-permute-start(bf16[512,512]{1,0:T(8,128)(2,1)} %param.7), channel_id=1, source_target_pairs={{0,0},{1,8},{2,16},{3,24},{4,4},{5,12},{6,20},{7,28},{8,1},{9,9},{... | collective-permute-start | bytes 1572872 | tf_op jit(solution)/shard_map/ppermute | solution.py:387
  5.7 0.9 copy-done
  6.7 0.7 copy-done.2
  7.4 1.7 %pack_queries.1 = (bf16[4,528,128]{2,1,0:T(8,128)(2,1)}, bf16[528,128]{1,0:T(8,128)(2,1)S(1)}, bf16[528,128]{1,0:T(8,128)(2,1)S(1)}, bf16[528,128]{1,0:T(8,128)(...) custom-call(s32[1]{0:T(128)} %bitcast.3.me_ref, s32[2,1,2]{2,1,0:T(1,128)S(1)} %copy-done.2, ...), custom_call_target="tpu_custom_call" | custom-call | tf_op jit(solution)/shard_map/pack_queries/pallas_call | solution.py:63
  9.1 5.2 %all-to-all-start = ((bf16[4,528,128]{2,1,0:T(8,128)(2,1)}), bf16[4,528,128]{2,1,0:T(8,128)(2,1)}, u32[]{:S(2)}, u32[]{:S(2)}) async-start(bf16[4,528,128]{2,1,0:T(8,128)(2,1)} %get-tuple-element.17.refs_0_), calls=%async_computation | async-start | bytes 1081344 | tf_op jit(solution)/shard_map/all_to_all | solution.py:411
  14.2 1.2 %collective-permute-start.2 = (bf16[528,128]{1,0:T(8,128)(2,1)S(1)}, bf16[528,128]{1,0:T(8,128)(2,1)S(1)}, u32[]{:S(2)}, u32[]{:S(2)}) collective-permute-start(bf16[528,128]{1,0:T(8,128)(2,1)S(1)} %get-tuple-element.19), channel_id=1, source_target_pairs={{0,16},{4,20},{8,24},{12,28},{16,0},{20,4},{24,8},{28,12},{1,17},{... | collective-permute-start | bytes 405512 | tf_op jit(solution)/shard_map/ppermute | solution.py:399
  15.5 3.1 %collective-permute-start.3 = (bf16[528,128]{1,0:T(8,128)(2,1)S(1)}, bf16[528,128]{1,0:T(8,128)(2,1)S(1)}, u32[]{:S(2)}, u32[]{:S(2)}) collective-permute-start(bf16[528,128]{1,0:T(8,128)(2,1)S(1)} %get-tuple-element.20), channel_id=1, source_target_pairs={{0,20},{4,16},{8,28},{12,24},{16,4},{20,0},{24,12},{28,8},{1,21},{... | collective-permute-start | bytes 405512 | tf_op jit(solution)/shard_map/ppermute | solution.py:399
  18.6 2.1 %collective-permute-start.6 = (bf16[528,128]{1,0:T(8,128)(2,1)}, bf16[528,128]{1,0:T(8,128)(2,1)}, u32[]{:S(2)}, u32[]{:S(2)}) collective-permute-start(bf16[528,128]{1,0:T(8,128)(2,1)} %get-tuple-element.23), channel_id=1, source_target_pairs={{0,24},{4,28},{8,16},{12,20},{16,8},{20,12},{24,0},{28,4},{1,25},{... | collective-permute-start | bytes 405512 | tf_op jit(solution)/shard_map/ppermute | solution.py:399
  20.8 0.9 copy-done.1
  21.7 2.2 %copy-done.4 = bf16[2,8192,128]{2,1,0:T(8,128)(2,1)S(1)} copy-done((bf16[2,8192,128]{2,1,0:T(8,128)(2,1)S(1)}, bf16[2,8192,128]{2,1,0:T(8,128)(2,1)}, u32[]{:S(2)}) %copy-start.4) | copy-done | bytes 4194328
  23.9 2.7 %own_pieces.1.refs_2_.refs_0_.own_ref = bf16[2,528,128]{2,1,0:T(8,128)(2,1)S(1)} custom-call(bf16[256,512]{1,0:T(8,128)(2,1)S(1)} %copy-done.1, bf16[2,8192,128]{2,1,0:T(8,128)(2,1)S(1)} %copy-done.4, bf16[4,528,128]{2,1,0:T(8,128)(2,1)} %get-tuple-element.17.refs_0_), custom_call_target="tpu_custom_call" | custom-call | flops 68719476736 | bytes 1073741824 | tf_op jit(solution)/shard_map/own_pieces/pallas_call | solution.py:133
  26.6 0.0 copy-start.7
  26.7 0.0 collective-permute-done
  26.7 2.7 %collective-permute-start.7 = (bf16[528,128]{1,0:T(8,128)(2,1)S(1)}, bf16[528,128]{1,0:T(8,128)(2,1)S(1)}, u32[]{:S(2)}, u32[]{:S(2)}) collective-permute-start(bf16[528,128]{1,0:T(8,128)(2,1)S(1)} %get-tuple-element.24), channel_id=1, source_target_pairs={{0,28},{4,24},{8,20},{12,16},{16,12},{20,8},{24,4},{28,0},{1,29},{... | collective-permute-start | bytes 405512 | tf_op jit(solution)/shard_map/ppermute | solution.py:399
  29.3 0.8 constant_dynamic-update-slice_fusion.1
  30.2 0.0 collective-permute-done.1
  30.2 0.8 constant_dynamic-update-slice_fusion.refs_3_.refs_4_.stack.refs_0_
  31.0 13.6 %collective-permute-start.13 = (bf16[1024,512]{1,0:T(8,128)(2,1)}, bf16[1024,512]{1,0:T(8,128)(2,1)}, u32[]{:S(2)}, u32[]{:S(2)}) collective-permute-start(bf16[1024,512]{1,0:T(8,128)(2,1)} %constant_dynamic-update-slice_fusion.refs_3_.refs_4_.stack.refs_0_), channel_id=1, source_target_pairs={{0,8},{4,12},{8,0},{12,4},{16,24},{20,28},{24,16},{28,20},{1,9},{5... | collective-permute-start | bytes 3145736 | tf_op jit(solution)/shard_map/ppermute | solution.py:399
  44.6 0.0 copy-done.5
  44.6 1.4 %serve_slots.3.refs_3_.self_ref = bf16[528,128]{1,0:T(8,128)(2,1)S(1)} custom-call(bf16[528,128]{1,0:T(8,128)(2,1)S(1)} %get-tuple-element.18.refs_0_, bf16[2,8192,128]{2,1,0:T(8,128)(2,1)S(1)} %copy-done.5, bf16[2,528,128]{2,1,0:T(8,128)(2,1)S(1)} %own_pieces.1.refs_2_.refs_0_.own_ref, ...), custom_call_target="tpu_custom_call" | custom-call | flops 68719476736 | bytes 1073741824 | tf_op jit(solution)/shard_map/serve_slots/pallas_call | solution.py:170
  46.0 0.0 copy-start.9
  46.1 0.0 collective-permute-done.2.refs_0_
  46.1 0.3 collective-permute-start.10
  46.4 3.7 %collective-permute-done.3.refs_1_ = bf16[528,128]{1,0:T(8,128)(2,1)S(1)} collective-permute-done((bf16[528,128]{1,0:T(8,128)(2,1)S(1)}, bf16[528,128]{1,0:T(8,128)(2,1)S(1)}, u32[]{:S(2)}, u32[]{:S(2)}) %collective-permute-start.3) | collective-permute-done | bytes 135200 | tf_op jit(solution)/shard_map/ppermute | solution.py:399
  50.1 3.5 %serve_slots.4 = (bf16[528,128]{1,0:T(8,128)(2,1)S(1)}, bf16[528,128]{1,0:T(8,128)(2,1)}) custom-call(bf16[528,128]{1,0:T(8,128)(2,1)S(1)} %collective-permute-done.2.refs_0_, bf16[528,128]{1,0:T(8,128)(2,1)S(1)} %collective-permute-done.3.refs_1_, bf16[2,8192,128]{2,1,0:T(8,128)(2,1)S(1)} %copy-done.5, bf16[528,128]{1,0:T(8,128)(2,1)S(1)} %serve_slots.3.refs_3_.self_ref, ...), custom_call_target="tpu_custom_call" | custom-call | flops 68719476736 | bytes 1073741824 | tf_op jit(solution)/shard_map/serve_slots/pallas_call | solution.py:170
  53.6 0.0 copy-done.9
  53.6 0.1 collective-permute-start.5
  53.7 0.0 collective-permute-done.6.refs_0_
  53.7 0.0 collective-permute-done.7.refs_1_
  53.7 4.3 %serve_slots.5 = (bf16[528,128]{1,0:T(8,128)(2,1)}, bf16[528,128]{1,0:T(8,128)(2,1)}) custom-call(bf16[528,128]{1,0:T(8,128)(2,1)} %collective-permute-done.6.refs_0_, bf16[528,128]{1,0:T(8,128)(2,1)S(1)} %collective-permute-done.7.refs_1_, bf16[2,8192,128]{2,1,0:T(8,128)(2,1)S(1)} %copy-done.5, bf16[528,128]{1,0:T(8,128)(2,1)} %get-tuple-element.22.refs_3_), custom_call_target="tpu_custom_call" | custom-call | flops 68719476736 | bytes 1073741824 | tf_op jit(solution)/shard_map/serve_slots/pallas_call | solution.py:170
  58.0 0.1 collective-permute-start.8
  58.1 3.5 %collective-permute-start.9 = (bf16[528,128]{1,0:T(8,128)(2,1)}, bf16[528,128]{1,0:T(8,128)(2,1)}, u32[]{:S(2)}, u32[]{:S(2)}) collective-permute-start(bf16[528,128]{1,0:T(8,128)(2,1)} %get-tuple-element.26.refs_0_.refs_1_), channel_id=1, source_target_pairs={{0,28},{4,24},{8,20},{12,16},{16,12},{20,8},{24,4},{28,0},{1,29},{... | collective-permute-start | bytes 405512 | tf_op jit(solution)/shard_map/ppermute | solution.py:399
  61.6 0.0 all-to-all-done.slots_ref
  61.6 0.0 copy-done.7
  61.6 2.2 %copy-done.6 = bf16[2,8192,128]{2,1,0:T(8,128)(2,1)S(1)} copy-done((bf16[2,8192,128]{2,1,0:T(8,128)(2,1)S(1)}, bf16[2,8192,128]{2,1,0:T(8,128)(2,1)}, u32[]{:S(2)}) %copy-start.6) | copy-done | bytes 4194328
  63.8 6.1 %serve_group.1 = bf16[4,528,128]{2,1,0:T(8,128)(2,1)} custom-call(s32[1]{0:T(128)} %bitcast.3.me_ref, bf16[4,528,128]{2,1,0:T(8,128)(2,1)} %all-to-all-done.slots_ref, bf16[2,8192,128]{2,1,0:T(8,128)(2,1)S(1)} %copy-done.6, bf16[2,528,128]{2,1,0:T(8,128)(2,1)S(1)} %own_pieces.1.refs_2_.refs_0_.own_ref), custom_call_target="tpu_custom_call" | custom-call | flops 68719476736 | bytes 1073741824 | tf_op jit(solution)/shard_map/serve_group/pallas_call | solution.py:209
  69.9 3.7 %all-to-all-start.1 = ((bf16[4,528,128]{2,1,0:T(8,128)(2,1)}), bf16[4,528,128]{2,1,0:T(8,128)(2,1)S(1)}, u32[]{:S(2)}, u32[]{:S(2)}) async-start(bf16[4,528,128]{2,1,0:T(8,128)(2,1)} %serve_group.1), calls=%async_computation.1 | async-start | bytes 1081344 | tf_op jit(solution)/shard_map/all_to_all | solution.py:411
  73.6 0.3 collective-permute-done.10.refs_4_.stack_x.refs_2_
  73.9 2.7 %collective-permute-start.4 = (bf16[528,128]{1,0:T(8,128)(2,1)S(1)}, bf16[528,128]{1,0:T(8,128)(2,1)S(1)}, u32[]{:S(2)}, u32[]{:S(2)}) collective-permute-start(bf16[528,128]{1,0:T(8,128)(2,1)S(1)} %get-tuple-element.21), channel_id=1, source_target_pairs={{0,16},{4,20},{8,24},{12,28},{16,0},{20,4},{24,8},{28,12},{1,17},{... | collective-permute-start | bytes 405512 | tf_op jit(solution)/shard_map/ppermute | solution.py:399
  76.6 1.1 %slice.9.refs_0_ = bf16[512,512]{1,0:T(8,128)(2,1)S(1)} slice(bf16[1024,512]{1,0:T(8,128)(2,1)} %collective-permute-done.10.refs_4_.stack_x.refs_2_), slice={[512:1024], [0:512]} | slice | bytes 1048576 | tf_op jit(solution)/shard_map/slice | solution.py:435
  77.7 3.6 %collective-permute-done.13.stack_z.refs_1_ = bf16[1024,512]{1,0:T(8,128)(2,1)} collective-permute-done((bf16[1024,512]{1,0:T(8,128)(2,1)}, bf16[1024,512]{1,0:T(8,128)(2,1)}, u32[]{:S(2)}, u32[]{:S(2)}) %collective-permute-start.13) | collective-permute-done | bytes 1048608 | tf_op jit(solution)/shard_map/ppermute | solution.py:399
  81.3 1.1 %slice.8.refs_0_ = bf16[512,512]{1,0:T(8,128)(2,1)S(1)} slice(bf16[1024,512]{1,0:T(8,128)(2,1)} %collective-permute-done.13.stack_z.refs_1_), slice={[0:512], [0:512]} | slice | bytes 1048576 | tf_op jit(solution)/shard_map/slice | solution.py:434
  82.4 0.0 copy-start.3
  82.4 0.0 copy-start.8
  82.4 2.0 %collective-permute-start.14 = (bf16[512,512]{1,0:T(8,128)(2,1)S(1)}, bf16[512,512]{1,0:T(8,128)(2,1)S(1)}, u32[]{:S(2)}, u32[]{:S(2)}) collective-permute-start(bf16[512,512]{1,0:T(8,128)(2,1)S(1)} %gate.5), channel_id=1, source_target_pairs={{0,4},{4,0},{8,12},{12,8},{16,20},{20,16},{24,28},{28,24},{1,5},{5... | collective-permute-start | bytes 1572872 | tf_op jit(solution)/shard_map/ppermute | solution.py:399
  84.4 0.0 collective-permute-done.9.refs_3_
  84.4 0.0 collective-permute-start.15
  84.5 0.3 collective-permute-done.4.refs_2_.refs_0_
  84.8 0.0 collective-permute-done.5.refs_3_.refs_1_
  84.8 3.6 %all-to-all-done.1.refs_1_.near_ref = bf16[4,528,128]{2,1,0:T(8,128)(2,1)S(1)} async-done(((bf16[4,528,128]{2,1,0:T(8,128)(2,1)}), bf16[4,528,128]{2,1,0:T(8,128)(2,1)S(1)}, u32[]{:S(2)}, u32[]{:S(2)}) %all-to-all-start.1) | async-done | bytes 540704 | tf_op jit(solution)/shard_map/all_to_all | solution.py:411
  88.4 0.0 collective-permute-done.8.refs_2_
  88.4 2.3 %combine_pieces.1.own_ref = bf16[256,512]{1,0:T(8,128)(2,1)S(1)} custom-call(s32[1]{0:T(128)} %bitcast.3.me_ref, s32[2,1,2]{2,1,0:T(1,128)S(1)} %copy-done.3, bf16[2,528,128]{2,1,0:T(8,128)(2,1)S(1)} %copy-done.8, bf16[528,128]{1,0:T(8,128)(2,1)S(1)} %copy-done.10, bf16[4,528,128]{2,1,0:T(8,128)(2,1)S(1)} %all-to-all-done.1.refs_1_.near_ref, ...), custom_call_target="tpu_custom_call" | custom-call | flops 68719476736 | bytes 1073741824 | tf_op jit(solution)/shard_map/combine_pieces/pallas_call | solution.py:281
  90.7 1.0 collective-permute-start.11
  91.8 0.4 collective-permute-start.12
  92.2 0.1 pad_add_fusion.numbers_ref
  92.2 0.7 collective-permute-done.11.core_ref
  92.9 2.4 %project.1 = (f32[256,512]{1,0:T(8,128)S(1)}, f32[256,512]{1,0:T(8,128)S(1)}) custom-call(s32[3]{0:T(128)S(1)} %pad_add_fusion.numbers_ref, bf16[256,512]{1,0:T(8,128)(2,1)S(1)} %combine_pieces.1.own_ref, bf16[256,512]{1,0:T(8,128)(2,1)S(1)} %collective-permute-done.11.core_ref, ...), custom_call_target="tpu_custom_call" | custom-call | tf_op jit(solution)/shard_map/project/pallas_call | solution.py:338
  95.4 4.7 %collective-permute-done.12.refs_0_ = bf16[256,512]{1,0:T(8,128)(2,1)S(1)} collective-permute-done((bf16[256,512]{1,0:T(8,128)(2,1)S(1)}, bf16[256,512]{1,0:T(8,128)(2,1)S(1)}, u32[]{:S(2)}, u32[]{:S(2)}) %collective-permute-start.12) | collective-permute-done | bytes 262176 | tf_op jit(solution)/shard_map/ppermute | solution.py:440
  100.1 0.0 collective-permute-done.14.refs_2_.refs_3_
  100.1 0.0 collective-permute-done.15.refs_3_.refs_4_
  100.1 0.1 collective-permute-start.16
  100.2 1.5 %collective-permute-done.16.both_ref = bf16[256,512]{1,0:T(8,128)(2,1)S(1)} collective-permute-done((bf16[256,512]{1,0:T(8,128)(2,1)S(1)}, bf16[256,512]{1,0:T(8,128)(2,1)S(1)}, u32[]{:S(2)}, u32[]{:S(2)}) %collective-permute-start.16) | collective-permute-done | bytes 262176 | tf_op jit(solution)/shard_map/ppermute | solution.py:446
  101.7 3.5 %finish.1 = bf16[256,1024]{1,0:T(8,128)(2,1)} custom-call(s32[3]{0:T(128)S(1)} %pad_add_fusion.numbers_ref, bf16[256,512]{1,0:T(8,128)(2,1)S(1)} %combine_pieces.1.own_ref, bf16[256,512]{1,0:T(8,128)(2,1)S(1)} %collective-permute-done.11.core_ref, bf16[256,512]{1,0:T(8,128)(2,1)S(1)} %gate.7.y_ref, bf16[256,512]{1,0:T(8,128)(2,1)S(1)} %collective-permute-done.16.both_ref, ...), custom_call_target="tpu_custom_call" | custom-call | tf_op jit(solution)/shard_map/finish/pallas_call | solution.py:350
  (14 shorter events, 0.0 us)
Async XLA Ops:
  0.0 30.2 %collective-permute-start.1 = (bf16[512,512]{1,0:T(8,128)(2,1)}, bf16[512,512]{1,0:T(8,128)(2,1)S(1)}, u32[]{:S(2)}, u32[]{:S(2)}) collective-permute-start(bf16[512,512]{1,0:T(8,128)(2,1)} %param.7), channel_id=1, source_target_pairs={{0,16},{1,24},{2,0},{3,8},{4,20},{5,28},{6,4},{7,12},{8,17},{9,25}... | collective-permute-start | bytes 1572872 | tf_op jit(solution)/shard_map/ppermute | solution.py:387
  4.0 22.6 %collective-permute-start = (bf16[512,512]{1,0:T(8,128)(2,1)}, bf16[512,512]{1,0:T(8,128)(2,1)S(1)}, u32[]{:S(2)}, u32[]{:S(2)}) collective-permute-start(bf16[512,512]{1,0:T(8,128)(2,1)} %param.7), channel_id=1, source_target_pairs={{0,0},{1,8},{2,16},{3,24},{4,4},{5,12},{6,20},{7,28},{8,1},{9,9},{... | collective-permute-start | bytes 1572872 | tf_op jit(solution)/shard_map/ppermute | solution.py:387
  5.7 0.9 copy-start
  6.7 0.7 copy-start.2
  9.1 52.6 %all-to-all-start = ((bf16[4,528,128]{2,1,0:T(8,128)(2,1)}), bf16[4,528,128]{2,1,0:T(8,128)(2,1)}, u32[]{:S(2)}, u32[]{:S(2)}) async-start(bf16[4,528,128]{2,1,0:T(8,128)(2,1)} %get-tuple-element.17.refs_0_), calls=%async_computation | async-start | bytes 1081344 | tf_op jit(solution)/shard_map/all_to_all | solution.py:411
  14.2 31.8 %collective-permute-start.2 = (bf16[528,128]{1,0:T(8,128)(2,1)S(1)}, bf16[528,128]{1,0:T(8,128)(2,1)S(1)}, u32[]{:S(2)}, u32[]{:S(2)}) collective-permute-start(bf16[528,128]{1,0:T(8,128)(2,1)S(1)} %get-tuple-element.19), channel_id=1, source_target_pairs={{0,16},{4,20},{8,24},{12,28},{16,0},{20,4},{24,8},{28,12},{1,17},{... | collective-permute-start | bytes 405512 | tf_op jit(solution)/shard_map/ppermute | solution.py:399
  15.5 34.6 %collective-permute-start.3 = (bf16[528,128]{1,0:T(8,128)(2,1)S(1)}, bf16[528,128]{1,0:T(8,128)(2,1)S(1)}, u32[]{:S(2)}, u32[]{:S(2)}) collective-permute-start(bf16[528,128]{1,0:T(8,128)(2,1)S(1)} %get-tuple-element.20), channel_id=1, source_target_pairs={{0,20},{4,16},{8,28},{12,24},{16,4},{20,0},{24,12},{28,8},{1,21},{... | collective-permute-start | bytes 405512 | tf_op jit(solution)/shard_map/ppermute | solution.py:399
  18.6 35.0 %collective-permute-start.6 = (bf16[528,128]{1,0:T(8,128)(2,1)}, bf16[528,128]{1,0:T(8,128)(2,1)}, u32[]{:S(2)}, u32[]{:S(2)}) collective-permute-start(bf16[528,128]{1,0:T(8,128)(2,1)} %get-tuple-element.23), channel_id=1, source_target_pairs={{0,24},{4,28},{8,16},{12,20},{16,8},{20,12},{24,0},{28,4},{1,25},{... | collective-permute-start | bytes 405512 | tf_op jit(solution)/shard_map/ppermute | solution.py:399
  20.8 0.9 copy-start.1
  21.7 2.2 %copy-start.4 = (bf16[2,8192,128]{2,1,0:T(8,128)(2,1)S(1)}, bf16[2,8192,128]{2,1,0:T(8,128)(2,1)}, u32[]{:S(2)}) copy-start(bf16[2,8192,128]{2,1,0:T(8,128)(2,1)} %refs_2_.3) | copy-start | bytes 12582916
  23.9 20.7 %copy-start.5 = (bf16[2,8192,128]{2,1,0:T(8,128)(2,1)S(1)}, bf16[2,8192,128]{2,1,0:T(8,128)(2,1)}, u32[]{:S(2)}) copy-start(bf16[2,8192,128]{2,1,0:T(8,128)(2,1)} %refs_2_.3) | copy-start | bytes 12582916
  26.6 35.0 %copy-start.7 = (bf16[2,528,128]{2,1,0:T(8,128)(2,1)}, bf16[2,528,128]{2,1,0:T(8,128)(2,1)S(1)}, u32[]{:S(2)}) copy-start(bf16[2,528,128]{2,1,0:T(8,128)(2,1)S(1)} %own_pieces.1.refs_2_.refs_0_.own_ref) | copy-start | bytes 811012
  26.7 27.0 %collective-permute-start.7 = (bf16[528,128]{1,0:T(8,128)(2,1)S(1)}, bf16[528,128]{1,0:T(8,128)(2,1)S(1)}, u32[]{:S(2)}, u32[]{:S(2)}) collective-permute-start(bf16[528,128]{1,0:T(8,128)(2,1)S(1)} %get-tuple-element.24), channel_id=1, source_target_pairs={{0,28},{4,24},{8,20},{12,16},{16,12},{20,8},{24,4},{28,0},{1,29},{... | collective-permute-start | bytes 405512 | tf_op jit(solution)/shard_map/ppermute | solution.py:399
  31.0 50.3 %collective-permute-start.13 = (bf16[1024,512]{1,0:T(8,128)(2,1)}, bf16[1024,512]{1,0:T(8,128)(2,1)}, u32[]{:S(2)}, u32[]{:S(2)}) collective-permute-start(bf16[1024,512]{1,0:T(8,128)(2,1)} %constant_dynamic-update-slice_fusion.refs_3_.refs_4_.stack.refs_0_), channel_id=1, source_target_pairs={{0,8},{4,12},{8,0},{12,4},{16,24},{20,28},{24,16},{28,20},{1,9},{5... | collective-permute-start | bytes 3145736 | tf_op jit(solution)/shard_map/ppermute | solution.py:399
  46.0 7.5 %copy-start.9 = (bf16[528,128]{1,0:T(8,128)(2,1)}, bf16[528,128]{1,0:T(8,128)(2,1)S(1)}, u32[]{:S(2)}) copy-start(bf16[528,128]{1,0:T(8,128)(2,1)S(1)} %serve_slots.3.refs_3_.self_ref) | copy-start | bytes 405508
  46.1 27.8 %collective-permute-start.10 = (bf16[1024,512]{1,0:T(8,128)(2,1)}, bf16[1024,512]{1,0:T(8,128)(2,1)}, u32[]{:S(2)}, u32[]{:S(2)}) collective-permute-start(bf16[1024,512]{1,0:T(8,128)(2,1)} %constant_dynamic-update-slice_fusion.refs_3_.refs_4_.stack.refs_0_), channel_id=1, source_target_pairs={{0,4},{4,0},{8,12},{12,8},{16,20},{20,16},{24,28},{28,24},{1,5},{5... | collective-permute-start | bytes 3145736 | tf_op jit(solution)/shard_map/ppermute | solution.py:399
  53.6 31.2 %collective-permute-start.5 = (bf16[528,128]{1,0:T(8,128)(2,1)}, bf16[528,128]{1,0:T(8,128)(2,1)}, u32[]{:S(2)}, u32[]{:S(2)}) collective-permute-start(bf16[528,128]{1,0:T(8,128)(2,1)} %get-tuple-element.22.refs_3_), channel_id=1, source_target_pairs={{0,20},{4,16},{8,28},{12,24},{16,4},{20,0},{24,12},{28,8},{1,21},{... | collective-permute-start | bytes 405512 | tf_op jit(solution)/shard_map/ppermute | solution.py:399
  58.0 30.4 %collective-permute-start.8 = (bf16[528,128]{1,0:T(8,128)(2,1)}, bf16[528,128]{1,0:T(8,128)(2,1)}, u32[]{:S(2)}, u32[]{:S(2)}) collective-permute-start(bf16[528,128]{1,0:T(8,128)(2,1)} %get-tuple-element.25), channel_id=1, source_target_pairs={{0,24},{4,28},{8,16},{12,20},{16,8},{20,12},{24,0},{28,4},{1,25},{... | collective-permute-start | bytes 405512 | tf_op jit(solution)/shard_map/ppermute | solution.py:399
  58.1 26.3 %collective-permute-start.9 = (bf16[528,128]{1,0:T(8,128)(2,1)}, bf16[528,128]{1,0:T(8,128)(2,1)}, u32[]{:S(2)}, u32[]{:S(2)}) collective-permute-start(bf16[528,128]{1,0:T(8,128)(2,1)} %get-tuple-element.26.refs_0_.refs_1_), channel_id=1, source_target_pairs={{0,28},{4,24},{8,20},{12,16},{16,12},{20,8},{24,4},{28,0},{1,29},{... | collective-permute-start | bytes 405512 | tf_op jit(solution)/shard_map/ppermute | solution.py:399
  61.6 2.2 %copy-start.6 = (bf16[2,8192,128]{2,1,0:T(8,128)(2,1)S(1)}, bf16[2,8192,128]{2,1,0:T(8,128)(2,1)}, u32[]{:S(2)}) copy-start(bf16[2,8192,128]{2,1,0:T(8,128)(2,1)} %refs_2_.3) | copy-start | bytes 12582916
  69.9 18.5 %all-to-all-start.1 = ((bf16[4,528,128]{2,1,0:T(8,128)(2,1)}), bf16[4,528,128]{2,1,0:T(8,128)(2,1)S(1)}, u32[]{:S(2)}, u32[]{:S(2)}) async-start(bf16[4,528,128]{2,1,0:T(8,128)(2,1)} %serve_group.1), calls=%async_computation.1 | async-start | bytes 1081344 | tf_op jit(solution)/shard_map/all_to_all | solution.py:411
  73.9 10.9 %collective-permute-start.4 = (bf16[528,128]{1,0:T(8,128)(2,1)S(1)}, bf16[528,128]{1,0:T(8,128)(2,1)S(1)}, u32[]{:S(2)}, u32[]{:S(2)}) collective-permute-start(bf16[528,128]{1,0:T(8,128)(2,1)S(1)} %get-tuple-element.21), channel_id=1, source_target_pairs={{0,16},{4,20},{8,24},{12,28},{16,0},{20,4},{24,8},{28,12},{1,17},{... | collective-permute-start | bytes 405512 | tf_op jit(solution)/shard_map/ppermute | solution.py:399
  82.4 6.1 %copy-start.3 = (s32[2,1,2]{2,1,0:T(1,128)S(1)}, s32[2,1,2]{2,1,0:T(1,128)}, u32[]{:S(2)}) copy-start(s32[2,1,2]{2,1,0:T(1,128)} %selected_ref.3) | copy-start | bytes 52
  82.4 6.0 %copy-start.8 = (bf16[2,528,128]{2,1,0:T(8,128)(2,1)S(1)}, bf16[2,528,128]{2,1,0:T(8,128)(2,1)}, u32[]{:S(2)}) copy-start(bf16[2,528,128]{2,1,0:T(8,128)(2,1)} %copy-done.7) | copy-start | bytes 811012
  82.4 6.0 %copy-start.10 = (bf16[528,128]{1,0:T(8,128)(2,1)S(1)}, bf16[528,128]{1,0:T(8,128)(2,1)}, u32[]{:S(2)}) copy-start(bf16[528,128]{1,0:T(8,128)(2,1)} %copy-done.9) | copy-start | bytes 405508
  82.4 17.7 %collective-permute-start.14 = (bf16[512,512]{1,0:T(8,128)(2,1)S(1)}, bf16[512,512]{1,0:T(8,128)(2,1)S(1)}, u32[]{:S(2)}, u32[]{:S(2)}) collective-permute-start(bf16[512,512]{1,0:T(8,128)(2,1)S(1)} %gate.5), channel_id=1, source_target_pairs={{0,4},{4,0},{8,12},{12,8},{16,20},{20,16},{24,28},{28,24},{1,5},{5... | collective-permute-start | bytes 1572872 | tf_op jit(solution)/shard_map/ppermute | solution.py:399
  84.4 15.6 %collective-permute-start.15 = (bf16[512,512]{1,0:T(8,128)(2,1)S(1)}, bf16[512,512]{1,0:T(8,128)(2,1)S(1)}, u32[]{:S(2)}, u32[]{:S(2)}) collective-permute-start(bf16[512,512]{1,0:T(8,128)(2,1)S(1)} %gate.6), channel_id=1, source_target_pairs={{0,8},{4,12},{8,0},{12,4},{16,24},{20,28},{24,16},{28,20},{1,9},{5... | collective-permute-start | bytes 1572872 | tf_op jit(solution)/shard_map/ppermute | solution.py:399
  90.7 2.2 %collective-permute-start.11 = (bf16[256,512]{1,0:T(8,128)(2,1)S(1)}, bf16[256,512]{1,0:T(8,128)(2,1)S(1)}, u32[]{:S(2)}, u32[]{:S(2)}) collective-permute-start(bf16[256,512]{1,0:T(8,128)(2,1)S(1)} %combine_pieces.1.own_ref), channel_id=1, source_target_pairs={{0,1},{1,0},{2,3},{3,2},{4,5},{5,4},{6,7},{7,6},{8,9},{9,8},{10,11... | collective-permute-start | bytes 786440 | tf_op jit(solution)/shard_map/ppermute | solution.py:441
  91.8 8.3 %collective-permute-start.12 = (bf16[256,512]{1,0:T(8,128)(2,1)S(1)}, bf16[256,512]{1,0:T(8,128)(2,1)S(1)}, u32[]{:S(2)}, u32[]{:S(2)}) collective-permute-start(bf16[256,512]{1,0:T(8,128)(2,1)S(1)} %combine_pieces.1.own_ref), channel_id=1, source_target_pairs={{0,2},{1,3},{2,0},{3,1},{4,6},{5,7},{6,4},{7,5},{8,10},{9,11},{10,... | collective-permute-start | bytes 786440 | tf_op jit(solution)/shard_map/ppermute | solution.py:440
  100.1 1.6 %collective-permute-start.16 = (bf16[256,512]{1,0:T(8,128)(2,1)S(1)}, bf16[256,512]{1,0:T(8,128)(2,1)S(1)}, u32[]{:S(2)}, u32[]{:S(2)}) collective-permute-start(bf16[256,512]{1,0:T(8,128)(2,1)S(1)} %gate.7.y_ref), channel_id=1, source_target_pairs={{0,1},{1,0},{2,3},{3,2},{4,5},{5,4},{6,7},{7,6},{8,9},{9,8},{10,11... | collective-permute-start | bytes 786440 | tf_op jit(solution)/shard_map/ppermute | solution.py:446

commit v7 on v5

--- a/solution.py
+++ b/solution.py
@@ -310,20 +310,16 @@
     rows = pl.ds(pl.multiple_of((1 - part) * depth, depth), depth)
     _, near_odd = halves(numbers_ref, own_ref[...], core_ref[...])
     even, odd = halves(numbers_ref, y_ref[...], both_ref[...])
-    whole = (
-        whole_ref[...]
-        + jnp.dot(even, stack[rows, :], preferred_element_type=jnp.float32)
-        + jnp.dot(odd, stack_z[rows, :], preferred_element_type=jnp.float32)
-    )
-    share = (
-        share_ref[...]
-        + jnp.dot(even, stack_x[rows, :], preferred_element_type=jnp.float32)
-        + jnp.dot(
-            jnp.where(part == 0, near_odd, odd), first_ref[...], preferred_element_type=jnp.float32
-        )
-        + jnp.dot(
-            jnp.where(part == 0, odd, near_odd), second_ref[...], preferred_element_type=jnp.float32
-        )
+    last = [jnp.where(part == 0, near_odd, odd), jnp.where(part == 0, odd, near_odd)]
+    whole = whole_ref[...] + jnp.dot(
+        jnp.concatenate([even, odd], axis=1),
+        jnp.concatenate([stack[rows, :], stack_z[rows, :]], axis=0),
+        preferred_element_type=jnp.float32,
+    )
+    share = share_ref[...] + jnp.dot(
+        jnp.concatenate([even, *last], axis=1),
+        jnp.concatenate([stack_x[rows, :], first_ref[...], second_ref[...]], axis=0),
+        preferred_element_type=jnp.float32,
     )
     out_ref[:, pl.ds(pl.multiple_of(x * width, width), width)] = whole.astype(jnp.bfloat16)
     out_ref[:, pl.ds(pl.multiple_of((x ^ 1) * width, width), width)] = share.astype(jnp.bfloat16)

time: 106 us -> 106 us (level)
  no operation moved by 1% of the time
where the time goes in v7:
time: 106 us; the launch traced here: 105 us
  starting transfers between devices  47.5 us (45%)
  Pallas kernels  27.1 us (26%)
  waiting for transfers between devices  19.7 us (19%)
  local copies, waits for them, and re-layouts  10.8 us (10%)
    ppermute x12, starting transfers between devices, move(): return lax.ppermute(array, 'seq', pairs(seq_count, offset))  31.8 us
    ppermute x12, waiting for transfers between devices, move(): return lax.ppermute(array, 'seq', pairs(seq_count, offset))  8.95 us
    all_to_all x2, starting transfers between devices, swap(): lax.all_to_all(array, 'seq', split_axis=0, concat_axis=0, axis_index_grou...  8.66 us
    unnamed x19, local copies, waits for them, and re-layouts  7.81 us
    pallas_call x1, Pallas kernels, serve_group(): pl.pallas_call(serve_group_kernel, out_shape=jax.ShapeDtypeStruct((NEAR,...  7.43 us
    pallas_call x2, Pallas kernels, serve(): pl.pallas_call(functools.partial(serve_kernel, count), out_shape=[jax.Sha...  6.93 us
    ppermute x2, starting transfers between devices, jump(): return lax.ppermute(weight, ('seq', 'kvh'), moves)  5.72 us
    ppermute x1, waiting for transfers between devices, per_device(): other_y = lax.ppermute(attention, 'kvh', pairs(kvh_count, 2))  4.68 us
  transfers between devices with their start and end apart: 19, of which 8 were waited for; matrix products, arithmetic and copies ran while one was open for 4% of the time, Pallas kernels for 22%

profile of v7, /device:TPU:0, one launch (start us, length us, event | category | flops | bytes accessed | tf_op | source)
XLA Modules:
  0.0 105.4 jit_solution(9836533071170911682)
XLA Ops:
  0.0 4.0 %collective-permute-start.3 = (bf16[512,512]{1,0:T(8,128)(2,1)}, bf16[512,512]{1,0:T(8,128)(2,1)S(1)}, u32[]{:S(2)}, u32[]{:S(2)}) collective-permute-start(bf16[512,512]{1,0:T(8,128)(2,1)} %param.7), channel_id=1, source_target_pairs={{0,16},{1,24},{2,0},{3,8},{4,20},{5,28},{6,4},{7,12},{8,17},{9,25}... | collective-permute-start | bytes 1572872 | tf_op jit(solution)/shard_map/ppermute | solution.py:379
  4.0 1.7 %collective-permute-start.2 = (bf16[512,512]{1,0:T(8,128)(2,1)}, bf16[512,512]{1,0:T(8,128)(2,1)S(1)}, u32[]{:S(2)}, u32[]{:S(2)}) collective-permute-start(bf16[512,512]{1,0:T(8,128)(2,1)} %param.7), channel_id=1, source_target_pairs={{0,0},{1,8},{2,16},{3,24},{4,4},{5,12},{6,20},{7,28},{8,1},{9,9},{... | collective-permute-start | bytes 1572872 | tf_op jit(solution)/shard_map/ppermute | solution.py:379
  5.7 0.0 copy-start
  5.7 0.9 copy-done
  6.7 0.7 copy-done.2
  7.4 1.6 %pack_queries.1 = (bf16[4,528,128]{2,1,0:T(8,128)(2,1)}, bf16[528,128]{1,0:T(8,128)(2,1)S(1)}, bf16[528,128]{1,0:T(8,128)(2,1)S(1)}, bf16[528,128]{1,0:T(8,128)(2,1)S(1)}, bf16[528,128]{1,0:T(8,128)(2,1)S(1)}) custom-call(s32[1]{0:T(128)} %bitcast.3.me_ref, s32[2,1,2]{2,1,0:T(1,128)S(1)} %copy-done.2, bf16[256,512]{1,0:T(8,128)(2,1)S(1)} %copy-done), custom_call_target="tpu_custom_call" | custom-call | tf_op jit(solution)/shard_map/pack_queries/pallas_call | solution.py:62
  9.0 5.2 %all-to-all-start = ((bf16[4,528,128]{2,1,0:T(8,128)(2,1)}), bf16[4,528,128]{2,1,0:T(8,128)(2,1)}, u32[]{:S(2)}, u32[]{:S(2)}) async-start(bf16[4,528,128]{2,1,0:T(8,128)(2,1)} %get-tuple-element.16.refs_0_), calls=%async_computation | async-start | bytes 1081344 | tf_op jit(solution)/shard_map/all_to_all | solution.py:403
  14.1 1.2 %collective-permute-start = (bf16[528,128]{1,0:T(8,128)(2,1)S(1)}, bf16[528,128]{1,0:T(8,128)(2,1)S(1)}, u32[]{:S(2)}, u32[]{:S(2)}) collective-permute-start(bf16[528,128]{1,0:T(8,128)(2,1)S(1)} %get-tuple-element.17), channel_id=1, source_target_pairs={{0,16},{4,20},{8,24},{12,28},{16,0},{20,4},{24,8},{28,12},{1,17},{... | collective-permute-start | bytes 405512 | tf_op jit(solution)/shard_map/ppermute | solution.py:391
  15.4 3.1 %collective-permute-start.1 = (bf16[528,128]{1,0:T(8,128)(2,1)S(1)}, bf16[528,128]{1,0:T(8,128)(2,1)S(1)}, u32[]{:S(2)}, u32[]{:S(2)}) collective-permute-start(bf16[528,128]{1,0:T(8,128)(2,1)S(1)} %get-tuple-element.18), channel_id=1, source_target_pairs={{0,20},{4,16},{8,28},{12,24},{16,4},{20,0},{24,12},{28,8},{1,21},{... | collective-permute-start | bytes 405512 | tf_op jit(solution)/shard_map/ppermute | solution.py:391
  18.5 2.2 %collective-permute-start.6 = (bf16[528,128]{1,0:T(8,128)(2,1)S(1)}, bf16[528,128]{1,0:T(8,128)(2,1)S(1)}, u32[]{:S(2)}, u32[]{:S(2)}) collective-permute-start(bf16[528,128]{1,0:T(8,128)(2,1)S(1)} %get-tuple-element.21), channel_id=1, source_target_pairs={{0,24},{4,28},{8,16},{12,20},{16,8},{20,12},{24,0},{28,4},{1,25},{... | collective-permute-start | bytes 405512 | tf_op jit(solution)/shard_map/ppermute | solution.py:391
  20.7 0.9 copy-done.1
  21.6 2.2 %copy-done.4 = bf16[2,8192,128]{2,1,0:T(8,128)(2,1)S(1)} copy-done((bf16[2,8192,128]{2,1,0:T(8,128)(2,1)S(1)}, bf16[2,8192,128]{2,1,0:T(8,128)(2,1)}, u32[]{:S(2)}) %copy-start.4) | copy-done | bytes 4194328
  23.8 2.7 %own_pieces.1.refs_0_.refs_3_.own_ref = bf16[2,528,128]{2,1,0:T(8,128)(2,1)S(1)} custom-call(bf16[256,512]{1,0:T(8,128)(2,1)S(1)} %copy-done.1, bf16[2,8192,128]{2,1,0:T(8,128)(2,1)S(1)} %copy-done.4, bf16[4,528,128]{2,1,0:T(8,128)(2,1)} %get-tuple-element.16.refs_0_), custom_call_target="tpu_custom_call" | custom-call | flops 68719476736 | bytes 1073741824 | tf_op jit(solution)/shard_map/own_pieces/pallas_call | solution.py:132
  26.6 0.0 copy-start.7
  26.6 0.0 collective-permute-done.2
  26.6 2.7 %collective-permute-start.7 = (bf16[528,128]{1,0:T(8,128)(2,1)S(1)}, bf16[528,128]{1,0:T(8,128)(2,1)S(1)}, u32[]{:S(2)}, u32[]{:S(2)}) collective-permute-start(bf16[528,128]{1,0:T(8,128)(2,1)S(1)} %get-tuple-element.22), channel_id=1, source_target_pairs={{0,28},{4,24},{8,20},{12,16},{16,12},{20,8},{24,4},{28,0},{1,29},{... | collective-permute-start | bytes 405512 | tf_op jit(solution)/shard_map/ppermute | solution.py:391
  29.3 0.8 constant_dynamic-update-slice_fusion.1
  30.2 0.0 collective-permute-done.3
  30.2 0.8 constant_dynamic-update-slice_fusion.refs_4_.stack.refs_0_
  31.0 13.6 %collective-permute-start.13 = (bf16[1024,512]{1,0:T(8,128)(2,1)}, bf16[1024,512]{1,0:T(8,128)(2,1)}, u32[]{:S(2)}, u32[]{:S(2)}) collective-permute-start(bf16[1024,512]{1,0:T(8,128)(2,1)} %constant_dynamic-update-slice_fusion.refs_4_.stack.refs_0_), channel_id=1, source_target_pairs={{0,8},{4,12},{8,0},{12,4},{16,24},{20,28},{24,16},{28,20},{1,9},{5... | collective-permute-start | bytes 3145736 | tf_op jit(solution)/shard_map/ppermute | solution.py:391
  44.6 0.0 collective-permute-done.refs_0_
  44.6 1.6 %collective-permute-start.10 = (bf16[1024,512]{1,0:T(8,128)(2,1)}, bf16[1024,512]{1,0:T(8,128)(2,1)}, u32[]{:S(2)}, u32[]{:S(2)}) collective-permute-start(bf16[1024,512]{1,0:T(8,128)(2,1)} %constant_dynamic-update-slice_fusion.refs_4_.stack.refs_0_), channel_id=1, source_target_pairs={{0,4},{4,0},{8,12},{12,8},{16,20},{20,16},{24,28},{28,24},{1,5},{5... | collective-permute-start | bytes 3145736 | tf_op jit(solution)/shard_map/ppermute | solution.py:391
  46.2 4.0 %collective-permute-done.1.refs_1_ = bf16[528,128]{1,0:T(8,128)(2,1)S(1)} collective-permute-done((bf16[528,128]{1,0:T(8,128)(2,1)S(1)}, bf16[528,128]{1,0:T(8,128)(2,1)S(1)}, u32[]{:S(2)}, u32[]{:S(2)}) %collective-permute-start.1) | collective-permute-done | bytes 135200 | tf_op jit(solution)/shard_map/ppermute | solution.py:391
  50.2 0.0 copy-done.5
  50.2 3.5 %serve_slots.2 = (bf16[528,128]{1,0:T(8,128)(2,1)S(1)}, bf16[528,128]{1,0:T(8,128)(2,1)}) custom-call(bf16[528,128]{1,0:T(8,128)(2,1)S(1)} %collective-permute-done.refs_0_, bf16[528,128]{1,0:T(8,128)(2,1)S(1)} %collective-permute-done.1.refs_1_, bf16[2,8192,128]{2,1,0:T(8,128)(2,1)S(1)} %copy-done.5, ...), custom_call_target="tpu_custom_call" | custom-call | flops 68719476736 | bytes 1073741824 | tf_op jit(solution)/shard_map/serve_slots/pallas_call | solution.py:169
  53.7 0.1 collective-permute-start.5
  53.8 0.0 collective-permute-done.6.refs_0_
  53.8 0.0 collective-permute-done.7.refs_1_
  53.8 3.4 %serve_slots.3 = (bf16[528,128]{1,0:T(8,128)(2,1)}, bf16[528,128]{1,0:T(8,128)(2,1)}) custom-call(bf16[528,128]{1,0:T(8,128)(2,1)S(1)} %collective-permute-done.6.refs_0_, bf16[528,128]{1,0:T(8,128)(2,1)S(1)} %collective-permute-done.7.refs_1_, bf16[2,8192,128]{2,1,0:T(8,128)(2,1)S(1)} %copy-done.5, bf16[528,128]{1,0:T(8,128)(2,1)} %get-tuple-element.20.refs_3_), custom_call_target="tpu_custom_call" | custom-call | flops 68719476736 | bytes 1073741824 | tf_op jit(solution)/shard_map/serve_slots/pallas_call | solution.py:169
  57.2 0.1 collective-permute-start.8
  57.3 3.5 %collective-permute-start.9 = (bf16[528,128]{1,0:T(8,128)(2,1)}, bf16[528,128]{1,0:T(8,128)(2,1)}, u32[]{:S(2)}, u32[]{:S(2)}) collective-permute-start(bf16[528,128]{1,0:T(8,128)(2,1)} %get-tuple-element.24.refs_0_), channel_id=1, source_target_pairs={{0,28},{4,24},{8,20},{12,16},{16,12},{20,8},{24,4},{28,0},{1,29},{... | collective-permute-start | bytes 405512 | tf_op jit(solution)/shard_map/ppermute | solution.py:391
  60.8 0.0 all-to-all-done.slots_ref
  60.8 0.0 copy-done.7
  60.8 2.2 %copy-done.6 = bf16[2,8192,128]{2,1,0:T(8,128)(2,1)S(1)} copy-done((bf16[2,8192,128]{2,1,0:T(8,128)(2,1)S(1)}, bf16[2,8192,128]{2,1,0:T(8,128)(2,1)}, u32[]{:S(2)}) %copy-start.6) | copy-done | bytes 4194328
  63.0 7.4 %serve_group.1.refs_1_ = bf16[4,528,128]{2,1,0:T(8,128)(2,1)} custom-call(bf16[4,528,128]{2,1,0:T(8,128)(2,1)} %all-to-all-done.slots_ref, bf16[2,8192,128]{2,1,0:T(8,128)(2,1)S(1)} %copy-done.6, bf16[2,528,128]{2,1,0:T(8,128)(2,1)S(1)} %own_pieces.1.refs_0_.refs_3_.own_ref), custom_call_target="tpu_custom_call" | custom-call | flops 68719476736 | bytes 1073741824 | tf_op jit(solution)/shard_map/serve_group/pallas_call | solution.py:204
  70.4 3.5 %all-to-all-start.1 = ((bf16[4,528,128]{2,1,0:T(8,128)(2,1)}), bf16[4,528,128]{2,1,0:T(8,128)(2,1)S(1)}, u32[]{:S(2)}, u32[]{:S(2)}) async-start(bf16[4,528,128]{2,1,0:T(8,128)(2,1)} %serve_group.1.refs_1_), calls=%async_computation.1 | async-start | bytes 1081344 | tf_op jit(solution)/shard_map/all_to_all | solution.py:403
  73.9 2.6 %collective-permute-done.10.refs_4_.stack_x.refs_2_ = bf16[1024,512]{1,0:T(8,128)(2,1)} collective-permute-done((bf16[1024,512]{1,0:T(8,128)(2,1)}, bf16[1024,512]{1,0:T(8,128)(2,1)}, u32[]{:S(2)}, u32[]{:S(2)}) %collective-permute-start.10) | collective-permute-done | bytes 1048608 | tf_op jit(solution)/shard_map/ppermute | solution.py:391
  76.5 0.3 collective-permute-start.4
  76.8 1.1 %slice.9.refs_0_ = bf16[512,512]{1,0:T(8,128)(2,1)S(1)} slice(bf16[1024,512]{1,0:T(8,128)(2,1)} %collective-permute-done.10.refs_4_.stack_x.refs_2_), slice={[512:1024], [0:512]} | slice | bytes 1048576 | tf_op jit(solution)/shard_map/slice | solution.py:426
  77.9 2.0 %collective-permute-done.13.stack_z.refs_1_ = bf16[1024,512]{1,0:T(8,128)(2,1)} collective-permute-done((bf16[1024,512]{1,0:T(8,128)(2,1)}, bf16[1024,512]{1,0:T(8,128)(2,1)}, u32[]{:S(2)}, u32[]{:S(2)}) %collective-permute-start.13) | collective-permute-done | bytes 1048608 | tf_op jit(solution)/shard_map/ppermute | solution.py:391
  79.8 1.1 %slice.8.refs_0_ = bf16[512,512]{1,0:T(8,128)(2,1)S(1)} slice(bf16[1024,512]{1,0:T(8,128)(2,1)} %collective-permute-done.13.stack_z.refs_1_), slice={[0:512], [0:512]} | slice | bytes 1048576 | tf_op jit(solution)/shard_map/slice | solution.py:425
  80.9 0.0 copy-start.3
  80.9 0.0 copy-start.8
  81.0 3.5 %collective-permute-start.14 = (bf16[512,512]{1,0:T(8,128)(2,1)S(1)}, bf16[512,512]{1,0:T(8,128)(2,1)S(1)}, u32[]{:S(2)}, u32[]{:S(2)}) collective-permute-start(bf16[512,512]{1,0:T(8,128)(2,1)S(1)} %gate.5), channel_id=1, source_target_pairs={{0,4},{4,0},{8,12},{12,8},{16,20},{20,16},{24,28},{28,24},{1,5},{5... | collective-permute-start | bytes 1572872 | tf_op jit(solution)/shard_map/ppermute | solution.py:391
  84.4 0.0 collective-permute-done.9.refs_3_
  84.4 0.0 collective-permute-start.15
  84.4 0.4 collective-permute-done.4.refs_2_.refs_0_
  84.8 0.0 collective-permute-done.5.refs_3_.refs_1_
  84.8 3.6 %all-to-all-done.1.refs_1_.near_ref = bf16[4,528,128]{2,1,0:T(8,128)(2,1)S(1)} async-done(((bf16[4,528,128]{2,1,0:T(8,128)(2,1)}), bf16[4,528,128]{2,1,0:T(8,128)(2,1)S(1)}, u32[]{:S(2)}, u32[]{:S(2)}) %all-to-all-start.1) | async-done | bytes 540704 | tf_op jit(solution)/shard_map/all_to_all | solution.py:403
  88.4 0.0 collective-permute-done.8.refs_2_
  88.4 0.0 copy-done.3
  88.4 0.0 copy-done.8
  88.4 2.5 %combine_pieces.1.own_ref = bf16[256,512]{1,0:T(8,128)(2,1)S(1)} custom-call(s32[1]{0:T(128)} %bitcast.3.me_ref, s32[2,1,2]{2,1,0:T(1,128)S(1)} %copy-done.3, bf16[2,528,128]{2,1,0:T(8,128)(2,1)S(1)} %copy-done.8, bf16[4,528,128]{2,1,0:T(8,128)(2,1)S(1)} %all-to-all-done.1.refs_1_.near_ref, bf16[528,128]{1,0:T(8,128)(2,1)S(1)} %collective-permute-done.4.refs_2_.refs_0_, ...), custom_call_target="tpu_custom_call" | custom-call | flops 68719476736 | bytes 1073741824 | tf_op jit(solution)/shard_map/combine_pieces/pallas_call | solution.py:277
  90.9 1.0 collective-permute-start.11
  92.0 0.2 collective-permute-start.12
  92.1 0.1 pad_add_fusion.numbers_ref
  92.2 0.9 collective-permute-done.11.core_ref
  93.1 2.4 %project.1 = (f32[256,512]{1,0:T(8,128)S(1)}, f32[256,512]{1,0:T(8,128)S(1)}) custom-call(s32[3]{0:T(128)S(1)} %pad_add_fusion.numbers_ref, bf16[256,512]{1,0:T(8,128)(2,1)S(1)} %combine_pieces.1.own_ref, bf16[256,512]{1,0:T(8,128)(2,1)S(1)} %collective-permute-done.11.core_ref, bf16[1024,512]{1,0:T(8,128)(2,1)} %constant_dynamic-update-slice_fusion.refs_4_.stack.refs_0_, ...), custom_call_target="tpu_custom_call" | custom-call | tf_op jit(solution)/shard_map/project/pallas_call | solution.py:330
  95.6 4.7 %collective-permute-done.12.refs_0_ = bf16[256,512]{1,0:T(8,128)(2,1)S(1)} collective-permute-done((bf16[256,512]{1,0:T(8,128)(2,1)S(1)}, bf16[256,512]{1,0:T(8,128)(2,1)S(1)}, u32[]{:S(2)}, u32[]{:S(2)}) %collective-permute-start.12) | collective-permute-done | bytes 262176 | tf_op jit(solution)/shard_map/ppermute | solution.py:431
  100.2 0.0 collective-permute-done.14.refs_2_.refs_3_
  100.2 0.0 collective-permute-done.15.refs_3_.refs_4_
  100.2 0.1 collective-permute-start.16
  100.3 1.5 %collective-permute-done.16.both_ref = bf16[256,512]{1,0:T(8,128)(2,1)S(1)} collective-permute-done((bf16[256,512]{1,0:T(8,128)(2,1)S(1)}, bf16[256,512]{1,0:T(8,128)(2,1)S(1)}, u32[]{:S(2)}, u32[]{:S(2)}) %collective-permute-start.16) | collective-permute-done | bytes 262176 | tf_op jit(solution)/shard_map/ppermute | solution.py:437
  101.8 3.5 %finish.1 = bf16[256,1024]{1,0:T(8,128)(2,1)} custom-call(s32[3]{0:T(128)S(1)} %pad_add_fusion.numbers_ref, bf16[256,512]{1,0:T(8,128)(2,1)S(1)} %combine_pieces.1.own_ref, bf16[256,512]{1,0:T(8,128)(2,1)S(1)} %collective-permute-done.11.core_ref, bf16[256,512]{1,0:T(8,128)(2,1)S(1)} %gate.7.y_ref, bf16[256,512]{1,0:T(8,128)(2,1)S(1)} %collective-permute-done.16.both_ref, ...), custom_call_target="tpu_custom_call" | custom-call | tf_op jit(solution)/shard_map/finish/pallas_call | solution.py:342
  (9 shorter events, 0.0 us)
Async XLA Ops:
  0.0 30.2 %collective-permute-start.3 = (bf16[512,512]{1,0:T(8,128)(2,1)}, bf16[512,512]{1,0:T(8,128)(2,1)S(1)}, u32[]{:S(2)}, u32[]{:S(2)}) collective-permute-start(bf16[512,512]{1,0:T(8,128)(2,1)} %param.7), channel_id=1, source_target_pairs={{0,16},{1,24},{2,0},{3,8},{4,20},{5,28},{6,4},{7,12},{8,17},{9,25}... | collective-permute-start | bytes 1572872 | tf_op jit(solution)/shard_map/ppermute | solution.py:379
  4.0 22.5 %collective-permute-start.2 = (bf16[512,512]{1,0:T(8,128)(2,1)}, bf16[512,512]{1,0:T(8,128)(2,1)S(1)}, u32[]{:S(2)}, u32[]{:S(2)}) collective-permute-start(bf16[512,512]{1,0:T(8,128)(2,1)} %param.7), channel_id=1, source_target_pairs={{0,0},{1,8},{2,16},{3,24},{4,4},{5,12},{6,20},{7,28},{8,1},{9,9},{... | collective-permute-start | bytes 1572872 | tf_op jit(solution)/shard_map/ppermute | solution.py:379
  5.7 0.9 copy-start
  6.7 0.7 copy-start.2
  9.0 51.8 %all-to-all-start = ((bf16[4,528,128]{2,1,0:T(8,128)(2,1)}), bf16[4,528,128]{2,1,0:T(8,128)(2,1)}, u32[]{:S(2)}, u32[]{:S(2)}) async-start(bf16[4,528,128]{2,1,0:T(8,128)(2,1)} %get-tuple-element.16.refs_0_), calls=%async_computation | async-start | bytes 1081344 | tf_op jit(solution)/shard_map/all_to_all | solution.py:403
  14.1 30.5 %collective-permute-start = (bf16[528,128]{1,0:T(8,128)(2,1)S(1)}, bf16[528,128]{1,0:T(8,128)(2,1)S(1)}, u32[]{:S(2)}, u32[]{:S(2)}) collective-permute-start(bf16[528,128]{1,0:T(8,128)(2,1)S(1)} %get-tuple-element.17), channel_id=1, source_target_pairs={{0,16},{4,20},{8,24},{12,28},{16,0},{20,4},{24,8},{28,12},{1,17},{... | collective-permute-start | bytes 405512 | tf_op jit(solution)/shard_map/ppermute | solution.py:391
  15.4 34.8 %collective-permute-start.1 = (bf16[528,128]{1,0:T(8,128)(2,1)S(1)}, bf16[528,128]{1,0:T(8,128)(2,1)S(1)}, u32[]{:S(2)}, u32[]{:S(2)}) collective-permute-start(bf16[528,128]{1,0:T(8,128)(2,1)S(1)} %get-tuple-element.18), channel_id=1, source_target_pairs={{0,20},{4,16},{8,28},{12,24},{16,4},{20,0},{24,12},{28,8},{1,21},{... | collective-permute-start | bytes 405512 | tf_op jit(solution)/shard_map/ppermute | solution.py:391
  18.5 35.2 %collective-permute-start.6 = (bf16[528,128]{1,0:T(8,128)(2,1)S(1)}, bf16[528,128]{1,0:T(8,128)(2,1)S(1)}, u32[]{:S(2)}, u32[]{:S(2)}) collective-permute-start(bf16[528,128]{1,0:T(8,128)(2,1)S(1)} %get-tuple-element.21), channel_id=1, source_target_pairs={{0,24},{4,28},{8,16},{12,20},{16,8},{20,12},{24,0},{28,4},{1,25},{... | collective-permute-start | bytes 405512 | tf_op jit(solution)/shard_map/ppermute | solution.py:391
  20.7 0.9 copy-start.1
  21.6 2.2 %copy-start.4 = (bf16[2,8192,128]{2,1,0:T(8,128)(2,1)S(1)}, bf16[2,8192,128]{2,1,0:T(8,128)(2,1)}, u32[]{:S(2)}) copy-start(bf16[2,8192,128]{2,1,0:T(8,128)(2,1)} %refs_2_.3) | copy-start | bytes 12582916
  23.8 26.4 %copy-start.5 = (bf16[2,8192,128]{2,1,0:T(8,128)(2,1)S(1)}, bf16[2,8192,128]{2,1,0:T(8,128)(2,1)}, u32[]{:S(2)}) copy-start(bf16[2,8192,128]{2,1,0:T(8,128)(2,1)} %refs_2_.3) | copy-start | bytes 12582916
  26.6 34.2 %copy-start.7 = (bf16[2,528,128]{2,1,0:T(8,128)(2,1)}, bf16[2,528,128]{2,1,0:T(8,128)(2,1)S(1)}, u32[]{:S(2)}) copy-start(bf16[2,528,128]{2,1,0:T(8,128)(2,1)S(1)} %own_pieces.1.refs_0_.refs_3_.own_ref) | copy-start | bytes 811012
  26.6 27.2 %collective-permute-start.7 = (bf16[528,128]{1,0:T(8,128)(2,1)S(1)}, bf16[528,128]{1,0:T(8,128)(2,1)S(1)}, u32[]{:S(2)}, u32[]{:S(2)}) collective-permute-start(bf16[528,128]{1,0:T(8,128)(2,1)S(1)} %get-tuple-element.22), channel_id=1, source_target_pairs={{0,28},{4,24},{8,20},{12,16},{16,12},{20,8},{24,4},{28,0},{1,29},{... | collective-permute-start | bytes 405512 | tf_op jit(solution)/shard_map/ppermute | solution.py:391
  31.0 48.8 %collective-permute-start.13 = (bf16[1024,512]{1,0:T(8,128)(2,1)}, bf16[1024,512]{1,0:T(8,128)(2,1)}, u32[]{:S(2)}, u32[]{:S(2)}) collective-permute-start(bf16[1024,512]{1,0:T(8,128)(2,1)} %constant_dynamic-update-slice_fusion.refs_4_.stack.refs_0_), channel_id=1, source_target_pairs={{0,8},{4,12},{8,0},{12,4},{16,24},{20,28},{24,16},{28,20},{1,9},{5... | collective-permute-start | bytes 3145736 | tf_op jit(solution)/shard_map/ppermute | solution.py:391
  44.6 31.9 %collective-permute-start.10 = (bf16[1024,512]{1,0:T(8,128)(2,1)}, bf16[1024,512]{1,0:T(8,128)(2,1)}, u32[]{:S(2)}, u32[]{:S(2)}) collective-permute-start(bf16[1024,512]{1,0:T(8,128)(2,1)} %constant_dynamic-update-slice_fusion.refs_4_.stack.refs_0_), channel_id=1, source_target_pairs={{0,4},{4,0},{8,12},{12,8},{16,20},{20,16},{24,28},{28,24},{1,5},{5... | collective-permute-start | bytes 3145736 | tf_op jit(solution)/shard_map/ppermute | solution.py:391
  53.7 31.1 %collective-permute-start.5 = (bf16[528,128]{1,0:T(8,128)(2,1)}, bf16[528,128]{1,0:T(8,128)(2,1)}, u32[]{:S(2)}, u32[]{:S(2)}) collective-permute-start(bf16[528,128]{1,0:T(8,128)(2,1)} %get-tuple-element.20.refs_3_), channel_id=1, source_target_pairs={{0,20},{4,16},{8,28},{12,24},{16,4},{20,0},{24,12},{28,8},{1,21},{... | collective-permute-start | bytes 405512 | tf_op jit(solution)/shard_map/ppermute | solution.py:391
  57.2 31.2 %collective-permute-start.8 = (bf16[528,128]{1,0:T(8,128)(2,1)}, bf16[528,128]{1,0:T(8,128)(2,1)}, u32[]{:S(2)}, u32[]{:S(2)}) collective-permute-start(bf16[528,128]{1,0:T(8,128)(2,1)} %get-tuple-element.23), channel_id=1, source_target_pairs={{0,24},{4,28},{8,16},{12,20},{16,8},{20,12},{24,0},{28,4},{1,25},{... | collective-permute-start | bytes 405512 | tf_op jit(solution)/shard_map/ppermute | solution.py:391
  57.3 27.1 %collective-permute-start.9 = (bf16[528,128]{1,0:T(8,128)(2,1)}, bf16[528,128]{1,0:T(8,128)(2,1)}, u32[]{:S(2)}, u32[]{:S(2)}) collective-permute-start(bf16[528,128]{1,0:T(8,128)(2,1)} %get-tuple-element.24.refs_0_), channel_id=1, source_target_pairs={{0,28},{4,24},{8,20},{12,16},{16,12},{20,8},{24,4},{28,0},{1,29},{... | collective-permute-start | bytes 405512 | tf_op jit(solution)/shard_map/ppermute | solution.py:391
  60.8 2.2 %copy-start.6 = (bf16[2,8192,128]{2,1,0:T(8,128)(2,1)S(1)}, bf16[2,8192,128]{2,1,0:T(8,128)(2,1)}, u32[]{:S(2)}) copy-start(bf16[2,8192,128]{2,1,0:T(8,128)(2,1)} %refs_2_.3) | copy-start | bytes 12582916
  70.4 18.0 %all-to-all-start.1 = ((bf16[4,528,128]{2,1,0:T(8,128)(2,1)}), bf16[4,528,128]{2,1,0:T(8,128)(2,1)S(1)}, u32[]{:S(2)}, u32[]{:S(2)}) async-start(bf16[4,528,128]{2,1,0:T(8,128)(2,1)} %serve_group.1.refs_1_), calls=%async_computation.1 | async-start | bytes 1081344 | tf_op jit(solution)/shard_map/all_to_all | solution.py:403
  76.5 8.3 %collective-permute-start.4 = (bf16[528,128]{1,0:T(8,128)(2,1)S(1)}, bf16[528,128]{1,0:T(8,128)(2,1)S(1)}, u32[]{:S(2)}, u32[]{:S(2)}) collective-permute-start(bf16[528,128]{1,0:T(8,128)(2,1)S(1)} %get-tuple-element.19), channel_id=1, source_target_pairs={{0,16},{4,20},{8,24},{12,28},{16,0},{20,4},{24,8},{28,12},{1,17},{... | collective-permute-start | bytes 405512 | tf_op jit(solution)/shard_map/ppermute | solution.py:391
  80.9 7.5 %copy-start.3 = (s32[2,1,2]{2,1,0:T(1,128)S(1)}, s32[2,1,2]{2,1,0:T(1,128)}, u32[]{:S(2)}) copy-start(s32[2,1,2]{2,1,0:T(1,128)} %selected_ref.3) | copy-start | bytes 52
  80.9 7.5 %copy-start.8 = (bf16[2,528,128]{2,1,0:T(8,128)(2,1)S(1)}, bf16[2,528,128]{2,1,0:T(8,128)(2,1)}, u32[]{:S(2)}) copy-start(bf16[2,528,128]{2,1,0:T(8,128)(2,1)} %copy-done.7) | copy-start | bytes 811012
  81.0 19.3 %collective-permute-start.14 = (bf16[512,512]{1,0:T(8,128)(2,1)S(1)}, bf16[512,512]{1,0:T(8,128)(2,1)S(1)}, u32[]{:S(2)}, u32[]{:S(2)}) collective-permute-start(bf16[512,512]{1,0:T(8,128)(2,1)S(1)} %gate.5), channel_id=1, source_target_pairs={{0,4},{4,0},{8,12},{12,8},{16,20},{20,16},{24,28},{28,24},{1,5},{5... | collective-permute-start | bytes 1572872 | tf_op jit(solution)/shard_map/ppermute | solution.py:391
  84.4 15.8 %collective-permute-start.15 = (bf16[512,512]{1,0:T(8,128)(2,1)S(1)}, bf16[512,512]{1,0:T(8,128)(2,1)S(1)}, u32[]{:S(2)}, u32[]{:S(2)}) collective-permute-start(bf16[512,512]{1,0:T(8,128)(2,1)S(1)} %gate.6), channel_id=1, source_target_pairs={{0,8},{4,12},{8,0},{12,4},{16,24},{20,28},{24,16},{28,20},{1,9},{5... | collective-permute-start | bytes 1572872 | tf_op jit(solution)/shard_map/ppermute | solution.py:391
  90.9 2.2 %collective-permute-start.11 = (bf16[256,512]{1,0:T(8,128)(2,1)S(1)}, bf16[256,512]{1,0:T(8,128)(2,1)S(1)}, u32[]{:S(2)}, u32[]{:S(2)}) collective-permute-start(bf16[256,512]{1,0:T(8,128)(2,1)S(1)} %combine_pieces.1.own_ref), channel_id=1, source_target_pairs={{0,1},{1,0},{2,3},{3,2},{4,5},{5,4},{6,7},{7,6},{8,9},{9,8},{10,11... | collective-permute-start | bytes 786440 | tf_op jit(solution)/shard_map/ppermute | solution.py:432
  92.0 8.3 %collective-permute-start.12 = (bf16[256,512]{1,0:T(8,128)(2,1)S(1)}, bf16[256,512]{1,0:T(8,128)(2,1)S(1)}, u32[]{:S(2)}, u32[]{:S(2)}) collective-permute-start(bf16[256,512]{1,0:T(8,128)(2,1)S(1)} %combine_pieces.1.own_ref), channel_id=1, source_target_pairs={{0,2},{1,3},{2,0},{3,1},{4,6},{5,7},{6,4},{7,5},{8,10},{9,11},{10,... | collective-permute-start | bytes 786440 | tf_op jit(solution)/shard_map/ppermute | solution.py:431
  100.2 1.6 %collective-permute-start.16 = (bf16[256,512]{1,0:T(8,128)(2,1)S(1)}, bf16[256,512]{1,0:T(8,128)(2,1)S(1)}, u32[]{:S(2)}, u32[]{:S(2)}) collective-permute-start(bf16[256,512]{1,0:T(8,128)(2,1)S(1)} %gate.7.y_ref), channel_id=1, source_target_pairs={{0,1},{1,0},{2,3},{3,2},{4,5},{5,4},{6,7},{7,6},{8,9},{9,8},{10,11... | collective-permute-start | bytes 786440 | tf_op jit(solution)/shard_map/ppermute | solution.py:437
